TPU v7x, 32 devices: a whole 2x2x4 slice. The times are simulated.
32 devices in a mesh: ctx: 4 (over z), tp: 4 (over y, x), dp: 2 (over core).
Axes of the slice: x: 2, y: 2, z: 4, core: 2. Of those that a mesh axis runs over, the one named last changes fastest.
Arguments:
- out_grad: bfloat16 [2, 512, 4096], P('dp', ('ctx', 'tp')), may hold values from -6 to 6
- gate_in: bfloat16 [2, 4096, 512], P('dp', 'tp', 'ctx'), may hold values from -6 to 6
- conv_in: bfloat16 [2, 4096, 512], P('dp', 'tp', 'ctx'), may hold values from -6 to 6
- filter_raw: float32 [4096, 512], P(('tp', 'ctx')), may hold values from -6 to 6
- out_weight: bfloat16 [4096, 4096], P('tp'), may hold values from -0.09375 to 0.09375
Outputs:
- gate_grad_out: bfloat16 [2, 4096, 512], P('dp', 'tp', 'ctx')
- conv_grad_out: bfloat16 [2, 4096, 512], P('dp', 'tp', 'ctx')
- filter_grad_out: float32 [4096, 512], P(('tp', 'ctx', 'dp'))
All inputs are finite; a program needn't handle non-finite values.
Results may differ from a plain program's by a relative error of at most 0.0049.
Values may be sent and summed in bfloat16 or wider, within the bound.
No kernel may reach another device: no remote copies, remote signals or barrier semaphores. Data moves between devices by JAX's collectives and lax.ppermute only.
A program may use at most 64 MiB of HBM per device.

v0:
```python
import functools
import math

import jax
import jax.numpy as jnp
import ml_dtypes
import numpy as np
from jax import lax
from jax.experimental import pallas as pl
from jax.experimental.pallas import tpu as pltpu
from jax.sharding import PartitionSpec as P


def wave_table(rows, cols, length, sign):
    product = (
        jnp.arange(rows, dtype=jnp.int32)[:, None]
        * jnp.arange(cols, dtype=jnp.int32)[None, :]
        % length
    )
    angle = product.astype(jnp.float32) * (2.0 * math.pi / length)
    return (jnp.cos(angle), sign * jnp.sin(angle))


def mix_einsum(form, left, right):
    return jnp.einsum(form, left, right, precision=lax.Precision.HIGHEST)


def forward_spectrum(signal):
    chans, length = signal.shape
    total_len = 2 * length
    bits = total_len.bit_length() - 1
    outer_len = 2 ** (bits // 2)
    inner_len = total_len // outer_len
    half_outer = outer_len // 2
    folded = signal.reshape(chans, half_outer, inner_len)
    first_re, first_im = wave_table(outer_len, half_outer, outer_len, -1.0)
    mid_re = mix_einsum("kn,cna->cka", first_re, folded)
    mid_im = mix_einsum("kn,cna->cka", first_im, folded)
    twist_re, twist_im = wave_table(outer_len, inner_len, total_len, -1.0)
    rot_re = mid_re * twist_re - mid_im * twist_im
    rot_im = mid_re * twist_im + mid_im * twist_re
    last_re, last_im = wave_table(inner_len, inner_len, inner_len, -1.0)
    out_re = mix_einsum("cka,aj->ckj", rot_re, last_re) - mix_einsum("cka,aj->ckj", rot_im, last_im)
    out_im = mix_einsum("cka,aj->ckj", rot_re, last_im) + mix_einsum("cka,aj->ckj", rot_im, last_re)
    return (out_re, out_im)


def inverse_signal(spec_re, spec_im):
    chans, outer_len, inner_len = spec_re.shape
    total_len = outer_len * inner_len
    last_re, last_im = wave_table(inner_len, inner_len, inner_len, 1.0)
    mid_re = mix_einsum("ckj,ja->cka", spec_re, last_re) - mix_einsum(
        "ckj,ja->cka", spec_im, last_im
    )
    mid_im = mix_einsum("ckj,ja->cka", spec_re, last_im) + mix_einsum(
        "ckj,ja->cka", spec_im, last_re
    )
    twist_re, twist_im = wave_table(outer_len, inner_len, total_len, 1.0)
    rot_re = mid_re * twist_re - mid_im * twist_im
    rot_im = mid_re * twist_im + mid_im * twist_re
    first_re, first_im = wave_table(outer_len // 2, outer_len, outer_len, 1.0)
    signal = mix_einsum("nk,cka->cna", first_re, rot_re) - mix_einsum(
        "nk,cka->cna", first_im, rot_im
    )
    return signal.reshape(chans, -1) / total_len


def two_level_on_device(out_grad, gate_in, conv_in, filter_raw, out_weight):
    grad_rows = out_grad[0]
    gate_local = gate_in[0]
    conv_local = conv_in[0]
    unit_grad = lax.dot_general(
        out_weight,
        lax.all_gather(grad_rows, "tp", axis=0, tiled=True),
        (((1,), (1,)), ((), ())),
        preferred_element_type=jnp.float32,
    )
    gate_grad = (unit_grad * gate_local.astype(jnp.float32)).astype(jnp.bfloat16)
    gate_chan, conv_chan = (
        lax.all_to_all(gate_grad, "ctx", split_axis=0, concat_axis=1, tiled=True),
        lax.all_to_all(conv_local, "ctx", split_axis=0, concat_axis=1, tiled=True),
    )
    length = filter_raw.shape[1]
    norm_scale = 1.0 / math.sqrt(length)
    filt_re, filt_im = forward_spectrum(filter_raw * norm_scale)
    conv_re, conv_im = forward_spectrum(conv_chan.astype(jnp.float32))
    gate_re, gate_im = forward_spectrum(gate_chan.astype(jnp.float32))
    conv_out = inverse_signal(
        filt_re * conv_re - filt_im * conv_im, filt_re * conv_im + filt_im * conv_re
    ).astype(jnp.bfloat16)
    conv_grad = inverse_signal(
        filt_re * gate_re + filt_im * gate_im, filt_re * gate_im - filt_im * gate_re
    ).astype(jnp.bfloat16)
    cross_re = gate_re * conv_re + gate_im * conv_im
    cross_im = gate_im * conv_re - gate_re * conv_im
    back_out, back_grad = (
        lax.all_to_all(conv_out, "ctx", split_axis=1, concat_axis=0, tiled=True),
        lax.all_to_all(conv_grad, "ctx", split_axis=1, concat_axis=0, tiled=True),
    )
    gate_out = (unit_grad * back_out.astype(jnp.float32)).astype(jnp.bfloat16)
    summed_re, summed_im = (
        lax.psum_scatter(cross_re * norm_scale, "dp", scatter_dimension=0, tiled=True),
        lax.psum_scatter(cross_im * norm_scale, "dp", scatter_dimension=0, tiled=True),
    )
    filter_grad = inverse_signal(summed_re, summed_im)
    return (gate_out[None], back_grad[None], filter_grad)


TABLE_LIMIT_BYTES = 4 * 2**20
VMEM_BYTES = 24 * 2**20


def split_high_low(values):
    high = values.astype(ml_dtypes.bfloat16)
    low = (values - high.astype(np.float64)).astype(ml_dtypes.bfloat16)
    return high, low


@functools.lru_cache(maxsize=None)
def dense_tables(length):
    total = 2 * length
    time = np.arange(length)[:, None]
    freq = np.arange(length)[None, :]
    angle = (time * freq % total) * (2.0 * np.pi / total)
    even_odd = 1.0 - 2.0 * (np.arange(length) % 2)
    real, imag = np.cos(angle), -np.sin(angle)
    imag[:, 0] = even_odd
    weight = np.full((length, 1), 2.0 / total)
    weight[0] = 1.0 / total
    forward = np.concatenate([real, imag], axis=1)
    inverse = np.concatenate([real.T * weight, imag.T * weight], axis=0)
    return split_high_low(forward) + split_high_low(inverse)


def mm(left, right):
    return jnp.dot(left, right, preferred_element_type=jnp.float32)


def mm_nt(left, right):
    return lax.dot_general(left, right, (((1,), (1,)), ((), ())), preferred_element_type=jnp.float32)


def halves(values):
    high = values.astype(jnp.bfloat16)
    return high, (values - high.astype(jnp.float32)).astype(jnp.bfloat16)


def spectrum_product(left, right, conj_left):
    length = left.shape[1] // 2
    lr, li = left[:, :length], left[:, length:]
    rr, ri = right[:, :length], right[:, length:]
    ends = lax.broadcasted_iota(jnp.int32, lr.shape, 1) == 0
    both = li * ri
    if conj_left:
        real = lr * rr + jnp.where(ends, 0.0, both)
        imag = jnp.where(ends, both, lr * ri - li * rr)
    else:
        real = lr * rr - jnp.where(ends, 0.0, both)
        imag = jnp.where(ends, both, lr * ri + li * rr)
    return jnp.concatenate([real, imag], axis=1)


def inverse_dense(spec, inv_hi, inv_lo):
    high, low = halves(spec)
    return mm(high, inv_hi[...]) + mm(low, inv_hi[...]) + mm(high, inv_lo[...])


def place(index, size):
    return pl.ds(pl.multiple_of(index * size, size), size)


def offsets(parts):
    return [0, *reversed(range(1, parts))]


def gather_tokens(pieces, whole, here):
    step = pieces[0].shape[1]
    for k, piece in zip(offsets(len(pieces)), pieces):
        whole[:, place(here ^ k, step)] = piece[...]


def scatter_tokens(whole, pieces, here):
    step = pieces[0].shape[1]
    for k, piece in zip(offsets(len(pieces)), pieces):
        piece[...] = whole[:, place(here ^ k, step)]


def blocks_kernel(source, *refs):
    out, sems = refs[:-1], refs[-1]
    here = lax.axis_index("ctx")
    rows = out[0].shape[0]
    copies = [
        pltpu.make_async_copy(source.at[place(here ^ k, rows), :], ref, sems.at[k])
        for k, ref in zip(offsets(len(out)), out)
    ]
    for copy in copies:
        copy.start()
    for copy in copies:
        copy.wait()


def filt_kernel(scale, filt, fwd_hi, fwd_lo, spec_filt):
    high, low = halves(filt[...] * scale)
    spec_filt[...] = mm(high, fwd_hi[...]) + mm(low, fwd_hi[...]) + mm(high, fwd_lo[...])


def spectrum_of(signal, fwd_hi, fwd_lo):
    return mm(signal, fwd_hi[...]) + mm(signal, fwd_lo[...])


def pair_rows(rows, mine):
    at = lax.axis_index("dp")
    return place(at if mine else 1 - at, rows)


def conv_kernel(parts, *refs):
    conv = refs[:parts]
    spec_filt, fwd_hi, fwd_lo, inv_hi, inv_lo = refs[parts : parts + 5]
    out = refs[parts + 5 : 2 * parts + 5]
    spec_own, send, spec_conv, whole = refs[2 * parts + 5 :]
    here = lax.axis_index("ctx")
    gather_tokens(conv, whole, here)
    rows = send.shape[0]
    send[...] = whole[pair_rows(rows, False), :]
    spec_conv[...] = spectrum_of(whole[...], fwd_hi, fwd_lo)
    product = spectrum_product(spec_filt[...], spec_conv[...], False)
    spec_own[...] = spec_conv[pair_rows(rows, True), :]
    whole[...] = inverse_dense(product, inv_hi, inv_lo).astype(jnp.bfloat16)
    scatter_tokens(whole, out, here)


def unit_kernel(parts, pieces, after, weight, gate, *refs):
    grads = refs[:pieces]
    unit = refs[pieces]
    out = refs[pieces + 1 : pieces + 1 + parts]
    rows_all = refs[pieces + 1 + parts]
    here, block = lax.axis_index("ctx"), lax.axis_index("tp")
    rows = grads[0].shape[0]
    half = rows_all.shape[1] // 2
    for k, ref in enumerate(grads[:3]):
        rows_all[place(block ^ k, rows), :] = ref[...]
    rows_all[place(block ^ 3, rows), :half] = grads[3][...]
    rows_all[place(block ^ 3, rows), half:] = grads[4][...]
    rows = out[0].shape[0]
    unit[...] = mm_nt(weight[...], rows_all[...])
    for k, ref in zip(offsets(parts), out):
        at = place(here ^ k, rows)
        ref[...] = (unit[at, :] * gate[at, :].astype(jnp.float32)).astype(jnp.bfloat16)


def grad_kernel(parts, *refs):
    gate = refs[:parts]
    spec_filt, fwd_hi, fwd_lo, inv_hi, inv_lo = refs[parts : parts + 5]
    out = refs[parts + 5 : 2 * parts + 5]
    spec_own, *send, spec_gate, whole = refs[2 * parts + 5 :]
    here = lax.axis_index("ctx")
    gather_tokens(gate, whole, here)
    rows = spec_own.shape[0]
    for i, ref in enumerate(send):
        at = pair_rows(rows, False).start + i * ref.shape[0]
        ref[...] = whole[pl.ds(pl.multiple_of(at, ref.shape[0]), ref.shape[0]), :]
    spec_gate[...] = spectrum_of(whole[...], fwd_hi, fwd_lo)
    product = spectrum_product(spec_filt[...], spec_gate[...], True)
    spec_own[...] = spec_gate[pair_rows(rows, True), :]
    whole[...] = inverse_dense(product, inv_hi, inv_lo).astype(jnp.bfloat16)
    scatter_tokens(whole, out, here)


def filter_kernel(parts, scale, spec_conv, spec_gate, conv_peer, gate_low, gate_high, *refs):
    fwd_hi, fwd_lo, inv_hi, inv_lo, unit = refs[:5]
    back = refs[5 : 5 + parts]
    filter_grad, out = refs[5 + parts :]
    here = lax.axis_index("ctx")
    rows = back[0].shape[0]
    for k, ref in zip(offsets(parts), back):
        at = place(here ^ k, rows)
        out[at, :] = (unit[at, :] * ref[...].astype(jnp.float32)).astype(jnp.bfloat16)
    conv_peer = spectrum_of(conv_peer[...], fwd_hi, fwd_lo)
    gate_peer = jnp.concatenate([gate_low[...], gate_high[...]], axis=0)
    gate_peer = spectrum_of(gate_peer, fwd_hi, fwd_lo)
    product = spectrum_product(spec_conv[...], spec_gate[...], True)
    product = product + spectrum_product(conv_peer, gate_peer, True)
    filter_grad[...] = inverse_dense(product, inv_hi, inv_lo) * scale


def last_kernel(parts, after, *refs):
    back, out = refs[:parts], refs[parts]
    here = lax.axis_index("ctx")
    rows = back[0].shape[0]
    for k, ref in zip(offsets(parts), back):
        out[place(here ^ k, rows), :] = ref[...]


def call(kernel, outs, args, scratch=(), far=0, cost=1.0):
    vmem = pl.BlockSpec(memory_space=pltpu.VMEM)
    hbm = pl.BlockSpec(memory_space=pltpu.HBM)
    held = [pltpu.with_memory_space_constraint(a, pltpu.HBM) for a in args[:far]]
    return pl.pallas_call(
        kernel,
        out_shape=outs,
        in_specs=[hbm] * far + [vmem] * (len(args) - far),
        out_specs=jax.tree.map(lambda _: vmem, outs),
        scratch_shapes=list(scratch),
        cost_estimate=pl.CostEstimate(
            flops=int(cost * 1e9), bytes_accessed=int(cost * 1e6), transcendentals=0
        ),
        compiler_params=pltpu.CompilerParams(vmem_limit_bytes=VMEM_BYTES),
    )(*held, *args[far:])


def dense_on_device(parts, groups, out_grad, gate_in, conv_in, filter_raw, out_weight):
    f32, bf16 = jnp.float32, jnp.bfloat16
    grad_rows, gate_local, conv_local = out_grad[0], gate_in[0], conv_in[0]
    chans, length = filter_raw.shape
    channels, tokens = conv_local.shape
    width = grad_rows.shape[1]
    scale = 1.0 / math.sqrt(length)
    tables = [jnp.asarray(t) for t in dense_tables(length)]
    shape = jax.ShapeDtypeStruct
    def swap(value, axis, size, k):
        return lax.ppermute(value, axis, [(i, i ^ k) for i in range(size)])

    def exchange(pieces):
        order = offsets(parts)[: len(pieces)]
        return [swap(p, "ctx", parts, k) if k else p for k, p in zip(order, pieces)]

    grad_1 = swap(grad_rows, "tp", groups, 1)
    grad_2 = swap(grad_rows, "tp", groups, 2)
    blocks = call(
        blocks_kernel,
        [shape((chans, tokens), bf16)] * parts,
        [conv_local],
        [pltpu.SemaphoreType.DMA((parts,))],
        far=1,
        cost=10.0,
    )
    conv_pieces = exchange(blocks)
    grad_3a = swap(grad_1[:, : width // 2], "tp", groups, 2)
    grad_3b = swap(grad_2[:, width // 2 :], "tp", groups, 1)

    piece = shape((chans, tokens), bf16)
    spectrum = shape((chans, 2 * length), f32)
    whole = pltpu.VMEM((chans, length), bf16)
    spec_filt = call(
        functools.partial(filt_kernel, scale), spectrum, [filter_raw, *tables[:2]], cost=2.0
    )
    half, half_spectrum = (chans // 2, length), shape((chans // 2, 2 * length), f32)
    work = [pltpu.VMEM(spectrum.shape, f32), whole]
    *conv_out, spec_conv, conv_send = call(
        functools.partial(conv_kernel, parts),
        [piece] * parts + [half_spectrum, shape(half, bf16)],
        [*conv_pieces, spec_filt, *tables],
        work,
        cost=2.0,
    )
    conv_back = exchange(conv_out)

    unit, *gate_pieces = call(
        functools.partial(unit_kernel, parts, 5),
        [shape((channels, tokens), f32)] + [piece] * parts,
        [conv_out[0], out_weight, gate_local, grad_rows, grad_1, grad_2, grad_3a, grad_3b],
        [pltpu.VMEM((groups * grad_rows.shape[0], width), bf16)],
    )
    gate_chan = exchange(gate_pieces)
    quarter = shape((half[0] // 2, length), bf16)
    *conv_grad, spec_gate, send_low, send_high = call(
        functools.partial(grad_kernel, parts),
        [piece] * parts + [half_spectrum, quarter, quarter],
        [*gate_chan, spec_filt, *tables],
        work,
    )
    grad_back = exchange(conv_grad)
    peer = [swap(a, "dp", 2, 1) for a in (conv_send, send_low, send_high)]
    local = shape((channels, tokens), bf16)
    filter_grad, gate_out = call(
        functools.partial(filter_kernel, parts, scale),
        [shape(half, f32), local],
        [spec_conv, spec_gate, *peer, *tables, unit, *conv_back],
        cost=2.0,
    )
    conv_grad_out = call(
        functools.partial(last_kernel, parts), local, [filter_grad, *grad_back], far=1
    )
    return (gate_out[None], conv_grad_out[None], filter_grad)


def solution(mesh):
    placed = (
        P("dp", ("ctx", "tp"), None),
        P("dp", "tp", "ctx"),
        P("dp", "tp", "ctx"),
        P(("tp", "ctx"), None),
        P("tp", None),
    )
    parts, groups, pair = mesh.shape["ctx"], mesh.shape["tp"], mesh.shape["dp"]

    def on_device(out_grad, gate_in, conv_in, filter_raw, out_weight):
        args = (out_grad, gate_in, conv_in, filter_raw, out_weight)
        table = 4 * filter_raw.shape[1] ** 2 * jnp.dtype(jnp.bfloat16).itemsize
        one_sequence = out_grad.shape[0] == 1
        power = parts & (parts - 1) == 0
        if one_sequence and power and parts > 1 and groups == 4 and pair == 2 and table <= TABLE_LIMIT_BYTES:
            return dense_on_device(parts, groups, *args)
        return two_level_on_device(*args)

    return jax.shard_map(
        on_device,
        mesh=mesh,
        in_specs=placed,
        out_specs=(P("dp", "tp", "ctx"), P("dp", "tp", "ctx"), P(("tp", "ctx", "dp"), None)),
        check_vma=False,
    )
```

profile of v0, /device:TPU:0, one launch (start us, length us, event | category | flops | bytes accessed | tf_op | source)
XLA Modules:
  0.0 42.6 jit_solution(10703696880769679581)
XLA Ops:
  0.6 3.0 %collective-permute-start.4 = (bf16[32,4096]{1,0:T(8,128)(2,1)}, bf16[32,4096]{1,0:T(8,128)(2,1)S(1)}, u32[]{:S(2)}, u32[]{:S(2)}) collective-permute-start(bf16[32,4096]{1,0:T(8,128)(2,1)} %bitcast.8), channel_id=1, source_target_pairs={{0,4},{2,6},{4,0},{6,2},{1,5},{3,7},{5,1},{7,3},{8,12},{10,14},{12... | collective-permute-start | bytes 786440 | tf_op jit(solution)/shard_map/ppermute | solution.py:321
  3.7 1.5 %collective-permute-start.3 = (bf16[32,4096]{1,0:T(8,128)(2,1)}, bf16[32,4096]{1,0:T(8,128)(2,1)S(1)}, u32[]{:S(2)}, u32[]{:S(2)}) collective-permute-start(bf16[32,4096]{1,0:T(8,128)(2,1)} %bitcast.9), channel_id=1, source_target_pairs={{0,2},{2,0},{4,6},{6,4},{1,3},{3,1},{5,7},{7,5},{8,10},{10,8},{12,... | collective-permute-start | bytes 786440 | tf_op jit(solution)/shard_map/ppermute | solution.py:321
  5.2 1.1 %shard_map.112 = (bf16[256,128]{1,0:T(8,128)(2,1)S(1)}, bf16[256,128]{1,0:T(8,128)(2,1)S(1)}, bf16[256,128]{1,0:T(8,128)(2,1)S(1)}, bf16[256,128]{1,0:T(8,128)(2,1)S(1)}) custom-call(bf16[1024,128]{1,0:T(8,128)(2,1)} %bitcast.11), custom_call_target="tpu_custom_call" | custom-call | flops 10000000000 | bytes 10000000 | tf_op jit(solution)/shard_map/pallas_call | solution.py:298
  6.4 3.7 %collective-permute-start = (bf16[256,128]{1,0:T(8,128)(2,1)S(1)}, bf16[256,128]{1,0:T(8,128)(2,1)S(1)}, u32[]{:S(2)}, u32[]{:S(2)}) collective-permute-start(bf16[256,128]{1,0:T(8,128)(2,1)S(1)} %get-tuple-element.28), channel_id=1, source_target_pairs={{0,24},{8,16},{16,8},{24,0},{1,25},{9,17},{17,9},{25,1},{2,26},{10... | collective-permute-start | bytes 196616 | tf_op jit(solution)/shard_map/ppermute | solution.py:321
  10.0 0.8 %collective-permute-start.2 = (bf16[256,128]{1,0:T(8,128)(2,1)S(1)}, bf16[256,128]{1,0:T(8,128)(2,1)S(1)}, u32[]{:S(2)}, u32[]{:S(2)}) collective-permute-start(bf16[256,128]{1,0:T(8,128)(2,1)S(1)} %get-tuple-element.30), channel_id=1, source_target_pairs={{0,8},{8,0},{16,24},{24,16},{1,9},{9,1},{17,25},{25,17},{2,10},{10... | collective-permute-start | bytes 196616 | tf_op jit(solution)/shard_map/ppermute | solution.py:321
  10.8 1.0 %shard_map.113.refs_4_ = f32[256,1024]{1,0:T(8,128)S(1)} custom-call(f32[256,512]{1,0:T(8,128)S(1)} %copy-done.6, bf16[512,1024]{1,0:T(8,128)(2,1)S(1)} %copy-done.1, bf16[512,1024]{1,0:T(8,128)(2,1)S(1)} %copy-done), custom_call_target="tpu_custom_call" | custom-call | flops 2000000000 | bytes 2000000 | tf_op jit(solution)/shard_map/pallas_call | solution.py:298
  11.8 0.6 %collective-permute-start.6 = (bf16[32,2048]{1,0:T(8,128)(2,1)S(1)}, bf16[32,2048]{1,0:T(8,128)(2,1)S(1)}, u32[]{:S(2)}, u32[]{:S(2)}) collective-permute-start(bf16[32,2048]{1,0:T(8,128)(2,1)S(1)} %slice.9), channel_id=1, source_target_pairs={{0,2},{2,0},{4,6},{6,4},{1,3},{3,1},{5,7},{7,5},{8,10},{10,8},{12,... | collective-permute-start | bytes 393224 | tf_op jit(solution)/shard_map/ppermute | solution.py:321
  12.5 1.1 %collective-permute-start.5 = (bf16[32,2048]{1,0:T(8,128)(2,1)S(1)}, bf16[32,2048]{1,0:T(8,128)(2,1)S(1)}, u32[]{:S(2)}, u32[]{:S(2)}) collective-permute-start(bf16[32,2048]{1,0:T(8,128)(2,1)S(1)} %slice.8), channel_id=1, source_target_pairs={{0,4},{2,6},{4,0},{6,2},{1,5},{3,7},{5,1},{7,3},{8,12},{10,14},{12... | collective-permute-start | bytes 393224 | tf_op jit(solution)/shard_map/ppermute | solution.py:321
  13.6 1.7 %collective-permute-done.1.refs_2_ = bf16[256,128]{1,0:T(8,128)(2,1)S(1)} collective-permute-done((bf16[256,128]{1,0:T(8,128)(2,1)S(1)}, bf16[256,128]{1,0:T(8,128)(2,1)S(1)}, u32[]{:S(2)}, u32[]{:S(2)}) %collective-permute-start.1) | collective-permute-done | bytes 65568 | tf_op jit(solution)/shard_map/ppermute | solution.py:321
  15.3 1.9 %shard_map.114 = (bf16[256,128]{1,0:T(8,128)(2,1)S(1)}, bf16[256,128]{1,0:T(8,128)(2,1)S(1)}, bf16[256,128]{1,0:T(8,128)(2,1)S(1)}, bf16[256,128]{1,0:T(8,128)(2...) custom-call(bf16[256,128]{1,0:T(8,128)(2,1)S(1)} %get-tuple-element.27.refs_0_, ...), custom_call_target="tpu_custom_call" | custom-call | flops 2000000000 | bytes 2000000 | tf_op jit(solution)/shard_map/pallas_call | solution.py:298
  17.5 2.5 %shard_map.115 = (f32[1024,128]{1,0:T(8,128)S(1)}, bf16[256,128]{1,0:T(8,128)(2,1)S(1)}, bf16[256,128]{1,0:T(8,128)(2,1)S(1)}, bf16[256,128]{1,0:T(8,128)(2,1)S(1)}, bf16[256,128]{1,0:T(8,128)(2,1)S(1)}) custom-call(bf16[256,128]{1,0:T(8,128)(2,1)S(1)} %get-tuple-element.32.after.refs_5_, bf16[1024,4096]{1,0:T(8,128)(2,1)S(1)} %bitcast.6, ...), custom_call_target="tpu_custom_call" | custom-call | flops 1000000000 | bytes 1000000 | tf_op jit(solution)/shard_map/pallas_call | solution.py:298
  20.0 3.7 %collective-permute-start.7 = (bf16[256,128]{1,0:T(8,128)(2,1)S(1)}, bf16[256,128]{1,0:T(8,128)(2,1)S(1)}, u32[]{:S(2)}, u32[]{:S(2)}) collective-permute-start(bf16[256,128]{1,0:T(8,128)(2,1)S(1)} %get-tuple-element.34), channel_id=1, source_target_pairs={{0,24},{8,16},{16,8},{24,0},{1,25},{9,17},{17,9},{25,1},{2,26},{10... | collective-permute-start | bytes 196616 | tf_op jit(solution)/shard_map/ppermute | solution.py:321
  23.7 0.8 %collective-permute-start.9 = (bf16[256,128]{1,0:T(8,128)(2,1)S(1)}, bf16[256,128]{1,0:T(8,128)(2,1)S(1)}, u32[]{:S(2)}, u32[]{:S(2)}) collective-permute-start(bf16[256,128]{1,0:T(8,128)(2,1)S(1)} %get-tuple-element.36), channel_id=1, source_target_pairs={{0,8},{8,0},{16,24},{24,16},{1,9},{9,1},{17,25},{25,17},{2,10},{10... | collective-permute-start | bytes 196616 | tf_op jit(solution)/shard_map/ppermute | solution.py:321
  24.5 3.6 %collective-permute-start.13 = (bf16[256,128]{1,0:T(8,128)(2,1)S(1)}, bf16[256,128]{1,0:T(8,128)(2,1)S(1)}, u32[]{:S(2)}, u32[]{:S(2)}) collective-permute-start(bf16[256,128]{1,0:T(8,128)(2,1)S(1)} %get-tuple-element.42), channel_id=1, source_target_pairs={{0,24},{8,16},{16,8},{24,0},{1,25},{9,17},{17,9},{25,1},{2,26},{10... | collective-permute-start | bytes 196616 | tf_op jit(solution)/shard_map/ppermute | solution.py:321
  28.1 0.8 %collective-permute-start.15 = (bf16[256,128]{1,0:T(8,128)(2,1)S(1)}, bf16[256,128]{1,0:T(8,128)(2,1)S(1)}, u32[]{:S(2)}, u32[]{:S(2)}) collective-permute-start(bf16[256,128]{1,0:T(8,128)(2,1)S(1)} %get-tuple-element.44), channel_id=1, source_target_pairs={{0,8},{8,0},{16,24},{24,16},{1,9},{9,1},{17,25},{25,17},{2,10},{10... | collective-permute-start | bytes 196616 | tf_op jit(solution)/shard_map/ppermute | solution.py:321
  28.9 1.4 %collective-permute-done.8.refs_2_ = bf16[256,128]{1,0:T(8,128)(2,1)S(1)} collective-permute-done((bf16[256,128]{1,0:T(8,128)(2,1)S(1)}, bf16[256,128]{1,0:T(8,128)(2,1)S(1)}, u32[]{:S(2)}, u32[]{:S(2)}) %collective-permute-start.8) | collective-permute-done | bytes 65568 | tf_op jit(solution)/shard_map/ppermute | solution.py:321
  30.3 1.9 %shard_map.116 = (bf16[256,128]{1,0:T(8,128)(2,1)S(1)}, bf16[256,128]{1,0:T(8,128)(2,1)S(1)}, bf16[256,128]{1,0:T(8,128)(2,1)S(1)}, bf16[256,128]{1,0:T(8,128)(2...) custom-call(bf16[256,128]{1,0:T(8,128)(2,1)S(1)} %get-tuple-element.33.refs_0_, ...), custom_call_target="tpu_custom_call" | custom-call | flops 1000000000 | bytes 1000000 | tf_op jit(solution)/shard_map/pallas_call | solution.py:298
  32.2 0.6 %collective-permute-start.11 = (bf16[64,512]{1,0:T(8,128)(2,1)S(1)}, bf16[64,512]{1,0:T(8,128)(2,1)S(1)}, u32[]{:S(2)}, u32[]{:S(2)}) collective-permute-start(bf16[64,512]{1,0:T(8,128)(2,1)S(1)} %get-tuple-element.39), channel_id=1, source_target_pairs={{0,1},{1,0},{2,3},{3,2},{4,5},{5,4},{6,7},{7,6},{8,9},{9,8},{10,11... | collective-permute-start | bytes 196616 | tf_op jit(solution)/shard_map/ppermute | solution.py:321
  32.9 0.8 %collective-permute-done.14.refs_7_ = bf16[256,128]{1,0:T(8,128)(2,1)S(1)} collective-permute-done((bf16[256,128]{1,0:T(8,128)(2,1)S(1)}, bf16[256,128]{1,0:T(8,128)(2,1)S(1)}, u32[]{:S(2)}, u32[]{:S(2)}) %collective-permute-start.14) | collective-permute-done | bytes 65568 | tf_op jit(solution)/shard_map/ppermute | solution.py:321
  33.6 2.0 %collective-permute-start.16 = (bf16[256,128]{1,0:T(8,128)(2,1)S(1)}, bf16[256,128]{1,0:T(8,128)(2,1)S(1)}, u32[]{:S(2)}, u32[]{:S(2)}) collective-permute-start(bf16[256,128]{1,0:T(8,128)(2,1)S(1)} %get-tuple-element.48), channel_id=1, source_target_pairs={{0,24},{8,16},{16,8},{24,0},{1,25},{9,17},{17,9},{25,1},{2,26},{10... | collective-permute-start | bytes 196616 | tf_op jit(solution)/shard_map/ppermute | solution.py:321
  35.7 2.3 %collective-permute-start.18 = (bf16[256,128]{1,0:T(8,128)(2,1)S(1)}, bf16[256,128]{1,0:T(8,128)(2,1)S(1)}, u32[]{:S(2)}, u32[]{:S(2)}) collective-permute-start(bf16[256,128]{1,0:T(8,128)(2,1)S(1)} %get-tuple-element.50), channel_id=1, source_target_pairs={{0,8},{8,0},{16,24},{24,16},{1,9},{9,1},{17,25},{25,17},{2,10},{10... | collective-permute-start | bytes 196616 | tf_op jit(solution)/shard_map/ppermute | solution.py:321
  38.1 2.1 %shard_map.117 = (f32[128,512]{1,0:T(8,128)}, bf16[1024,128]{1,0:T(8,128)(2,1)}) custom-call(f32[128,1024]{1,0:T(8,128)S(1)} %get-tuple-element.31.spec_conv, f32[128,1024]{1,0:T(8,128)S(1)} %get-tuple-element.37.spec_gate, bf16[128,512]{1,0:T(8,128)(2,1)S(1)} %collective-permute-done.10.conv_peer, bf16[64,512]{1,0:T(8,128)(2,1)S(1)} %collective-permute-done.11.gate_low, ...), custom_call_target="tpu_custom_call" | custom-call | flops 2000000000 | bytes 2000000 | tf_op jit(solution)/shard_map/pallas_call | solution.py:298
  40.2 1.7 %collective-permute-done.17.refs_2_ = bf16[256,128]{1,0:T(8,128)(2,1)S(1)} collective-permute-done((bf16[256,128]{1,0:T(8,128)(2,1)S(1)}, bf16[256,128]{1,0:T(8,128)(2,1)S(1)}, u32[]{:S(2)}, u32[]{:S(2)}) %collective-permute-start.17) | collective-permute-done | bytes 65568 | tf_op jit(solution)/shard_map/ppermute | solution.py:321
  41.9 0.7 %shard_map.118 = bf16[1024,128]{1,0:T(8,128)(2,1)} custom-call(f32[128,512]{1,0:T(8,128)} %get-tuple-element.26.after, bf16[256,128]{1,0:T(8,128)(2,1)S(1)} %get-tuple-element.47.refs_0_, bf16[256,128]{1,0:T(8,128)(2,1)S(1)} %collective-permute-done.16.refs_1_, bf16[256,128]{1,0:T(8,128)(2,1)S(1)} %collective-permute-done.17.refs_2_, ...), custom_call_target="tpu_custom_call" | custom-call | flops 1000000000 | bytes 1000000 | tf_op jit(solution)/shard_map/pallas_call | solution.py:298
  (42 shorter events, 0.5 us)
Async XLA Ops:
  0.6 11.2 %collective-permute-start.4 = (bf16[32,4096]{1,0:T(8,128)(2,1)}, bf16[32,4096]{1,0:T(8,128)(2,1)S(1)}, u32[]{:S(2)}, u32[]{:S(2)}) collective-permute-start(bf16[32,4096]{1,0:T(8,128)(2,1)} %bitcast.8), channel_id=1, source_target_pairs={{0,4},{2,6},{4,0},{6,2},{1,5},{3,7},{5,1},{7,3},{8,12},{10,14},{12... | collective-permute-start | bytes 786440 | tf_op jit(solution)/shard_map/ppermute | solution.py:321
  3.7 8.8 %collective-permute-start.3 = (bf16[32,4096]{1,0:T(8,128)(2,1)}, bf16[32,4096]{1,0:T(8,128)(2,1)S(1)}, u32[]{:S(2)}, u32[]{:S(2)}) collective-permute-start(bf16[32,4096]{1,0:T(8,128)(2,1)} %bitcast.9), channel_id=1, source_target_pairs={{0,2},{2,0},{4,6},{6,4},{1,3},{3,1},{5,7},{7,5},{8,10},{10,8},{12,... | collective-permute-start | bytes 786440 | tf_op jit(solution)/shard_map/ppermute | solution.py:321
  5.2 10.1 %copy-start.2 = (bf16[1024,512]{1,0:T(8,128)(2,1)S(1)}, bf16[1024,512]{1,0:T(8,128)(2,1)}, u32[]{:S(2)}) copy-start(bf16[1024,512]{1,0:T(8,128)(2,1)} %constant.11.clone.refs_8_.refs_3_) | copy-start | bytes 3145732
  5.2 10.1 %copy-start.3 = (bf16[1024,512]{1,0:T(8,128)(2,1)S(1)}, bf16[1024,512]{1,0:T(8,128)(2,1)}, u32[]{:S(2)}) copy-start(bf16[1024,512]{1,0:T(8,128)(2,1)} %constant.10.clone.refs_7_.refs_2_) | copy-start | bytes 3145732
  6.3 11.2 %slice-start = ((s8[8388608]{0:T(1024)(128)(4,1)}), s8[4194304]{0:T(1024)(128)(4,1)S(1)}, s32[]{:S(2)}) async-start(s8[8388608]{0:T(1024)(128)(4,1)} %bitcast.5), calls=%async_computation | async-start | bytes 8388608
  6.3 11.2 %copy-start.4 = (bf16[1,1024,128]{2,1,0:T(8,128)(2,1)S(1)}, bf16[1,1024,128]{2,1,0:T(8,128)(2,1)}, u32[]{:S(2)}) copy-start(bf16[1,1024,128]{2,1,0:T(8,128)(2,1)} %param.10) | copy-start | bytes 786436
  6.3 11.2 %copy-start.5 = (bf16[1,32,4096]{2,1,0:T(8,128)(2,1)S(1)}, bf16[1,32,4096]{2,1,0:T(8,128)(2,1)}, u32[]{:S(2)}) copy-start(bf16[1,32,4096]{2,1,0:T(8,128)(2,1)} %param.9) | copy-start | bytes 786436
  6.4 7.2 %collective-permute-start = (bf16[256,128]{1,0:T(8,128)(2,1)S(1)}, bf16[256,128]{1,0:T(8,128)(2,1)S(1)}, u32[]{:S(2)}, u32[]{:S(2)}) collective-permute-start(bf16[256,128]{1,0:T(8,128)(2,1)S(1)} %get-tuple-element.28), channel_id=1, source_target_pairs={{0,24},{8,16},{16,8},{24,0},{1,25},{9,17},{17,9},{25,1},{2,26},{10... | collective-permute-start | bytes 196616 | tf_op jit(solution)/shard_map/ppermute | solution.py:321
  10.0 5.2 %collective-permute-start.1 = (bf16[256,128]{1,0:T(8,128)(2,1)S(1)}, bf16[256,128]{1,0:T(8,128)(2,1)S(1)}, u32[]{:S(2)}, u32[]{:S(2)}) collective-permute-start(bf16[256,128]{1,0:T(8,128)(2,1)S(1)} %get-tuple-element.29), channel_id=1, source_target_pairs={{0,16},{8,24},{16,0},{24,8},{1,17},{9,25},{17,1},{25,9},{2,18},{10... | collective-permute-start | bytes 196616 | tf_op jit(solution)/shard_map/ppermute | solution.py:321
  10.0 5.2 %collective-permute-start.2 = (bf16[256,128]{1,0:T(8,128)(2,1)S(1)}, bf16[256,128]{1,0:T(8,128)(2,1)S(1)}, u32[]{:S(2)}, u32[]{:S(2)}) collective-permute-start(bf16[256,128]{1,0:T(8,128)(2,1)S(1)} %get-tuple-element.30), channel_id=1, source_target_pairs={{0,8},{8,0},{16,24},{24,16},{1,9},{9,1},{17,25},{25,17},{2,10},{10... | collective-permute-start | bytes 196616 | tf_op jit(solution)/shard_map/ppermute | solution.py:321
  11.8 5.4 %collective-permute-start.6 = (bf16[32,2048]{1,0:T(8,128)(2,1)S(1)}, bf16[32,2048]{1,0:T(8,128)(2,1)S(1)}, u32[]{:S(2)}, u32[]{:S(2)}) collective-permute-start(bf16[32,2048]{1,0:T(8,128)(2,1)S(1)} %slice.9), channel_id=1, source_target_pairs={{0,2},{2,0},{4,6},{6,4},{1,3},{3,1},{5,7},{7,5},{8,10},{10,8},{12,... | collective-permute-start | bytes 393224 | tf_op jit(solution)/shard_map/ppermute | solution.py:321
  12.5 5.0 %collective-permute-start.5 = (bf16[32,2048]{1,0:T(8,128)(2,1)S(1)}, bf16[32,2048]{1,0:T(8,128)(2,1)S(1)}, u32[]{:S(2)}, u32[]{:S(2)}) collective-permute-start(bf16[32,2048]{1,0:T(8,128)(2,1)S(1)} %slice.8), channel_id=1, source_target_pairs={{0,4},{2,6},{4,0},{6,2},{1,5},{3,7},{5,1},{7,3},{8,12},{10,14},{12... | collective-permute-start | bytes 393224 | tf_op jit(solution)/shard_map/ppermute | solution.py:321
  20.0 8.1 %collective-permute-start.7 = (bf16[256,128]{1,0:T(8,128)(2,1)S(1)}, bf16[256,128]{1,0:T(8,128)(2,1)S(1)}, u32[]{:S(2)}, u32[]{:S(2)}) collective-permute-start(bf16[256,128]{1,0:T(8,128)(2,1)S(1)} %get-tuple-element.34), channel_id=1, source_target_pairs={{0,24},{8,16},{16,8},{24,0},{1,25},{9,17},{17,9},{25,1},{2,26},{10... | collective-permute-start | bytes 196616 | tf_op jit(solution)/shard_map/ppermute | solution.py:321
  23.7 6.6 %collective-permute-start.8 = (bf16[256,128]{1,0:T(8,128)(2,1)S(1)}, bf16[256,128]{1,0:T(8,128)(2,1)S(1)}, u32[]{:S(2)}, u32[]{:S(2)}) collective-permute-start(bf16[256,128]{1,0:T(8,128)(2,1)S(1)} %get-tuple-element.35), channel_id=1, source_target_pairs={{0,16},{8,24},{16,0},{24,8},{1,17},{9,25},{17,1},{25,9},{2,18},{10... | collective-permute-start | bytes 196616 | tf_op jit(solution)/shard_map/ppermute | solution.py:321
  23.7 6.6 %collective-permute-start.9 = (bf16[256,128]{1,0:T(8,128)(2,1)S(1)}, bf16[256,128]{1,0:T(8,128)(2,1)S(1)}, u32[]{:S(2)}, u32[]{:S(2)}) collective-permute-start(bf16[256,128]{1,0:T(8,128)(2,1)S(1)} %get-tuple-element.36), channel_id=1, source_target_pairs={{0,8},{8,0},{16,24},{24,16},{1,9},{9,1},{17,25},{25,17},{2,10},{10... | collective-permute-start | bytes 196616 | tf_op jit(solution)/shard_map/ppermute | solution.py:321
  24.5 8.3 %collective-permute-start.13 = (bf16[256,128]{1,0:T(8,128)(2,1)S(1)}, bf16[256,128]{1,0:T(8,128)(2,1)S(1)}, u32[]{:S(2)}, u32[]{:S(2)}) collective-permute-start(bf16[256,128]{1,0:T(8,128)(2,1)S(1)} %get-tuple-element.42), channel_id=1, source_target_pairs={{0,24},{8,16},{16,8},{24,0},{1,25},{9,17},{17,9},{25,1},{2,26},{10... | collective-permute-start | bytes 196616 | tf_op jit(solution)/shard_map/ppermute | solution.py:321
  28.1 5.6 %collective-permute-start.14 = (bf16[256,128]{1,0:T(8,128)(2,1)S(1)}, bf16[256,128]{1,0:T(8,128)(2,1)S(1)}, u32[]{:S(2)}, u32[]{:S(2)}) collective-permute-start(bf16[256,128]{1,0:T(8,128)(2,1)S(1)} %get-tuple-element.43), channel_id=1, source_target_pairs={{0,16},{8,24},{16,0},{24,8},{1,17},{9,25},{17,1},{25,9},{2,18},{10... | collective-permute-start | bytes 196616 | tf_op jit(solution)/shard_map/ppermute | solution.py:321
  28.1 7.6 %collective-permute-start.15 = (bf16[256,128]{1,0:T(8,128)(2,1)S(1)}, bf16[256,128]{1,0:T(8,128)(2,1)S(1)}, u32[]{:S(2)}, u32[]{:S(2)}) collective-permute-start(bf16[256,128]{1,0:T(8,128)(2,1)S(1)} %get-tuple-element.44), channel_id=1, source_target_pairs={{0,8},{8,0},{16,24},{24,16},{1,9},{9,1},{17,25},{25,17},{2,10},{10... | collective-permute-start | bytes 196616 | tf_op jit(solution)/shard_map/ppermute | solution.py:321
  30.3 5.4 %collective-permute-start.10 = (bf16[128,512]{1,0:T(8,128)(2,1)S(1)}, bf16[128,512]{1,0:T(8,128)(2,1)S(1)}, u32[]{:S(2)}, u32[]{:S(2)}) collective-permute-start(bf16[128,512]{1,0:T(8,128)(2,1)S(1)} %get-tuple-element.38), channel_id=1, source_target_pairs={{0,1},{1,0},{2,3},{3,2},{4,5},{5,4},{6,7},{7,6},{8,9},{9,8},{10,11... | collective-permute-start | bytes 393224 | tf_op jit(solution)/shard_map/ppermute | solution.py:321
  32.2 5.9 %collective-permute-start.11 = (bf16[64,512]{1,0:T(8,128)(2,1)S(1)}, bf16[64,512]{1,0:T(8,128)(2,1)S(1)}, u32[]{:S(2)}, u32[]{:S(2)}) collective-permute-start(bf16[64,512]{1,0:T(8,128)(2,1)S(1)} %get-tuple-element.39), channel_id=1, source_target_pairs={{0,1},{1,0},{2,3},{3,2},{4,5},{5,4},{6,7},{7,6},{8,9},{9,8},{10,11... | collective-permute-start | bytes 196616 | tf_op jit(solution)/shard_map/ppermute | solution.py:321
  32.8 5.3 %collective-permute-start.12 = (bf16[64,512]{1,0:T(8,128)(2,1)S(1)}, bf16[64,512]{1,0:T(8,128)(2,1)S(1)}, u32[]{:S(2)}, u32[]{:S(2)}) collective-permute-start(bf16[64,512]{1,0:T(8,128)(2,1)S(1)} %get-tuple-element.40), channel_id=1, source_target_pairs={{0,1},{1,0},{2,3},{3,2},{4,5},{5,4},{6,7},{7,6},{8,9},{9,8},{10,11... | collective-permute-start | bytes 196616 | tf_op jit(solution)/shard_map/ppermute | solution.py:321
  33.6 6.5 %collective-permute-start.16 = (bf16[256,128]{1,0:T(8,128)(2,1)S(1)}, bf16[256,128]{1,0:T(8,128)(2,1)S(1)}, u32[]{:S(2)}, u32[]{:S(2)}) collective-permute-start(bf16[256,128]{1,0:T(8,128)(2,1)S(1)} %get-tuple-element.48), channel_id=1, source_target_pairs={{0,24},{8,16},{16,8},{24,0},{1,25},{9,17},{17,9},{25,1},{2,26},{10... | collective-permute-start | bytes 196616 | tf_op jit(solution)/shard_map/ppermute | solution.py:321
  35.7 6.2 %collective-permute-start.17 = (bf16[256,128]{1,0:T(8,128)(2,1)S(1)}, bf16[256,128]{1,0:T(8,128)(2,1)S(1)}, u32[]{:S(2)}, u32[]{:S(2)}) collective-permute-start(bf16[256,128]{1,0:T(8,128)(2,1)S(1)} %get-tuple-element.49), channel_id=1, source_target_pairs={{0,16},{8,24},{16,0},{24,8},{1,17},{9,25},{17,1},{25,9},{2,18},{10... | collective-permute-start | bytes 196616 | tf_op jit(solution)/shard_map/ppermute | solution.py:321
  35.7 6.2 %collective-permute-start.18 = (bf16[256,128]{1,0:T(8,128)(2,1)S(1)}, bf16[256,128]{1,0:T(8,128)(2,1)S(1)}, u32[]{:S(2)}, u32[]{:S(2)}) collective-permute-start(bf16[256,128]{1,0:T(8,128)(2,1)S(1)} %get-tuple-element.50), channel_id=1, source_target_pairs={{0,8},{8,0},{16,24},{24,16},{1,9},{9,1},{17,25},{25,17},{2,10},{10... | collective-permute-start | bytes 196616 | tf_op jit(solution)/shard_map/ppermute | solution.py:321
  (4 other events, 22.6 us)
where the time goes:
time: 42.8 us; the launch traced here: 42.6 us
  starting transfers between devices  24.6 us (57%)
  Pallas kernels  11.2 us (26%)
  waiting for transfers between devices  5.94 us (14%)
  between operations  0.79 us (2%)
    ppermute x19, starting transfers between devices, swap(): return lax.ppermute(value, axis, [(i, i ^ k) for i in range(size)])  24.6 us
    pallas_call x7, Pallas kernels, call(): pl.pallas_call(kernel, out_shape=outs, in_specs=[hbm] * far + [vmem] * (l...  11.2 us
    ppermute x19, waiting for transfers between devices, swap(): return lax.ppermute(value, axis, [(i, i ^ k) for i in range(size)])  5.94 us
  transfers between devices with their start and end apart: 19, of which 5 were waited for; matrix products, arithmetic and copies ran while one was open for 0% of the time, Pallas kernels for 19%

commit v1 on v0

--- a/solution.py
+++ b/solution.py
@@ -179,9 +179,9 @@
         whole[:, place(here ^ k, step)] = piece[...]
 
 
-def scatter_tokens(whole, pieces, here):
+def scatter_tokens(whole, pieces, here, order):
     step = pieces[0].shape[1]
-    for k, piece in zip(offsets(len(pieces)), pieces):
+    for k, piece in zip(order, pieces):
         piece[...] = whole[:, place(here ^ k, step)]
 
 
@@ -199,7 +199,7 @@
         copy.wait()
 
 
-def filt_kernel(scale, filt, fwd_hi, fwd_lo, spec_filt):
+def filt_kernel(scale, filt, fwd_hi, fwd_lo, after_1, after_2, spec_filt):
     high, low = halves(filt[...] * scale)
     spec_filt[...] = mm(high, fwd_hi[...]) + mm(low, fwd_hi[...]) + mm(high, fwd_lo[...])
 
@@ -217,16 +217,13 @@
     conv = refs[:parts]
     spec_filt, fwd_hi, fwd_lo, inv_hi, inv_lo = refs[parts : parts + 5]
     out = refs[parts + 5 : 2 * parts + 5]
-    spec_own, send, spec_conv, whole = refs[2 * parts + 5 :]
+    spec_conv, whole = refs[2 * parts + 5 :]
     here = lax.axis_index("ctx")
     gather_tokens(conv, whole, here)
-    rows = send.shape[0]
-    send[...] = whole[pair_rows(rows, False), :]
     spec_conv[...] = spectrum_of(whole[...], fwd_hi, fwd_lo)
     product = spectrum_product(spec_filt[...], spec_conv[...], False)
-    spec_own[...] = spec_conv[pair_rows(rows, True), :]
     whole[...] = inverse_dense(product, inv_hi, inv_lo).astype(jnp.bfloat16)
-    scatter_tokens(whole, out, here)
+    scatter_tokens(whole, out, here, offsets(parts))
 
 
 def unit_kernel(parts, pieces, after, weight, gate, *refs):
@@ -252,60 +249,63 @@
     gate = refs[:parts]
     spec_filt, fwd_hi, fwd_lo, inv_hi, inv_lo = refs[parts : parts + 5]
     out = refs[parts + 5 : 2 * parts + 5]
-    spec_own, *send, spec_gate, whole = refs[2 * parts + 5 :]
+    spec_gate, whole = refs[2 * parts + 5 :]
     here = lax.axis_index("ctx")
     gather_tokens(gate, whole, here)
-    rows = spec_own.shape[0]
-    for i, ref in enumerate(send):
-        at = pair_rows(rows, False).start + i * ref.shape[0]
-        ref[...] = whole[pl.ds(pl.multiple_of(at, ref.shape[0]), ref.shape[0]), :]
     spec_gate[...] = spectrum_of(whole[...], fwd_hi, fwd_lo)
     product = spectrum_product(spec_filt[...], spec_gate[...], True)
-    spec_own[...] = spec_gate[pair_rows(rows, True), :]
     whole[...] = inverse_dense(product, inv_hi, inv_lo).astype(jnp.bfloat16)
-    scatter_tokens(whole, out, here)
-
-
-def filter_kernel(parts, scale, spec_conv, spec_gate, conv_peer, gate_low, gate_high, *refs):
-    fwd_hi, fwd_lo, inv_hi, inv_lo, unit = refs[:5]
-    back = refs[5 : 5 + parts]
-    filter_grad, out = refs[5 + parts :]
+    scatter_tokens(whole, out, here, offsets(parts))
+
+
+def filter_kernel(parts, scale, spec_conv, spec_gate, inv_hi, inv_lo, unit, *refs):
+    back = refs[:parts]
+    keep, *send, out, whole = refs[parts:]
     here = lax.axis_index("ctx")
     rows = back[0].shape[0]
     for k, ref in zip(offsets(parts), back):
         at = place(here ^ k, rows)
         out[at, :] = (unit[at, :] * ref[...].astype(jnp.float32)).astype(jnp.bfloat16)
-    conv_peer = spectrum_of(conv_peer[...], fwd_hi, fwd_lo)
-    gate_peer = jnp.concatenate([gate_low[...], gate_high[...]], axis=0)
-    gate_peer = spectrum_of(gate_peer, fwd_hi, fwd_lo)
     product = spectrum_product(spec_conv[...], spec_gate[...], True)
-    product = product + spectrum_product(conv_peer, gate_peer, True)
-    filter_grad[...] = inverse_dense(product, inv_hi, inv_lo) * scale
-
-
-def last_kernel(parts, after, *refs):
-    back, out = refs[:parts], refs[parts]
+    whole[...] = inverse_dense(product, inv_hi, inv_lo) * scale
+    rows = keep.shape[0]
+    keep[...] = whole[pair_rows(rows, True), :]
+    for i, ref in enumerate(send):
+        step = ref.shape[0]
+        at = pl.multiple_of(pair_rows(rows, False).start + i * step, step)
+        ref[...] = whole[pl.ds(at, step), :].astype(jnp.bfloat16)
+
+
+def last_kernel(parts, *refs):
+    back, (low, high, keep, total, out) = refs[:parts], refs[parts:]
+    step = low.shape[0]
+    for i, ref in enumerate((low, high)):
+        at = slice(i * step, (i + 1) * step)
+        total[at, :] = keep[at, :] + ref[...].astype(jnp.float32)
     here = lax.axis_index("ctx")
     rows = back[0].shape[0]
     for k, ref in zip(offsets(parts), back):
         out[place(here ^ k, rows), :] = ref[...]
 
 
-def call(kernel, outs, args, scratch=(), far=0, cost=1.0):
+def call(kernel, outs, args, scratch=(), far=(), cost=1.0):
     vmem = pl.BlockSpec(memory_space=pltpu.VMEM)
     hbm = pl.BlockSpec(memory_space=pltpu.HBM)
-    held = [pltpu.with_memory_space_constraint(a, pltpu.HBM) for a in args[:far]]
+    held = [
+        pltpu.with_memory_space_constraint(a, pltpu.HBM) if i in far else a
+        for i, a in enumerate(args)
+    ]
     return pl.pallas_call(
         kernel,
         out_shape=outs,
-        in_specs=[hbm] * far + [vmem] * (len(args) - far),
+        in_specs=[hbm if i in far else vmem for i in range(len(args))],
         out_specs=jax.tree.map(lambda _: vmem, outs),
         scratch_shapes=list(scratch),
         cost_estimate=pl.CostEstimate(
             flops=int(cost * 1e9), bytes_accessed=int(cost * 1e6), transcendentals=0
         ),
         compiler_params=pltpu.CompilerParams(vmem_limit_bytes=VMEM_BYTES),
-    )(*held, *args[far:])
+    )(*held)
 
 
 def dense_on_device(parts, groups, out_grad, gate_in, conv_in, filter_raw, out_weight):
@@ -320,8 +320,7 @@
     def swap(value, axis, size, k):
         return lax.ppermute(value, axis, [(i, i ^ k) for i in range(size)])
 
-    def exchange(pieces):
-        order = offsets(parts)[: len(pieces)]
+    def exchange(pieces, order):
         return [swap(p, "ctx", parts, k) if k else p for k, p in zip(order, pieces)]
 
     grad_1 = swap(grad_rows, "tp", groups, 1)
@@ -331,10 +330,10 @@
         [shape((chans, tokens), bf16)] * parts,
         [conv_local],
         [pltpu.SemaphoreType.DMA((parts,))],
-        far=1,
+        far=(0,),
         cost=10.0,
     )
-    conv_pieces = exchange(blocks)
+    conv_pieces = exchange(blocks, offsets(parts))
     grad_3a = swap(grad_1[:, : width // 2], "tp", groups, 2)
     grad_3b = swap(grad_2[:, width // 2 :], "tp", groups, 1)
 
@@ -342,18 +341,19 @@
     spectrum = shape((chans, 2 * length), f32)
     whole = pltpu.VMEM((chans, length), bf16)
     spec_filt = call(
-        functools.partial(filt_kernel, scale), spectrum, [filter_raw, *tables[:2]], cost=2.0
-    )
-    half, half_spectrum = (chans // 2, length), shape((chans // 2, 2 * length), f32)
-    work = [pltpu.VMEM(spectrum.shape, f32), whole]
-    *conv_out, spec_conv, conv_send = call(
+        functools.partial(filt_kernel, scale),
+        spectrum,
+        [filter_raw, *tables[:2], grad_1, grad_2],
+        cost=2.0,
+    )
+    *conv_out, spec_conv = call(
         functools.partial(conv_kernel, parts),
-        [piece] * parts + [half_spectrum, shape(half, bf16)],
+        [piece] * parts + [spectrum],
         [*conv_pieces, spec_filt, *tables],
-        work,
+        [whole],
         cost=2.0,
     )
-    conv_back = exchange(conv_out)
+    conv_back = exchange(conv_out, offsets(parts))
 
     unit, *gate_pieces = call(
         functools.partial(unit_kernel, parts, 5),
@@ -361,25 +361,27 @@
         [conv_out[0], out_weight, gate_local, grad_rows, grad_1, grad_2, grad_3a, grad_3b],
         [pltpu.VMEM((groups * grad_rows.shape[0], width), bf16)],
     )
-    gate_chan = exchange(gate_pieces)
-    quarter = shape((half[0] // 2, length), bf16)
-    *conv_grad, spec_gate, send_low, send_high = call(
+    gate_chan = exchange(gate_pieces, offsets(parts))
+    *conv_grad, spec_gate = call(
         functools.partial(grad_kernel, parts),
-        [piece] * parts + [half_spectrum, quarter, quarter],
+        [piece] * parts + [spectrum],
         [*gate_chan, spec_filt, *tables],
-        work,
-    )
-    grad_back = exchange(conv_grad)
-    peer = [swap(a, "dp", 2, 1) for a in (conv_send, send_low, send_high)]
-    local = shape((channels, tokens), bf16)
-    filter_grad, gate_out = call(
+        [whole],
+    )
+    grad_back = exchange(conv_grad, offsets(parts))
+    half, local = shape((chans // 2, length), f32), shape((channels, tokens), bf16)
+    quarter = shape((chans // 4, length), bf16)
+    keep, send_low, send_high, gate_out = call(
         functools.partial(filter_kernel, parts, scale),
-        [shape(half, f32), local],
-        [spec_conv, spec_gate, *peer, *tables, unit, *conv_back],
+        [half, quarter, quarter, local],
+        [spec_conv, spec_gate, *tables[2:], unit, *conv_back],
+        [pltpu.VMEM((chans, length), f32)],
         cost=2.0,
     )
-    conv_grad_out = call(
-        functools.partial(last_kernel, parts), local, [filter_grad, *grad_back], far=1
+    filter_grad, conv_grad_out = call(
+        functools.partial(last_kernel, parts),
+        [half, local],
+        [*grad_back, swap(send_low, "dp", 2, 1), swap(send_high, "dp", 2, 1), keep],
     )
     return (gate_out[None], conv_grad_out[None], filter_grad)
 

time: 42.8 us -> 40.5 us (0.946)
  waiting for transfers between devices: 5.94 us -> 3.34 us
  starting transfers between devices: 24.6 us -> 25.5 us
  Pallas kernels: 11.2 us -> 10.7 us
    ppermute x19 -> x18, waiting for transfers between devices: 5.94 us -> 3.34 us  [swap(): return lax.ppermute(value, axis, [(i, i ^ k) for i in range(size)])]
    ppermute x19 -> x18, starting transfers between devices: 24.6 us -> 25.5 us  [swap(): return lax.ppermute(value, axis, [(i, i ^ k) for i in range(size)])]
    pallas_call x7, Pallas kernels: 11.2 us -> 10.7 us  [call(): pl.pallas_call(kernel, out_shape=outs, in_specs=[hbm if i in far else vme...]
  transfers between devices with their start and end apart: 19 -> 18, of which waited for: 5 -> 3; matrix products, arithmetic and copies ran while one was open for 0% -> 0% of each run, Pallas kernels for 19% -> 18%
where the time goes in v1:
time: 40.5 us; the launch traced here: 40.4 us
  starting transfers between devices  25.5 us (63%)
  Pallas kernels  10.7 us (26%)
  waiting for transfers between devices  3.34 us (8%)
  between operations  0.81 us (2%)
    ppermute x18, starting transfers between devices, swap(): return lax.ppermute(value, axis, [(i, i ^ k) for i in range(size)])  25.5 us
    pallas_call x7, Pallas kernels, call(): pl.pallas_call(kernel, out_shape=outs, in_specs=[hbm if i in far else vme...  10.7 us
    ppermute x18, waiting for transfers between devices, swap(): return lax.ppermute(value, axis, [(i, i ^ k) for i in range(size)])  3.34 us
  transfers between devices with their start and end apart: 18, of which 3 were waited for; matrix products, arithmetic and copies ran while one was open for 0% of the time, Pallas kernels for 18%

profile of v1, /device:TPU:0, one launch (start us, length us, event | category | flops | bytes accessed | tf_op | source)
XLA Modules:
  0.0 40.4 jit_solution(6249858497569859729)
XLA Ops:
  0.6 3.0 %collective-permute-start.4 = (bf16[32,4096]{1,0:T(8,128)(2,1)}, bf16[32,4096]{1,0:T(8,128)(2,1)S(1)}, u32[]{:S(2)}, u32[]{:S(2)}) collective-permute-start(bf16[32,4096]{1,0:T(8,128)(2,1)} %bitcast.7), channel_id=1, source_target_pairs={{0,4},{2,6},{4,0},{6,2},{1,5},{3,7},{5,1},{7,3},{8,12},{10,14},{12... | collective-permute-start | bytes 786440 | tf_op jit(solution)/shard_map/ppermute | solution.py:321
  3.7 1.5 %collective-permute-start.3 = (bf16[32,4096]{1,0:T(8,128)(2,1)}, bf16[32,4096]{1,0:T(8,128)(2,1)S(1)}, u32[]{:S(2)}, u32[]{:S(2)}) collective-permute-start(bf16[32,4096]{1,0:T(8,128)(2,1)} %bitcast.8), channel_id=1, source_target_pairs={{0,2},{2,0},{4,6},{6,4},{1,3},{3,1},{5,7},{7,5},{8,10},{10,8},{12,... | collective-permute-start | bytes 786440 | tf_op jit(solution)/shard_map/ppermute | solution.py:321
  5.2 1.1 %shard_map.112 = (bf16[256,128]{1,0:T(8,128)(2,1)S(1)}, bf16[256,128]{1,0:T(8,128)(2,1)S(1)}, bf16[256,128]{1,0:T(8,128)(2,1)S(1)}, bf16[256,128]{1,0:T(8,128)(2,1)S(1)}) custom-call(bf16[1024,128]{1,0:T(8,128)(2,1)} %bitcast.11), custom_call_target="tpu_custom_call" | custom-call | flops 10000000000 | bytes 10000000 | tf_op jit(solution)/shard_map/pallas_call | solution.py:298
  6.4 3.7 %collective-permute-start = (bf16[256,128]{1,0:T(8,128)(2,1)S(1)}, bf16[256,128]{1,0:T(8,128)(2,1)S(1)}, u32[]{:S(2)}, u32[]{:S(2)}) collective-permute-start(bf16[256,128]{1,0:T(8,128)(2,1)S(1)} %get-tuple-element.29), channel_id=1, source_target_pairs={{0,24},{8,16},{16,8},{24,0},{1,25},{9,17},{17,9},{25,1},{2,26},{10... | collective-permute-start | bytes 196616 | tf_op jit(solution)/shard_map/ppermute | solution.py:321
  10.0 0.8 %collective-permute-start.2 = (bf16[256,128]{1,0:T(8,128)(2,1)S(1)}, bf16[256,128]{1,0:T(8,128)(2,1)S(1)}, u32[]{:S(2)}, u32[]{:S(2)}) collective-permute-start(bf16[256,128]{1,0:T(8,128)(2,1)S(1)} %get-tuple-element.31), channel_id=1, source_target_pairs={{0,8},{8,0},{16,24},{24,16},{1,9},{9,1},{17,25},{25,17},{2,10},{10... | collective-permute-start | bytes 196616 | tf_op jit(solution)/shard_map/ppermute | solution.py:321
  10.8 1.1 %collective-permute-start.6 = (bf16[32,2048]{1,0:T(8,128)(2,1)S(1)}, bf16[32,2048]{1,0:T(8,128)(2,1)S(1)}, u32[]{:S(2)}, u32[]{:S(2)}) collective-permute-start(bf16[32,2048]{1,0:T(8,128)(2,1)S(1)} %slice.9), channel_id=1, source_target_pairs={{0,2},{2,0},{4,6},{6,4},{1,3},{3,1},{5,7},{7,5},{8,10},{10,8},{12,... | collective-permute-start | bytes 393224 | tf_op jit(solution)/shard_map/ppermute | solution.py:321
  12.0 0.0 slice-start.1
  12.0 1.6 %collective-permute-start.5 = (bf16[32,2048]{1,0:T(8,128)(2,1)S(1)}, bf16[32,2048]{1,0:T(8,128)(2,1)S(1)}, u32[]{:S(2)}, u32[]{:S(2)}) collective-permute-start(bf16[32,2048]{1,0:T(8,128)(2,1)S(1)} %slice.8), channel_id=1, source_target_pairs={{0,4},{2,6},{4,0},{6,2},{1,5},{3,7},{5,1},{7,3},{8,12},{10,14},{12... | collective-permute-start | bytes 393224 | tf_op jit(solution)/shard_map/ppermute | solution.py:321
  13.6 1.0 %shard_map.113.refs_4_ = f32[256,1024]{1,0:T(8,128)S(1)} custom-call(f32[256,512]{1,0:T(8,128)S(1)} %copy-done.6, bf16[512,1024]{1,0:T(8,128)(2,1)S(1)} %copy-done.3, bf16[512,1024]{1,0:T(8,128)(2,1)S(1)} %copy-done.2, bf16[32,4096]{1,0:T(8,128)(2,1)S(1)} %collective-permute-done.3.after_1.refs_1_, bf16[32,4096]{1,0:T(8,128)(2,1)S(1)} %collective-permute-done.4.after_2.refs_2_), custom_call_target="tpu_custom_call" | custom-call | flops 2000000000 | bytes 2000000 | tf_op jit(solution)/shard_map/pallas_call | solution.py:298
  14.6 0.7 %collective-permute-done.1.refs_2_ = bf16[256,128]{1,0:T(8,128)(2,1)S(1)} collective-permute-done((bf16[256,128]{1,0:T(8,128)(2,1)S(1)}, bf16[256,128]{1,0:T(8,128)(2,1)S(1)}, u32[]{:S(2)}, u32[]{:S(2)}) %collective-permute-start.1) | collective-permute-done | bytes 65568 | tf_op jit(solution)/shard_map/ppermute | solution.py:321
  15.3 1.7 %shard_map.114 = (bf16[256,128]{1,0:T(8,128)(2,1)S(1)}, bf16[256,128]{1,0:T(8,128)(2,1)S(1)}, bf16[256,128]{1,0:T(8,128)(2,1)S(1)}, bf16[256,128]{1,0:T(8,128)(2,1)S(1)}, f32[256,1024]{1,0:T(8,128)S(1)}) custom-call(bf16[256,128]{1,0:T(8,128)(2,1)S(1)} %get-tuple-element.28.refs_0_, bf16[256,128]{1,0:T(8,128)(2,1)S(1)} %collective-permute-done.refs_1_, ...), custom_call_target="tpu_custom_call" | custom-call | flops 2000000000 | bytes 2000000 | tf_op jit(solution)/shard_map/pallas_call | solution.py:298
  17.1 2.5 %shard_map.115 = (f32[1024,128]{1,0:T(8,128)S(1)}, bf16[256,128]{1,0:T(8,128)(2,1)S(1)}, bf16[256,128]{1,0:T(8,128)(2,1)S(1)}, bf16[256,128]{1,0:T(8,128)(2,1)S(1)}, bf16[256,128]{1,0:T(8,128)(2,1)S(1)}) custom-call(bf16[256,128]{1,0:T(8,128)(2,1)S(1)} %get-tuple-element.33.after.refs_0_, bf16[1024,4096]{1,0:T(8,128)(2,1)S(1)} %bitcast.6, ...), custom_call_target="tpu_custom_call" | custom-call | flops 1000000000 | bytes 1000000 | tf_op jit(solution)/shard_map/pallas_call | solution.py:298
  19.6 3.6 %collective-permute-start.7 = (bf16[256,128]{1,0:T(8,128)(2,1)S(1)}, bf16[256,128]{1,0:T(8,128)(2,1)S(1)}, u32[]{:S(2)}, u32[]{:S(2)}) collective-permute-start(bf16[256,128]{1,0:T(8,128)(2,1)S(1)} %get-tuple-element.35), channel_id=1, source_target_pairs={{0,24},{8,16},{16,8},{24,0},{1,25},{9,17},{17,9},{25,1},{2,26},{10... | collective-permute-start | bytes 196616 | tf_op jit(solution)/shard_map/ppermute | solution.py:321
  23.2 0.8 %collective-permute-start.9 = (bf16[256,128]{1,0:T(8,128)(2,1)S(1)}, bf16[256,128]{1,0:T(8,128)(2,1)S(1)}, u32[]{:S(2)}, u32[]{:S(2)}) collective-permute-start(bf16[256,128]{1,0:T(8,128)(2,1)S(1)} %get-tuple-element.37), channel_id=1, source_target_pairs={{0,8},{8,0},{16,24},{24,16},{1,9},{9,1},{17,25},{25,17},{2,10},{10... | collective-permute-start | bytes 196616 | tf_op jit(solution)/shard_map/ppermute | solution.py:321
  24.0 3.6 %collective-permute-start.10 = (bf16[256,128]{1,0:T(8,128)(2,1)S(1)}, bf16[256,128]{1,0:T(8,128)(2,1)S(1)}, u32[]{:S(2)}, u32[]{:S(2)}) collective-permute-start(bf16[256,128]{1,0:T(8,128)(2,1)S(1)} %get-tuple-element.40), channel_id=1, source_target_pairs={{0,24},{8,16},{16,8},{24,0},{1,25},{9,17},{17,9},{25,1},{2,26},{10... | collective-permute-start | bytes 196616 | tf_op jit(solution)/shard_map/ppermute | solution.py:321
  27.6 0.8 %collective-permute-start.12 = (bf16[256,128]{1,0:T(8,128)(2,1)S(1)}, bf16[256,128]{1,0:T(8,128)(2,1)S(1)}, u32[]{:S(2)}, u32[]{:S(2)}) collective-permute-start(bf16[256,128]{1,0:T(8,128)(2,1)S(1)} %get-tuple-element.42), channel_id=1, source_target_pairs={{0,8},{8,0},{16,24},{24,16},{1,9},{9,1},{17,25},{25,17},{2,10},{10... | collective-permute-start | bytes 196616 | tf_op jit(solution)/shard_map/ppermute | solution.py:321
  28.4 1.7 %collective-permute-done.8.refs_2_ = bf16[256,128]{1,0:T(8,128)(2,1)S(1)} collective-permute-done((bf16[256,128]{1,0:T(8,128)(2,1)S(1)}, bf16[256,128]{1,0:T(8,128)(2,1)S(1)}, u32[]{:S(2)}, u32[]{:S(2)}) %collective-permute-start.8) | collective-permute-done | bytes 65568 | tf_op jit(solution)/shard_map/ppermute | solution.py:321
  30.1 1.7 %shard_map.116 = (bf16[256,128]{1,0:T(8,128)(2,1)S(1)}, bf16[256,128]{1,0:T(8,128)(2,1)S(1)}, bf16[256,128]{1,0:T(8,128)(2,1)S(1)}, bf16[256,128]{1,0:T(8,128)(2,1)S(1)}, f32[256,1024]{1,0:T(8,128)S(1)}) custom-call(bf16[256,128]{1,0:T(8,128)(2,1)S(1)} %get-tuple-element.34.refs_0_, bf16[256,128]{1,0:T(8,128)(2,1)S(1)} %collective-permute-done.7.refs_1_, ...), custom_call_target="tpu_custom_call" | custom-call | flops 1000000000 | bytes 1000000 | tf_op jit(solution)/shard_map/pallas_call | solution.py:298
  31.9 2.5 %collective-permute-start.13 = (bf16[256,128]{1,0:T(8,128)(2,1)S(1)}, bf16[256,128]{1,0:T(8,128)(2,1)S(1)}, u32[]{:S(2)}, u32[]{:S(2)}) collective-permute-start(bf16[256,128]{1,0:T(8,128)(2,1)S(1)} %get-tuple-element.45), channel_id=1, source_target_pairs={{0,24},{8,16},{16,8},{24,0},{1,25},{9,17},{17,9},{25,1},{2,26},{10... | collective-permute-start | bytes 196616 | tf_op jit(solution)/shard_map/ppermute | solution.py:321
  34.4 1.9 %collective-permute-start.15 = (bf16[256,128]{1,0:T(8,128)(2,1)S(1)}, bf16[256,128]{1,0:T(8,128)(2,1)S(1)}, u32[]{:S(2)}, u32[]{:S(2)}) collective-permute-start(bf16[256,128]{1,0:T(8,128)(2,1)S(1)} %get-tuple-element.47), channel_id=1, source_target_pairs={{0,8},{8,0},{16,24},{24,16},{1,9},{9,1},{17,25},{25,17},{2,10},{10... | collective-permute-start | bytes 196616 | tf_op jit(solution)/shard_map/ppermute | solution.py:321
  36.3 1.8 %shard_map.117 = (f32[128,512]{1,0:T(8,128)S(1)}, bf16[64,512]{1,0:T(8,128)(2,1)S(1)}, bf16[64,512]{1,0:T(8,128)(2,1)S(1)}, bf16[1024,128]{1,0:T(8,128)(2,1)}) custom-call(f32[256,1024]{1,0:T(8,128)S(1)} %get-tuple-element.32.spec_conv, f32[256,1024]{1,0:T(8,128)S(1)} %get-tuple-element.38.spec_gate, bf16[1024,512]{1,0:T(8,128)(2,1)S(1)} %copy-done.1, ...), custom_call_target="tpu_custom_call" | custom-call | flops 2000000000 | bytes 2000000 | tf_op jit(solution)/shard_map/pallas_call | solution.py:298
  38.1 0.5 %collective-permute-start.17 = (bf16[64,512]{1,0:T(8,128)(2,1)S(1)}, bf16[64,512]{1,0:T(8,128)(2,1)S(1)}, u32[]{:S(2)}, u32[]{:S(2)}) collective-permute-start(bf16[64,512]{1,0:T(8,128)(2,1)S(1)} %get-tuple-element.49), channel_id=1, source_target_pairs={{0,1},{1,0},{2,3},{3,2},{4,5},{5,4},{6,7},{7,6},{8,9},{9,8},{10,11... | collective-permute-start | bytes 196616 | tf_op jit(solution)/shard_map/ppermute | solution.py:321
  38.6 0.9 %collective-permute-done.14.refs_2_ = bf16[256,128]{1,0:T(8,128)(2,1)S(1)} collective-permute-done((bf16[256,128]{1,0:T(8,128)(2,1)S(1)}, bf16[256,128]{1,0:T(8,128)(2,1)S(1)}, u32[]{:S(2)}, u32[]{:S(2)}) %collective-permute-start.14) | collective-permute-done | bytes 65568 | tf_op jit(solution)/shard_map/ppermute | solution.py:321
  39.6 0.8 %shard_map.118 = (f32[128,512]{1,0:T(8,128)}, bf16[1024,128]{1,0:T(8,128)(2,1)}) custom-call(bf16[256,128]{1,0:T(8,128)(2,1)S(1)} %get-tuple-element.44.refs_0_, bf16[256,128]{1,0:T(8,128)(2,1)S(1)} %collective-permute-done.13.refs_1_, bf16[256,128]{1,0:T(8,128)(2,1)S(1)} %collective-permute-done.14.refs_2_, ...), custom_call_target="tpu_custom_call" | custom-call | flops 1000000000 | bytes 1000000 | tf_op jit(solution)/shard_map/pallas_call | solution.py:298
  (40 shorter events, 0.1 us)
Async XLA Ops:
  0.6 10.2 %collective-permute-start.4 = (bf16[32,4096]{1,0:T(8,128)(2,1)}, bf16[32,4096]{1,0:T(8,128)(2,1)S(1)}, u32[]{:S(2)}, u32[]{:S(2)}) collective-permute-start(bf16[32,4096]{1,0:T(8,128)(2,1)} %bitcast.7), channel_id=1, source_target_pairs={{0,4},{2,6},{4,0},{6,2},{1,5},{3,7},{5,1},{7,3},{8,12},{10,14},{12... | collective-permute-start | bytes 786440 | tf_op jit(solution)/shard_map/ppermute | solution.py:321
  3.7 8.3 %collective-permute-start.3 = (bf16[32,4096]{1,0:T(8,128)(2,1)}, bf16[32,4096]{1,0:T(8,128)(2,1)S(1)}, u32[]{:S(2)}, u32[]{:S(2)}) collective-permute-start(bf16[32,4096]{1,0:T(8,128)(2,1)} %bitcast.8), channel_id=1, source_target_pairs={{0,2},{2,0},{4,6},{6,4},{1,3},{3,1},{5,7},{7,5},{8,10},{10,8},{12,... | collective-permute-start | bytes 786440 | tf_op jit(solution)/shard_map/ppermute | solution.py:321
  5.2 8.4 %copy-start.6 = (f32[256,512]{1,0:T(8,128)S(1)}, f32[256,512]{1,0:T(8,128)}, u32[]{:S(2)}) copy-start(f32[256,512]{1,0:T(8,128)} %filt.1) | copy-start | bytes 1572868
  5.2 10.1 %copy-start = (bf16[1024,512]{1,0:T(8,128)(2,1)S(1)}, bf16[1024,512]{1,0:T(8,128)(2,1)}, u32[]{:S(2)}) copy-start(bf16[1024,512]{1,0:T(8,128)(2,1)} %constant.11.clone.refs_8_.inv_lo) | copy-start | bytes 3145732
  5.2 10.1 %copy-start.1 = (bf16[1024,512]{1,0:T(8,128)(2,1)S(1)}, bf16[1024,512]{1,0:T(8,128)(2,1)}, u32[]{:S(2)}) copy-start(bf16[1024,512]{1,0:T(8,128)(2,1)} %constant.10.clone.refs_7_.inv_hi) | copy-start | bytes 3145732
  6.3 10.7 %slice-start = ((s8[8388608]{0:T(1024)(128)(4,1)}), s8[4194304]{0:T(1024)(128)(4,1)S(1)}, s32[]{:S(2)}) async-start(s8[8388608]{0:T(1024)(128)(4,1)} %bitcast.5), calls=%async_computation | async-start | bytes 8388608
  6.3 10.7 %copy-start.4 = (bf16[1,32,4096]{2,1,0:T(8,128)(2,1)S(1)}, bf16[1,32,4096]{2,1,0:T(8,128)(2,1)}, u32[]{:S(2)}) copy-start(bf16[1,32,4096]{2,1,0:T(8,128)(2,1)} %param.9) | copy-start | bytes 786436
  6.3 10.7 %copy-start.5 = (bf16[1,1024,128]{2,1,0:T(8,128)(2,1)S(1)}, bf16[1,1024,128]{2,1,0:T(8,128)(2,1)}, u32[]{:S(2)}) copy-start(bf16[1,1024,128]{2,1,0:T(8,128)(2,1)} %param.10) | copy-start | bytes 786436
  6.4 8.2 %collective-permute-start = (bf16[256,128]{1,0:T(8,128)(2,1)S(1)}, bf16[256,128]{1,0:T(8,128)(2,1)S(1)}, u32[]{:S(2)}, u32[]{:S(2)}) collective-permute-start(bf16[256,128]{1,0:T(8,128)(2,1)S(1)} %get-tuple-element.29), channel_id=1, source_target_pairs={{0,24},{8,16},{16,8},{24,0},{1,25},{9,17},{17,9},{25,1},{2,26},{10... | collective-permute-start | bytes 196616 | tf_op jit(solution)/shard_map/ppermute | solution.py:321
  10.0 5.2 %collective-permute-start.1 = (bf16[256,128]{1,0:T(8,128)(2,1)S(1)}, bf16[256,128]{1,0:T(8,128)(2,1)S(1)}, u32[]{:S(2)}, u32[]{:S(2)}) collective-permute-start(bf16[256,128]{1,0:T(8,128)(2,1)S(1)} %get-tuple-element.30), channel_id=1, source_target_pairs={{0,16},{8,24},{16,0},{24,8},{1,17},{9,25},{17,1},{25,9},{2,18},{10... | collective-permute-start | bytes 196616 | tf_op jit(solution)/shard_map/ppermute | solution.py:321
  10.0 5.2 %collective-permute-start.2 = (bf16[256,128]{1,0:T(8,128)(2,1)S(1)}, bf16[256,128]{1,0:T(8,128)(2,1)S(1)}, u32[]{:S(2)}, u32[]{:S(2)}) collective-permute-start(bf16[256,128]{1,0:T(8,128)(2,1)S(1)} %get-tuple-element.31), channel_id=1, source_target_pairs={{0,8},{8,0},{16,24},{24,16},{1,9},{9,1},{17,25},{25,17},{2,10},{10... | collective-permute-start | bytes 196616 | tf_op jit(solution)/shard_map/ppermute | solution.py:321
  10.8 6.2 %collective-permute-start.6 = (bf16[32,2048]{1,0:T(8,128)(2,1)S(1)}, bf16[32,2048]{1,0:T(8,128)(2,1)S(1)}, u32[]{:S(2)}, u32[]{:S(2)}) collective-permute-start(bf16[32,2048]{1,0:T(8,128)(2,1)S(1)} %slice.9), channel_id=1, source_target_pairs={{0,2},{2,0},{4,6},{6,4},{1,3},{3,1},{5,7},{7,5},{8,10},{10,8},{12,... | collective-permute-start | bytes 393224 | tf_op jit(solution)/shard_map/ppermute | solution.py:321
  12.0 5.0 %collective-permute-start.5 = (bf16[32,2048]{1,0:T(8,128)(2,1)S(1)}, bf16[32,2048]{1,0:T(8,128)(2,1)S(1)}, u32[]{:S(2)}, u32[]{:S(2)}) collective-permute-start(bf16[32,2048]{1,0:T(8,128)(2,1)S(1)} %slice.8), channel_id=1, source_target_pairs={{0,4},{2,6},{4,0},{6,2},{1,5},{3,7},{5,1},{7,3},{8,12},{10,14},{12... | collective-permute-start | bytes 393224 | tf_op jit(solution)/shard_map/ppermute | solution.py:321
  19.6 8.0 %collective-permute-start.7 = (bf16[256,128]{1,0:T(8,128)(2,1)S(1)}, bf16[256,128]{1,0:T(8,128)(2,1)S(1)}, u32[]{:S(2)}, u32[]{:S(2)}) collective-permute-start(bf16[256,128]{1,0:T(8,128)(2,1)S(1)} %get-tuple-element.35), channel_id=1, source_target_pairs={{0,24},{8,16},{16,8},{24,0},{1,25},{9,17},{17,9},{25,1},{2,26},{10... | collective-permute-start | bytes 196616 | tf_op jit(solution)/shard_map/ppermute | solution.py:321
  23.2 6.9 %collective-permute-start.8 = (bf16[256,128]{1,0:T(8,128)(2,1)S(1)}, bf16[256,128]{1,0:T(8,128)(2,1)S(1)}, u32[]{:S(2)}, u32[]{:S(2)}) collective-permute-start(bf16[256,128]{1,0:T(8,128)(2,1)S(1)} %get-tuple-element.36), channel_id=1, source_target_pairs={{0,16},{8,24},{16,0},{24,8},{1,17},{9,25},{17,1},{25,9},{2,18},{10... | collective-permute-start | bytes 196616 | tf_op jit(solution)/shard_map/ppermute | solution.py:321
  23.2 6.9 %collective-permute-start.9 = (bf16[256,128]{1,0:T(8,128)(2,1)S(1)}, bf16[256,128]{1,0:T(8,128)(2,1)S(1)}, u32[]{:S(2)}, u32[]{:S(2)}) collective-permute-start(bf16[256,128]{1,0:T(8,128)(2,1)S(1)} %get-tuple-element.37), channel_id=1, source_target_pairs={{0,8},{8,0},{16,24},{24,16},{1,9},{9,1},{17,25},{25,17},{2,10},{10... | collective-permute-start | bytes 196616 | tf_op jit(solution)/shard_map/ppermute | solution.py:321
  24.0 10.3 %collective-permute-start.10 = (bf16[256,128]{1,0:T(8,128)(2,1)S(1)}, bf16[256,128]{1,0:T(8,128)(2,1)S(1)}, u32[]{:S(2)}, u32[]{:S(2)}) collective-permute-start(bf16[256,128]{1,0:T(8,128)(2,1)S(1)} %get-tuple-element.40), channel_id=1, source_target_pairs={{0,24},{8,16},{16,8},{24,0},{1,25},{9,17},{17,9},{25,1},{2,26},{10... | collective-permute-start | bytes 196616 | tf_op jit(solution)/shard_map/ppermute | solution.py:321
  27.6 8.7 %collective-permute-start.11 = (bf16[256,128]{1,0:T(8,128)(2,1)S(1)}, bf16[256,128]{1,0:T(8,128)(2,1)S(1)}, u32[]{:S(2)}, u32[]{:S(2)}) collective-permute-start(bf16[256,128]{1,0:T(8,128)(2,1)S(1)} %get-tuple-element.41), channel_id=1, source_target_pairs={{0,16},{8,24},{16,0},{24,8},{1,17},{9,25},{17,1},{25,9},{2,18},{10... | collective-permute-start | bytes 196616 | tf_op jit(solution)/shard_map/ppermute | solution.py:321
  27.6 8.7 %collective-permute-start.12 = (bf16[256,128]{1,0:T(8,128)(2,1)S(1)}, bf16[256,128]{1,0:T(8,128)(2,1)S(1)}, u32[]{:S(2)}, u32[]{:S(2)}) collective-permute-start(bf16[256,128]{1,0:T(8,128)(2,1)S(1)} %get-tuple-element.42), channel_id=1, source_target_pairs={{0,8},{8,0},{16,24},{24,16},{1,9},{9,1},{17,25},{25,17},{2,10},{10... | collective-permute-start | bytes 196616 | tf_op jit(solution)/shard_map/ppermute | solution.py:321
  31.9 6.7 %collective-permute-start.13 = (bf16[256,128]{1,0:T(8,128)(2,1)S(1)}, bf16[256,128]{1,0:T(8,128)(2,1)S(1)}, u32[]{:S(2)}, u32[]{:S(2)}) collective-permute-start(bf16[256,128]{1,0:T(8,128)(2,1)S(1)} %get-tuple-element.45), channel_id=1, source_target_pairs={{0,24},{8,16},{16,8},{24,0},{1,25},{9,17},{17,9},{25,1},{2,26},{10... | collective-permute-start | bytes 196616 | tf_op jit(solution)/shard_map/ppermute | solution.py:321
  34.4 5.2 %collective-permute-start.14 = (bf16[256,128]{1,0:T(8,128)(2,1)S(1)}, bf16[256,128]{1,0:T(8,128)(2,1)S(1)}, u32[]{:S(2)}, u32[]{:S(2)}) collective-permute-start(bf16[256,128]{1,0:T(8,128)(2,1)S(1)} %get-tuple-element.46), channel_id=1, source_target_pairs={{0,16},{8,24},{16,0},{24,8},{1,17},{9,25},{17,1},{25,9},{2,18},{10... | collective-permute-start | bytes 196616 | tf_op jit(solution)/shard_map/ppermute | solution.py:321
  34.4 5.2 %collective-permute-start.15 = (bf16[256,128]{1,0:T(8,128)(2,1)S(1)}, bf16[256,128]{1,0:T(8,128)(2,1)S(1)}, u32[]{:S(2)}, u32[]{:S(2)}) collective-permute-start(bf16[256,128]{1,0:T(8,128)(2,1)S(1)} %get-tuple-element.47), channel_id=1, source_target_pairs={{0,8},{8,0},{16,24},{24,16},{1,9},{9,1},{17,25},{25,17},{2,10},{10... | collective-permute-start | bytes 196616 | tf_op jit(solution)/shard_map/ppermute | solution.py:321
  38.1 1.5 %collective-permute-start.16 = (bf16[64,512]{1,0:T(8,128)(2,1)S(1)}, bf16[64,512]{1,0:T(8,128)(2,1)S(1)}, u32[]{:S(2)}, u32[]{:S(2)}) collective-permute-start(bf16[64,512]{1,0:T(8,128)(2,1)S(1)} %get-tuple-element.48), channel_id=1, source_target_pairs={{0,1},{1,0},{2,3},{3,2},{4,5},{5,4},{6,7},{7,6},{8,9},{9,8},{10,11... | collective-permute-start | bytes 196616 | tf_op jit(solution)/shard_map/ppermute | solution.py:321
  38.1 1.5 %collective-permute-start.17 = (bf16[64,512]{1,0:T(8,128)(2,1)S(1)}, bf16[64,512]{1,0:T(8,128)(2,1)S(1)}, u32[]{:S(2)}, u32[]{:S(2)}) collective-permute-start(bf16[64,512]{1,0:T(8,128)(2,1)S(1)} %get-tuple-element.49), channel_id=1, source_target_pairs={{0,1},{1,0},{2,3},{3,2},{4,5},{5,4},{6,7},{7,6},{8,9},{9,8},{10,11... | collective-permute-start | bytes 196616 | tf_op jit(solution)/shard_map/ppermute | solution.py:321
  (3 other events, 22.0 us)

commit v2 on v1

--- a/solution.py
+++ b/solution.py
@@ -173,6 +173,10 @@
     return [0, *reversed(range(1, parts))]
 
 
+def back_offsets(parts):
+    return [0, parts - 1, *range(1, parts - 1)]
+
+
 def gather_tokens(pieces, whole, here):
     step = pieces[0].shape[1]
     for k, piece in zip(offsets(len(pieces)), pieces):
@@ -223,7 +227,7 @@
     spec_conv[...] = spectrum_of(whole[...], fwd_hi, fwd_lo)
     product = spectrum_product(spec_filt[...], spec_conv[...], False)
     whole[...] = inverse_dense(product, inv_hi, inv_lo).astype(jnp.bfloat16)
-    scatter_tokens(whole, out, here, offsets(parts))
+    scatter_tokens(whole, out, here, back_offsets(parts))
 
 
 def unit_kernel(parts, pieces, after, weight, gate, *refs):
@@ -233,16 +237,17 @@
     rows_all = refs[pieces + 1 + parts]
     here, block = lax.axis_index("ctx"), lax.axis_index("tp")
     rows = grads[0].shape[0]
-    half = rows_all.shape[1] // 2
+    cut = grads[3].shape[1]
     for k, ref in enumerate(grads[:3]):
         rows_all[place(block ^ k, rows), :] = ref[...]
-    rows_all[place(block ^ 3, rows), :half] = grads[3][...]
-    rows_all[place(block ^ 3, rows), half:] = grads[4][...]
+    rows_all[place(block ^ 3, rows), :cut] = grads[3][...]
+    rows_all[place(block ^ 3, rows), cut:] = grads[4][...]
     rows = out[0].shape[0]
-    unit[...] = mm_nt(weight[...], rows_all[...])
     for k, ref in zip(offsets(parts), out):
         at = place(here ^ k, rows)
-        ref[...] = (unit[at, :] * gate[at, :].astype(jnp.float32)).astype(jnp.bfloat16)
+        got = mm_nt(weight[at, :], rows_all[...])
+        unit[at, :] = got
+        ref[...] = (got * gate[at, :].astype(jnp.float32)).astype(jnp.bfloat16)
 
 
 def grad_kernel(parts, *refs):
@@ -263,7 +268,7 @@
     keep, *send, out, whole = refs[parts:]
     here = lax.axis_index("ctx")
     rows = back[0].shape[0]
-    for k, ref in zip(offsets(parts), back):
+    for k, ref in zip(back_offsets(parts), back):
         at = place(here ^ k, rows)
         out[at, :] = (unit[at, :] * ref[...].astype(jnp.float32)).astype(jnp.bfloat16)
     product = spectrum_product(spec_conv[...], spec_gate[...], True)
@@ -334,8 +339,9 @@
         cost=10.0,
     )
     conv_pieces = exchange(blocks, offsets(parts))
-    grad_3a = swap(grad_1[:, : width // 2], "tp", groups, 2)
-    grad_3b = swap(grad_2[:, width // 2 :], "tp", groups, 1)
+    cut = width * 3 // 8
+    grad_3a = swap(grad_1[:, :cut], "tp", groups, 2)
+    grad_3b = swap(grad_2[:, cut:], "tp", groups, 1)
 
     piece = shape((chans, tokens), bf16)
     spectrum = shape((chans, 2 * length), f32)
@@ -353,7 +359,7 @@
         [whole],
         cost=2.0,
     )
-    conv_back = exchange(conv_out, offsets(parts))
+    conv_back = exchange(conv_out, back_offsets(parts))
 
     unit, *gate_pieces = call(
         functools.partial(unit_kernel, parts, 5),

time: 40.5 us -> 40 us (0.988)
  waiting for transfers between devices: 3.34 us -> 2.89 us
    ppermute x18, waiting for transfers between devices: 3.34 us -> 2.89 us  [swap(): return lax.ppermute(value, axis, [(i, i ^ k) for i in range(size)])]
where the time goes in v2:
time: 40 us; the launch traced here: 39.9 us
  starting transfers between devices  25.5 us (64%)
  Pallas kernels  10.6 us (26%)
  waiting for transfers between devices  2.89 us (7%)
  between operations  0.81 us (2%)
    ppermute x18, starting transfers between devices, swap(): return lax.ppermute(value, axis, [(i, i ^ k) for i in range(size)])  25.5 us
    pallas_call x7, Pallas kernels, call(): pl.pallas_call(kernel, out_shape=outs, in_specs=[hbm if i in far else vme...  10.6 us
    ppermute x18, waiting for transfers between devices, swap(): return lax.ppermute(value, axis, [(i, i ^ k) for i in range(size)])  2.89 us
  transfers between devices with their start and end apart: 18, of which 3 were waited for; matrix products, arithmetic and copies ran while one was open for 0% of the time, Pallas kernels for 18%

profile of v2, /device:TPU:0, one launch (start us, length us, event | category | flops | bytes accessed | tf_op | source)
XLA Modules:
  0.0 39.9 jit_solution(543724536350986369)
XLA Ops:
  0.6 3.0 %collective-permute-start.4 = (bf16[32,4096]{1,0:T(8,128)(2,1)}, bf16[32,4096]{1,0:T(8,128)(2,1)S(1)}, u32[]{:S(2)}, u32[]{:S(2)}) collective-permute-start(bf16[32,4096]{1,0:T(8,128)(2,1)} %bitcast.7), channel_id=1, source_target_pairs={{0,4},{2,6},{4,0},{6,2},{1,5},{3,7},{5,1},{7,3},{8,12},{10,14},{12... | collective-permute-start | bytes 786440 | tf_op jit(solution)/shard_map/ppermute | solution.py:326
  3.7 1.5 %collective-permute-start.3 = (bf16[32,4096]{1,0:T(8,128)(2,1)}, bf16[32,4096]{1,0:T(8,128)(2,1)S(1)}, u32[]{:S(2)}, u32[]{:S(2)}) collective-permute-start(bf16[32,4096]{1,0:T(8,128)(2,1)} %bitcast.8), channel_id=1, source_target_pairs={{0,2},{2,0},{4,6},{6,4},{1,3},{3,1},{5,7},{7,5},{8,10},{10,8},{12,... | collective-permute-start | bytes 786440 | tf_op jit(solution)/shard_map/ppermute | solution.py:326
  5.2 1.1 %shard_map.112 = (bf16[256,128]{1,0:T(8,128)(2,1)S(1)}, bf16[256,128]{1,0:T(8,128)(2,1)S(1)}, bf16[256,128]{1,0:T(8,128)(2,1)S(1)}, bf16[256,128]{1,0:T(8,128)(2,1)S(1)}) custom-call(bf16[1024,128]{1,0:T(8,128)(2,1)} %bitcast.11), custom_call_target="tpu_custom_call" | custom-call | flops 10000000000 | bytes 10000000 | tf_op jit(solution)/shard_map/pallas_call | solution.py:303
  6.4 3.7 %collective-permute-start = (bf16[256,128]{1,0:T(8,128)(2,1)S(1)}, bf16[256,128]{1,0:T(8,128)(2,1)S(1)}, u32[]{:S(2)}, u32[]{:S(2)}) collective-permute-start(bf16[256,128]{1,0:T(8,128)(2,1)S(1)} %get-tuple-element.29), channel_id=1, source_target_pairs={{0,24},{8,16},{16,8},{24,0},{1,25},{9,17},{17,9},{25,1},{2,26},{10... | collective-permute-start | bytes 196616 | tf_op jit(solution)/shard_map/ppermute | solution.py:326
  10.0 0.8 %collective-permute-start.2 = (bf16[256,128]{1,0:T(8,128)(2,1)S(1)}, bf16[256,128]{1,0:T(8,128)(2,1)S(1)}, u32[]{:S(2)}, u32[]{:S(2)}) collective-permute-start(bf16[256,128]{1,0:T(8,128)(2,1)S(1)} %get-tuple-element.31), channel_id=1, source_target_pairs={{0,8},{8,0},{16,24},{24,16},{1,9},{9,1},{17,25},{25,17},{2,10},{10... | collective-permute-start | bytes 196616 | tf_op jit(solution)/shard_map/ppermute | solution.py:326
  10.8 1.1 %collective-permute-start.6 = (bf16[32,2560]{1,0:T(8,128)(2,1)S(1)}, bf16[32,2560]{1,0:T(8,128)(2,1)S(1)}, u32[]{:S(2)}, u32[]{:S(2)}) collective-permute-start(bf16[32,2560]{1,0:T(8,128)(2,1)S(1)} %slice.9), channel_id=1, source_target_pairs={{0,2},{2,0},{4,6},{6,4},{1,3},{3,1},{5,7},{7,5},{8,10},{10,8},{12,... | collective-permute-start | bytes 491528 | tf_op jit(solution)/shard_map/ppermute | solution.py:326
  12.0 0.0 slice-start.1
  12.0 1.6 %collective-permute-start.5 = (bf16[32,1536]{1,0:T(8,128)(2,1)S(1)}, bf16[32,1536]{1,0:T(8,128)(2,1)S(1)}, u32[]{:S(2)}, u32[]{:S(2)}) collective-permute-start(bf16[32,1536]{1,0:T(8,128)(2,1)S(1)} %slice.8), channel_id=1, source_target_pairs={{0,4},{2,6},{4,0},{6,2},{1,5},{3,7},{5,1},{7,3},{8,12},{10,14},{12... | collective-permute-start | bytes 294920 | tf_op jit(solution)/shard_map/ppermute | solution.py:326
  13.6 1.0 %shard_map.113.refs_4_ = f32[256,1024]{1,0:T(8,128)S(1)} custom-call(f32[256,512]{1,0:T(8,128)S(1)} %copy-done.6, bf16[512,1024]{1,0:T(8,128)(2,1)S(1)} %copy-done.3, bf16[512,1024]{1,0:T(8,128)(2,1)S(1)} %copy-done.2, bf16[32,4096]{1,0:T(8,128)(2,1)S(1)} %collective-permute-done.3.after_1.refs_1_, bf16[32,4096]{1,0:T(8,128)(2,1)S(1)} %collective-permute-done.4.after_2.refs_2_), custom_call_target="tpu_custom_call" | custom-call | flops 2000000000 | bytes 2000000 | tf_op jit(solution)/shard_map/pallas_call | solution.py:303
  14.6 0.7 %collective-permute-done.1.refs_2_ = bf16[256,128]{1,0:T(8,128)(2,1)S(1)} collective-permute-done((bf16[256,128]{1,0:T(8,128)(2,1)S(1)}, bf16[256,128]{1,0:T(8,128)(2,1)S(1)}, u32[]{:S(2)}, u32[]{:S(2)}) %collective-permute-start.1) | collective-permute-done | bytes 65568 | tf_op jit(solution)/shard_map/ppermute | solution.py:326
  15.3 1.7 %shard_map.114 = (bf16[256,128]{1,0:T(8,128)(2,1)S(1)}, bf16[256,128]{1,0:T(8,128)(2,1)S(1)}, bf16[256,128]{1,0:T(8,128)(2,1)S(1)}, bf16[256,128]{1,0:T(8,128)(2,1)S(1)}, f32[256,1024]{1,0:T(8,128)S(1)}) custom-call(bf16[256,128]{1,0:T(8,128)(2,1)S(1)} %get-tuple-element.28.refs_0_, bf16[256,128]{1,0:T(8,128)(2,1)S(1)} %collective-permute-done.refs_1_, ...), custom_call_target="tpu_custom_call" | custom-call | flops 2000000000 | bytes 2000000 | tf_op jit(solution)/shard_map/pallas_call | solution.py:303
  17.1 2.4 %shard_map.115 = (f32[1024,128]{1,0:T(8,128)S(1)}, bf16[256,128]{1,0:T(8,128)(2,1)S(1)}, bf16[256,128]{1,0:T(8,128)(2,1)S(1)}, bf16[256,128]{1,0:T(8,128)(2,1)S(1)}, bf16[256,128]{1,0:T(8,128)(2,1)S(1)}) custom-call(bf16[256,128]{1,0:T(8,128)(2,1)S(1)} %get-tuple-element.33.after.refs_0_, bf16[1024,4096]{1,0:T(8,128)(2,1)S(1)} %bitcast.6, ...), custom_call_target="tpu_custom_call" | custom-call | flops 1000000000 | bytes 1000000 | tf_op jit(solution)/shard_map/pallas_call | solution.py:303
  19.5 3.3 %collective-permute-start.7 = (bf16[256,128]{1,0:T(8,128)(2,1)S(1)}, bf16[256,128]{1,0:T(8,128)(2,1)S(1)}, u32[]{:S(2)}, u32[]{:S(2)}) collective-permute-start(bf16[256,128]{1,0:T(8,128)(2,1)S(1)} %get-tuple-element.35), channel_id=1, source_target_pairs={{0,24},{8,16},{16,8},{24,0},{1,25},{9,17},{17,9},{25,1},{2,26},{10... | collective-permute-start | bytes 196616 | tf_op jit(solution)/shard_map/ppermute | solution.py:326
  22.8 1.2 %collective-permute-start.9 = (bf16[256,128]{1,0:T(8,128)(2,1)S(1)}, bf16[256,128]{1,0:T(8,128)(2,1)S(1)}, u32[]{:S(2)}, u32[]{:S(2)}) collective-permute-start(bf16[256,128]{1,0:T(8,128)(2,1)S(1)} %get-tuple-element.37), channel_id=1, source_target_pairs={{0,8},{8,0},{16,24},{24,16},{1,9},{9,1},{17,25},{25,17},{2,10},{10... | collective-permute-start | bytes 196616 | tf_op jit(solution)/shard_map/ppermute | solution.py:326
  24.0 3.2 %collective-permute-start.10 = (bf16[256,128]{1,0:T(8,128)(2,1)S(1)}, bf16[256,128]{1,0:T(8,128)(2,1)S(1)}, u32[]{:S(2)}, u32[]{:S(2)}) collective-permute-start(bf16[256,128]{1,0:T(8,128)(2,1)S(1)} %get-tuple-element.40), channel_id=1, source_target_pairs={{0,24},{8,16},{16,8},{24,0},{1,25},{9,17},{17,9},{25,1},{2,26},{10... | collective-permute-start | bytes 196616 | tf_op jit(solution)/shard_map/ppermute | solution.py:326
  27.2 1.2 %collective-permute-start.12 = (bf16[256,128]{1,0:T(8,128)(2,1)S(1)}, bf16[256,128]{1,0:T(8,128)(2,1)S(1)}, u32[]{:S(2)}, u32[]{:S(2)}) collective-permute-start(bf16[256,128]{1,0:T(8,128)(2,1)S(1)} %get-tuple-element.42), channel_id=1, source_target_pairs={{0,16},{8,24},{16,0},{24,8},{1,17},{9,25},{17,1},{25,9},{2,18},{10... | collective-permute-start | bytes 196616 | tf_op jit(solution)/shard_map/ppermute | solution.py:326
  28.4 1.1 %collective-permute-done.8.refs_2_ = bf16[256,128]{1,0:T(8,128)(2,1)S(1)} collective-permute-done((bf16[256,128]{1,0:T(8,128)(2,1)S(1)}, bf16[256,128]{1,0:T(8,128)(2,1)S(1)}, u32[]{:S(2)}, u32[]{:S(2)}) %collective-permute-start.8) | collective-permute-done | bytes 65568 | tf_op jit(solution)/shard_map/ppermute | solution.py:326
  29.4 1.7 %shard_map.116 = (bf16[256,128]{1,0:T(8,128)(2,1)S(1)}, bf16[256,128]{1,0:T(8,128)(2,1)S(1)}, bf16[256,128]{1,0:T(8,128)(2,1)S(1)}, bf16[256,128]{1,0:T(8,128)(2,1)S(1)}, f32[256,1024]{1,0:T(8,128)S(1)}) custom-call(bf16[256,128]{1,0:T(8,128)(2,1)S(1)} %get-tuple-element.34.refs_0_, bf16[256,128]{1,0:T(8,128)(2,1)S(1)} %collective-permute-done.7.refs_1_, ...), custom_call_target="tpu_custom_call" | custom-call | flops 1000000000 | bytes 1000000 | tf_op jit(solution)/shard_map/pallas_call | solution.py:303
  31.2 2.4 %collective-permute-start.13 = (bf16[256,128]{1,0:T(8,128)(2,1)S(1)}, bf16[256,128]{1,0:T(8,128)(2,1)S(1)}, u32[]{:S(2)}, u32[]{:S(2)}) collective-permute-start(bf16[256,128]{1,0:T(8,128)(2,1)S(1)} %get-tuple-element.45), channel_id=1, source_target_pairs={{0,24},{8,16},{16,8},{24,0},{1,25},{9,17},{17,9},{25,1},{2,26},{10... | collective-permute-start | bytes 196616 | tf_op jit(solution)/shard_map/ppermute | solution.py:326
  33.6 2.1 %collective-permute-start.15 = (bf16[256,128]{1,0:T(8,128)(2,1)S(1)}, bf16[256,128]{1,0:T(8,128)(2,1)S(1)}, u32[]{:S(2)}, u32[]{:S(2)}) collective-permute-start(bf16[256,128]{1,0:T(8,128)(2,1)S(1)} %get-tuple-element.47), channel_id=1, source_target_pairs={{0,8},{8,0},{16,24},{24,16},{1,9},{9,1},{17,25},{25,17},{2,10},{10... | collective-permute-start | bytes 196616 | tf_op jit(solution)/shard_map/ppermute | solution.py:326
  35.6 1.8 %shard_map.117 = (f32[128,512]{1,0:T(8,128)S(1)}, bf16[64,512]{1,0:T(8,128)(2,1)S(1)}, bf16[64,512]{1,0:T(8,128)(2,1)S(1)}, bf16[1024,128]{1,0:T(8,128)(2,1)}) custom-call(f32[256,1024]{1,0:T(8,128)S(1)} %get-tuple-element.32.spec_conv, f32[256,1024]{1,0:T(8,128)S(1)} %get-tuple-element.38.spec_gate, bf16[1024,512]{1,0:T(8,128)(2,1)S(1)} %copy-done.1, ...), custom_call_target="tpu_custom_call" | custom-call | flops 2000000000 | bytes 2000000 | tf_op jit(solution)/shard_map/pallas_call | solution.py:303
  37.4 0.5 %collective-permute-start.17 = (bf16[64,512]{1,0:T(8,128)(2,1)S(1)}, bf16[64,512]{1,0:T(8,128)(2,1)S(1)}, u32[]{:S(2)}, u32[]{:S(2)}) collective-permute-start(bf16[64,512]{1,0:T(8,128)(2,1)S(1)} %get-tuple-element.49), channel_id=1, source_target_pairs={{0,1},{1,0},{2,3},{3,2},{4,5},{5,4},{6,7},{7,6},{8,9},{9,8},{10,11... | collective-permute-start | bytes 196616 | tf_op jit(solution)/shard_map/ppermute | solution.py:326
  37.9 1.1 %collective-permute-done.14.refs_2_ = bf16[256,128]{1,0:T(8,128)(2,1)S(1)} collective-permute-done((bf16[256,128]{1,0:T(8,128)(2,1)S(1)}, bf16[256,128]{1,0:T(8,128)(2,1)S(1)}, u32[]{:S(2)}, u32[]{:S(2)}) %collective-permute-start.14) | collective-permute-done | bytes 65568 | tf_op jit(solution)/shard_map/ppermute | solution.py:326
  39.0 0.8 %shard_map.118 = (f32[128,512]{1,0:T(8,128)}, bf16[1024,128]{1,0:T(8,128)(2,1)}) custom-call(bf16[256,128]{1,0:T(8,128)(2,1)S(1)} %get-tuple-element.44.refs_0_, bf16[256,128]{1,0:T(8,128)(2,1)S(1)} %collective-permute-done.13.refs_1_, bf16[256,128]{1,0:T(8,128)(2,1)S(1)} %collective-permute-done.14.refs_2_, ...), custom_call_target="tpu_custom_call" | custom-call | flops 1000000000 | bytes 1000000 | tf_op jit(solution)/shard_map/pallas_call | solution.py:303
  (40 shorter events, 0.1 us)
Async XLA Ops:
  0.6 10.2 %collective-permute-start.4 = (bf16[32,4096]{1,0:T(8,128)(2,1)}, bf16[32,4096]{1,0:T(8,128)(2,1)S(1)}, u32[]{:S(2)}, u32[]{:S(2)}) collective-permute-start(bf16[32,4096]{1,0:T(8,128)(2,1)} %bitcast.7), channel_id=1, source_target_pairs={{0,4},{2,6},{4,0},{6,2},{1,5},{3,7},{5,1},{7,3},{8,12},{10,14},{12... | collective-permute-start | bytes 786440 | tf_op jit(solution)/shard_map/ppermute | solution.py:326
  3.7 8.3 %collective-permute-start.3 = (bf16[32,4096]{1,0:T(8,128)(2,1)}, bf16[32,4096]{1,0:T(8,128)(2,1)S(1)}, u32[]{:S(2)}, u32[]{:S(2)}) collective-permute-start(bf16[32,4096]{1,0:T(8,128)(2,1)} %bitcast.8), channel_id=1, source_target_pairs={{0,2},{2,0},{4,6},{6,4},{1,3},{3,1},{5,7},{7,5},{8,10},{10,8},{12,... | collective-permute-start | bytes 786440 | tf_op jit(solution)/shard_map/ppermute | solution.py:326
  5.2 8.4 %copy-start.6 = (f32[256,512]{1,0:T(8,128)S(1)}, f32[256,512]{1,0:T(8,128)}, u32[]{:S(2)}) copy-start(f32[256,512]{1,0:T(8,128)} %filt.1) | copy-start | bytes 1572868
  5.2 10.1 %copy-start = (bf16[1024,512]{1,0:T(8,128)(2,1)S(1)}, bf16[1024,512]{1,0:T(8,128)(2,1)}, u32[]{:S(2)}) copy-start(bf16[1024,512]{1,0:T(8,128)(2,1)} %constant.11.clone.refs_8_.inv_lo) | copy-start | bytes 3145732
  5.2 10.1 %copy-start.1 = (bf16[1024,512]{1,0:T(8,128)(2,1)S(1)}, bf16[1024,512]{1,0:T(8,128)(2,1)}, u32[]{:S(2)}) copy-start(bf16[1024,512]{1,0:T(8,128)(2,1)} %constant.10.clone.refs_7_.inv_hi) | copy-start | bytes 3145732
  6.3 10.7 %slice-start = ((s8[8388608]{0:T(1024)(128)(4,1)}), s8[4194304]{0:T(1024)(128)(4,1)S(1)}, s32[]{:S(2)}) async-start(s8[8388608]{0:T(1024)(128)(4,1)} %bitcast.5), calls=%async_computation | async-start | bytes 8388608
  6.3 10.7 %copy-start.4 = (bf16[1,32,4096]{2,1,0:T(8,128)(2,1)S(1)}, bf16[1,32,4096]{2,1,0:T(8,128)(2,1)}, u32[]{:S(2)}) copy-start(bf16[1,32,4096]{2,1,0:T(8,128)(2,1)} %param.9) | copy-start | bytes 786436
  6.3 10.7 %copy-start.5 = (bf16[1,1024,128]{2,1,0:T(8,128)(2,1)S(1)}, bf16[1,1024,128]{2,1,0:T(8,128)(2,1)}, u32[]{:S(2)}) copy-start(bf16[1,1024,128]{2,1,0:T(8,128)(2,1)} %param.10) | copy-start | bytes 786436
  6.4 8.2 %collective-permute-start = (bf16[256,128]{1,0:T(8,128)(2,1)S(1)}, bf16[256,128]{1,0:T(8,128)(2,1)S(1)}, u32[]{:S(2)}, u32[]{:S(2)}) collective-permute-start(bf16[256,128]{1,0:T(8,128)(2,1)S(1)} %get-tuple-element.29), channel_id=1, source_target_pairs={{0,24},{8,16},{16,8},{24,0},{1,25},{9,17},{17,9},{25,1},{2,26},{10... | collective-permute-start | bytes 196616 | tf_op jit(solution)/shard_map/ppermute | solution.py:326
  10.0 5.2 %collective-permute-start.1 = (bf16[256,128]{1,0:T(8,128)(2,1)S(1)}, bf16[256,128]{1,0:T(8,128)(2,1)S(1)}, u32[]{:S(2)}, u32[]{:S(2)}) collective-permute-start(bf16[256,128]{1,0:T(8,128)(2,1)S(1)} %get-tuple-element.30), channel_id=1, source_target_pairs={{0,16},{8,24},{16,0},{24,8},{1,17},{9,25},{17,1},{25,9},{2,18},{10... | collective-permute-start | bytes 196616 | tf_op jit(solution)/shard_map/ppermute | solution.py:326
  10.0 5.2 %collective-permute-start.2 = (bf16[256,128]{1,0:T(8,128)(2,1)S(1)}, bf16[256,128]{1,0:T(8,128)(2,1)S(1)}, u32[]{:S(2)}, u32[]{:S(2)}) collective-permute-start(bf16[256,128]{1,0:T(8,128)(2,1)S(1)} %get-tuple-element.31), channel_id=1, source_target_pairs={{0,8},{8,0},{16,24},{24,16},{1,9},{9,1},{17,25},{25,17},{2,10},{10... | collective-permute-start | bytes 196616 | tf_op jit(solution)/shard_map/ppermute | solution.py:326
  10.8 6.2 %collective-permute-start.6 = (bf16[32,2560]{1,0:T(8,128)(2,1)S(1)}, bf16[32,2560]{1,0:T(8,128)(2,1)S(1)}, u32[]{:S(2)}, u32[]{:S(2)}) collective-permute-start(bf16[32,2560]{1,0:T(8,128)(2,1)S(1)} %slice.9), channel_id=1, source_target_pairs={{0,2},{2,0},{4,6},{6,4},{1,3},{3,1},{5,7},{7,5},{8,10},{10,8},{12,... | collective-permute-start | bytes 491528 | tf_op jit(solution)/shard_map/ppermute | solution.py:326
  12.0 5.0 %collective-permute-start.5 = (bf16[32,1536]{1,0:T(8,128)(2,1)S(1)}, bf16[32,1536]{1,0:T(8,128)(2,1)S(1)}, u32[]{:S(2)}, u32[]{:S(2)}) collective-permute-start(bf16[32,1536]{1,0:T(8,128)(2,1)S(1)} %slice.8), channel_id=1, source_target_pairs={{0,4},{2,6},{4,0},{6,2},{1,5},{3,7},{5,1},{7,3},{8,12},{10,14},{12... | collective-permute-start | bytes 294920 | tf_op jit(solution)/shard_map/ppermute | solution.py:326
  19.5 7.7 %collective-permute-start.7 = (bf16[256,128]{1,0:T(8,128)(2,1)S(1)}, bf16[256,128]{1,0:T(8,128)(2,1)S(1)}, u32[]{:S(2)}, u32[]{:S(2)}) collective-permute-start(bf16[256,128]{1,0:T(8,128)(2,1)S(1)} %get-tuple-element.35), channel_id=1, source_target_pairs={{0,24},{8,16},{16,8},{24,0},{1,25},{9,17},{17,9},{25,1},{2,26},{10... | collective-permute-start | bytes 196616 | tf_op jit(solution)/shard_map/ppermute | solution.py:326
  22.8 6.6 %collective-permute-start.8 = (bf16[256,128]{1,0:T(8,128)(2,1)S(1)}, bf16[256,128]{1,0:T(8,128)(2,1)S(1)}, u32[]{:S(2)}, u32[]{:S(2)}) collective-permute-start(bf16[256,128]{1,0:T(8,128)(2,1)S(1)} %get-tuple-element.36), channel_id=1, source_target_pairs={{0,16},{8,24},{16,0},{24,8},{1,17},{9,25},{17,1},{25,9},{2,18},{10... | collective-permute-start | bytes 196616 | tf_op jit(solution)/shard_map/ppermute | solution.py:326
  22.8 6.6 %collective-permute-start.9 = (bf16[256,128]{1,0:T(8,128)(2,1)S(1)}, bf16[256,128]{1,0:T(8,128)(2,1)S(1)}, u32[]{:S(2)}, u32[]{:S(2)}) collective-permute-start(bf16[256,128]{1,0:T(8,128)(2,1)S(1)} %get-tuple-element.37), channel_id=1, source_target_pairs={{0,8},{8,0},{16,24},{24,16},{1,9},{9,1},{17,25},{25,17},{2,10},{10... | collective-permute-start | bytes 196616 | tf_op jit(solution)/shard_map/ppermute | solution.py:326
  24.0 9.6 %collective-permute-start.10 = (bf16[256,128]{1,0:T(8,128)(2,1)S(1)}, bf16[256,128]{1,0:T(8,128)(2,1)S(1)}, u32[]{:S(2)}, u32[]{:S(2)}) collective-permute-start(bf16[256,128]{1,0:T(8,128)(2,1)S(1)} %get-tuple-element.40), channel_id=1, source_target_pairs={{0,24},{8,16},{16,8},{24,0},{1,25},{9,17},{17,9},{25,1},{2,26},{10... | collective-permute-start | bytes 196616 | tf_op jit(solution)/shard_map/ppermute | solution.py:326
  27.2 8.4 %collective-permute-start.11 = (bf16[256,128]{1,0:T(8,128)(2,1)S(1)}, bf16[256,128]{1,0:T(8,128)(2,1)S(1)}, u32[]{:S(2)}, u32[]{:S(2)}) collective-permute-start(bf16[256,128]{1,0:T(8,128)(2,1)S(1)} %get-tuple-element.41), channel_id=1, source_target_pairs={{0,8},{8,0},{16,24},{24,16},{1,9},{9,1},{17,25},{25,17},{2,10},{10... | collective-permute-start | bytes 196616 | tf_op jit(solution)/shard_map/ppermute | solution.py:326
  27.2 8.4 %collective-permute-start.12 = (bf16[256,128]{1,0:T(8,128)(2,1)S(1)}, bf16[256,128]{1,0:T(8,128)(2,1)S(1)}, u32[]{:S(2)}, u32[]{:S(2)}) collective-permute-start(bf16[256,128]{1,0:T(8,128)(2,1)S(1)} %get-tuple-element.42), channel_id=1, source_target_pairs={{0,16},{8,24},{16,0},{24,8},{1,17},{9,25},{17,1},{25,9},{2,18},{10... | collective-permute-start | bytes 196616 | tf_op jit(solution)/shard_map/ppermute | solution.py:326
  31.2 6.8 %collective-permute-start.13 = (bf16[256,128]{1,0:T(8,128)(2,1)S(1)}, bf16[256,128]{1,0:T(8,128)(2,1)S(1)}, u32[]{:S(2)}, u32[]{:S(2)}) collective-permute-start(bf16[256,128]{1,0:T(8,128)(2,1)S(1)} %get-tuple-element.45), channel_id=1, source_target_pairs={{0,24},{8,16},{16,8},{24,0},{1,25},{9,17},{17,9},{25,1},{2,26},{10... | collective-permute-start | bytes 196616 | tf_op jit(solution)/shard_map/ppermute | solution.py:326
  33.6 5.5 %collective-permute-start.14 = (bf16[256,128]{1,0:T(8,128)(2,1)S(1)}, bf16[256,128]{1,0:T(8,128)(2,1)S(1)}, u32[]{:S(2)}, u32[]{:S(2)}) collective-permute-start(bf16[256,128]{1,0:T(8,128)(2,1)S(1)} %get-tuple-element.46), channel_id=1, source_target_pairs={{0,16},{8,24},{16,0},{24,8},{1,17},{9,25},{17,1},{25,9},{2,18},{10... | collective-permute-start | bytes 196616 | tf_op jit(solution)/shard_map/ppermute | solution.py:326
  33.6 5.5 %collective-permute-start.15 = (bf16[256,128]{1,0:T(8,128)(2,1)S(1)}, bf16[256,128]{1,0:T(8,128)(2,1)S(1)}, u32[]{:S(2)}, u32[]{:S(2)}) collective-permute-start(bf16[256,128]{1,0:T(8,128)(2,1)S(1)} %get-tuple-element.47), channel_id=1, source_target_pairs={{0,8},{8,0},{16,24},{24,16},{1,9},{9,1},{17,25},{25,17},{2,10},{10... | collective-permute-start | bytes 196616 | tf_op jit(solution)/shard_map/ppermute | solution.py:326
  37.4 1.6 %collective-permute-start.16 = (bf16[64,512]{1,0:T(8,128)(2,1)S(1)}, bf16[64,512]{1,0:T(8,128)(2,1)S(1)}, u32[]{:S(2)}, u32[]{:S(2)}) collective-permute-start(bf16[64,512]{1,0:T(8,128)(2,1)S(1)} %get-tuple-element.48), channel_id=1, source_target_pairs={{0,1},{1,0},{2,3},{3,2},{4,5},{5,4},{6,7},{7,6},{8,9},{9,8},{10,11... | collective-permute-start | bytes 196616 | tf_op jit(solution)/shard_map/ppermute | solution.py:326
  37.4 1.6 %collective-permute-start.17 = (bf16[64,512]{1,0:T(8,128)(2,1)S(1)}, bf16[64,512]{1,0:T(8,128)(2,1)S(1)}, u32[]{:S(2)}, u32[]{:S(2)}) collective-permute-start(bf16[64,512]{1,0:T(8,128)(2,1)S(1)} %get-tuple-element.49), channel_id=1, source_target_pairs={{0,1},{1,0},{2,3},{3,2},{4,5},{5,4},{6,7},{7,6},{8,9},{9,8},{10,11... | collective-permute-start | bytes 196616 | tf_op jit(solution)/shard_map/ppermute | solution.py:326
  (3 other events, 22.0 us)

commit v3 on v2

--- a/solution.py
+++ b/solution.py
@@ -173,8 +173,8 @@
     return [0, *reversed(range(1, parts))]
 
 
-def back_offsets(parts):
-    return [0, parts - 1, *range(1, parts - 1)]
+def middle_offsets(parts):
+    return [0, *range(parts // 2, parts), *range(1, parts // 2)]
 
 
 def gather_tokens(pieces, whole, here):
@@ -227,27 +227,34 @@
     spec_conv[...] = spectrum_of(whole[...], fwd_hi, fwd_lo)
     product = spectrum_product(spec_filt[...], spec_conv[...], False)
     whole[...] = inverse_dense(product, inv_hi, inv_lo).astype(jnp.bfloat16)
-    scatter_tokens(whole, out, here, back_offsets(parts))
-
-
-def unit_kernel(parts, pieces, after, weight, gate, *refs):
-    grads = refs[:pieces]
-    unit = refs[pieces]
-    out = refs[pieces + 1 : pieces + 1 + parts]
-    rows_all = refs[pieces + 1 + parts]
-    here, block = lax.axis_index("ctx"), lax.axis_index("tp")
+    scatter_tokens(whole, out, here, range(parts))
+
+
+def unit_rows(order, weight, gate, rows_all, unit, out):
+    here = lax.axis_index("ctx")
+    for k, grad, ref in zip(order, unit, out):
+        rows = grad.shape[0]
+        at = place(here ^ k, rows)
+        got = mm_nt(weight[at, :], rows_all[...])
+        grad[...] = got
+        ref[...] = (got * gate[at, :].astype(jnp.float32)).astype(jnp.bfloat16)
+
+
+def far_unit_kernel(order, pieces, after, weight, gate, *refs):
+    grads, count = refs[:pieces], len(order)
+    unit, out, rows_all = refs[pieces : pieces + count], refs[pieces + count : -1], refs[-1]
+    block = lax.axis_index("tp")
     rows = grads[0].shape[0]
     cut = grads[3].shape[1]
     for k, ref in enumerate(grads[:3]):
         rows_all[place(block ^ k, rows), :] = ref[...]
     rows_all[place(block ^ 3, rows), :cut] = grads[3][...]
     rows_all[place(block ^ 3, rows), cut:] = grads[4][...]
-    rows = out[0].shape[0]
-    for k, ref in zip(offsets(parts), out):
-        at = place(here ^ k, rows)
-        got = mm_nt(weight[at, :], rows_all[...])
-        unit[at, :] = got
-        ref[...] = (got * gate[at, :].astype(jnp.float32)).astype(jnp.bfloat16)
+    unit_rows(order, weight, gate, rows_all, unit, out)
+
+
+def own_unit_kernel(order, weight, gate, rows_all, unit, out):
+    unit_rows(order, weight, gate, rows_all, [unit], [out])
 
 
 def grad_kernel(parts, *refs):
@@ -260,17 +267,11 @@
     spec_gate[...] = spectrum_of(whole[...], fwd_hi, fwd_lo)
     product = spectrum_product(spec_filt[...], spec_gate[...], True)
     whole[...] = inverse_dense(product, inv_hi, inv_lo).astype(jnp.bfloat16)
-    scatter_tokens(whole, out, here, offsets(parts))
-
-
-def filter_kernel(parts, scale, spec_conv, spec_gate, inv_hi, inv_lo, unit, *refs):
-    back = refs[:parts]
-    keep, *send, out, whole = refs[parts:]
-    here = lax.axis_index("ctx")
-    rows = back[0].shape[0]
-    for k, ref in zip(back_offsets(parts), back):
-        at = place(here ^ k, rows)
-        out[at, :] = (unit[at, :] * ref[...].astype(jnp.float32)).astype(jnp.bfloat16)
+    scatter_tokens(whole, out, here, middle_offsets(parts))
+
+
+def filter_kernel(parts, scale, spec_conv, spec_gate, inv_hi, inv_lo, *refs):
+    keep, *send, whole = refs[parts:]
     product = spectrum_product(spec_conv[...], spec_gate[...], True)
     whole[...] = inverse_dense(product, inv_hi, inv_lo) * scale
     rows = keep.shape[0]
@@ -281,6 +282,15 @@
         ref[...] = whole[pl.ds(at, step), :].astype(jnp.bfloat16)
 
 
+def gate_kernel(parts, *refs):
+    unit, back, out = refs[:parts], refs[parts : 2 * parts], refs[2 * parts]
+    here = lax.axis_index("ctx")
+    rows = back[0].shape[0]
+    for k, grad, ref in zip(range(parts), unit, back):
+        gated = grad[...] * ref[...].astype(jnp.float32)
+        out[place(here ^ k, rows), :] = gated.astype(jnp.bfloat16)
+
+
 def last_kernel(parts, *refs):
     back, (low, high, keep, total, out) = refs[:parts], refs[parts:]
     step = low.shape[0]
@@ -289,7 +299,7 @@
         total[at, :] = keep[at, :] + ref[...].astype(jnp.float32)
     here = lax.axis_index("ctx")
     rows = back[0].shape[0]
-    for k, ref in zip(offsets(parts), back):
+    for k, ref in zip(middle_offsets(parts), back):
         out[place(here ^ k, rows), :] = ref[...]
 
 
@@ -322,6 +332,7 @@
     scale = 1.0 / math.sqrt(length)
     tables = [jnp.asarray(t) for t in dense_tables(length)]
     shape = jax.ShapeDtypeStruct
+
     def swap(value, axis, size, k):
         return lax.ppermute(value, axis, [(i, i ^ k) for i in range(size)])
 
@@ -339,7 +350,7 @@
         cost=10.0,
     )
     conv_pieces = exchange(blocks, offsets(parts))
-    cut = width * 3 // 8
+    cut = width // 16 * 5
     grad_3a = swap(grad_1[:, :cut], "tp", groups, 2)
     grad_3b = swap(grad_2[:, cut:], "tp", groups, 1)
 
@@ -359,28 +370,42 @@
         [whole],
         cost=2.0,
     )
-    conv_back = exchange(conv_out, back_offsets(parts))
-
-    unit, *gate_pieces = call(
-        functools.partial(unit_kernel, parts, 5),
-        [shape((channels, tokens), f32)] + [piece] * parts,
+
+    away = offsets(parts)[1:]
+    grad_all = shape((groups * grad_rows.shape[0], width), bf16)
+    unit_piece = shape((chans, tokens), f32)
+    *far, grad_all = call(
+        functools.partial(far_unit_kernel, away, 5),
+        [unit_piece] * len(away) + [piece] * len(away) + [grad_all],
         [conv_out[0], out_weight, gate_local, grad_rows, grad_1, grad_2, grad_3a, grad_3b],
-        [pltpu.VMEM((groups * grad_rows.shape[0], width), bf16)],
-    )
-    gate_chan = exchange(gate_pieces, offsets(parts))
+    )
+    unit_own, gate_own = call(
+        functools.partial(own_unit_kernel, [0]),
+        [unit_piece, piece],
+        [out_weight, gate_local, grad_all],
+    )
+    *conv_out, gate_own = lax.optimization_barrier((*conv_out, gate_own))
+    conv_back = exchange(conv_out, range(parts))
+    gate_chan = exchange([gate_own, *far[len(away) :]], offsets(parts))
+    unit = dict(zip(offsets(parts), [unit_own, *far[: len(away)]]))
     *conv_grad, spec_gate = call(
         functools.partial(grad_kernel, parts),
         [piece] * parts + [spectrum],
         [*gate_chan, spec_filt, *tables],
         [whole],
     )
-    grad_back = exchange(conv_grad, offsets(parts))
+    grad_back = exchange(conv_grad, middle_offsets(parts))
     half, local = shape((chans // 2, length), f32), shape((channels, tokens), bf16)
     quarter = shape((chans // 4, length), bf16)
-    keep, send_low, send_high, gate_out = call(
+    gate_out = call(
+        functools.partial(gate_kernel, parts),
+        local,
+        [*(unit[k] for k in range(parts)), *conv_back],
+    )
+    keep, send_low, send_high = call(
         functools.partial(filter_kernel, parts, scale),
-        [half, quarter, quarter, local],
-        [spec_conv, spec_gate, *tables[2:], unit, *conv_back],
+        [half, quarter, quarter],
+        [spec_conv, spec_gate, *tables[2:], *conv_back],
         [pltpu.VMEM((chans, length), f32)],
         cost=2.0,
     )

time: 40 us -> 39.5 us (0.988)
  starting transfers between devices: 25.5 us -> 24.7 us
    ppermute x18, starting transfers between devices: 25.5 us -> 24.7 us  [swap(): return lax.ppermute(value, axis, [(i, i ^ k) for i in range(size)])]
    pallas_call x7 -> x9, Pallas kernels: 10.6 us -> 10.8 us  [call(): pl.pallas_call(kernel, out_shape=outs, in_specs=[hbm if i in far else vme...]
  transfers between devices with their start and end apart: 18 -> 18, of which waited for: 3 -> 5; matrix products, arithmetic and copies ran while one was open for 0% -> 0% of each run, Pallas kernels for 18% -> 21%
where the time goes in v3:
time: 39.5 us; the launch traced here: 39.3 us
  starting transfers between devices  24.7 us (63%)
  Pallas kernels  10.8 us (27%)
  waiting for transfers between devices  2.88 us (7%)
  between operations  0.83 us (2%)
    ppermute x18, starting transfers between devices, swap(): return lax.ppermute(value, axis, [(i, i ^ k) for i in range(size)])  24.7 us
    pallas_call x9, Pallas kernels, call(): pl.pallas_call(kernel, out_shape=outs, in_specs=[hbm if i in far else vme...  10.8 us
    ppermute x18, waiting for transfers between devices, swap(): return lax.ppermute(value, axis, [(i, i ^ k) for i in range(size)])  2.88 us
  transfers between devices with their start and end apart: 18, of which 5 were waited for; matrix products, arithmetic and copies ran while one was open for 0% of the time, Pallas kernels for 21%

profile of v3, /device:TPU:0, one launch (start us, length us, event | category | flops | bytes accessed | tf_op | source)
XLA Modules:
  0.0 39.3 jit_solution(16791644041408987581)
XLA Ops:
  0.6 3.0 %collective-permute-start.4 = (bf16[32,4096]{1,0:T(8,128)(2,1)}, bf16[32,4096]{1,0:T(8,128)(2,1)S(1)}, u32[]{:S(2)}, u32[]{:S(2)}) collective-permute-start(bf16[32,4096]{1,0:T(8,128)(2,1)} %bitcast.9), channel_id=1, source_target_pairs={{0,4},{2,6},{4,0},{6,2},{1,5},{3,7},{5,1},{7,3},{8,12},{10,14},{12... | collective-permute-start | bytes 786440 | tf_op jit(solution)/shard_map/ppermute | solution.py:337
  3.7 1.5 %collective-permute-start.3 = (bf16[32,4096]{1,0:T(8,128)(2,1)}, bf16[32,4096]{1,0:T(8,128)(2,1)S(1)}, u32[]{:S(2)}, u32[]{:S(2)}) collective-permute-start(bf16[32,4096]{1,0:T(8,128)(2,1)} %bitcast.10), channel_id=1, source_target_pairs={{0,2},{2,0},{4,6},{6,4},{1,3},{3,1},{5,7},{7,5},{8,10},{10,8},{12,... | collective-permute-start | bytes 786440 | tf_op jit(solution)/shard_map/ppermute | solution.py:337
  5.2 1.1 %shard_map.112 = (bf16[256,128]{1,0:T(8,128)(2,1)S(1)}, bf16[256,128]{1,0:T(8,128)(2,1)S(1)}, bf16[256,128]{1,0:T(8,128)(2,1)S(1)}, bf16[256,128]{1,0:T(8,128)(2,1)S(1)}) custom-call(bf16[1024,128]{1,0:T(8,128)(2,1)} %bitcast.12), custom_call_target="tpu_custom_call" | custom-call | flops 10000000000 | bytes 10000000 | tf_op jit(solution)/shard_map/pallas_call | solution.py:313
  6.4 3.7 %collective-permute-start = (bf16[256,128]{1,0:T(8,128)(2,1)S(1)}, bf16[256,128]{1,0:T(8,128)(2,1)S(1)}, u32[]{:S(2)}, u32[]{:S(2)}) collective-permute-start(bf16[256,128]{1,0:T(8,128)(2,1)S(1)} %get-tuple-element.37), channel_id=1, source_target_pairs={{0,24},{8,16},{16,8},{24,0},{1,25},{9,17},{17,9},{25,1},{2,26},{10... | collective-permute-start | bytes 196616 | tf_op jit(solution)/shard_map/ppermute | solution.py:337
  10.0 0.8 %collective-permute-start.2 = (bf16[256,128]{1,0:T(8,128)(2,1)S(1)}, bf16[256,128]{1,0:T(8,128)(2,1)S(1)}, u32[]{:S(2)}, u32[]{:S(2)}) collective-permute-start(bf16[256,128]{1,0:T(8,128)(2,1)S(1)} %get-tuple-element.39), channel_id=1, source_target_pairs={{0,8},{8,0},{16,24},{24,16},{1,9},{9,1},{17,25},{25,17},{2,10},{10... | collective-permute-start | bytes 196616 | tf_op jit(solution)/shard_map/ppermute | solution.py:337
  10.8 1.1 %collective-permute-start.6 = (bf16[32,2816]{1,0:T(8,128)(2,1)S(1)}, bf16[32,2816]{1,0:T(8,128)(2,1)S(1)}, u32[]{:S(2)}, u32[]{:S(2)}) collective-permute-start(bf16[32,2816]{1,0:T(8,128)(2,1)S(1)} %slice.9), channel_id=1, source_target_pairs={{0,2},{2,0},{4,6},{6,4},{1,3},{3,1},{5,7},{7,5},{8,10},{10,8},{12,... | collective-permute-start | bytes 540680 | tf_op jit(solution)/shard_map/ppermute | solution.py:337
  12.0 1.6 %collective-permute-start.5 = (bf16[32,1280]{1,0:T(8,128)(2,1)S(1)}, bf16[32,1280]{1,0:T(8,128)(2,1)S(1)}, u32[]{:S(2)}, u32[]{:S(2)}) collective-permute-start(bf16[32,1280]{1,0:T(8,128)(2,1)S(1)} %slice.8), channel_id=1, source_target_pairs={{0,4},{2,6},{4,0},{6,2},{1,5},{3,7},{5,1},{7,3},{8,12},{10,14},{12... | collective-permute-start | bytes 245768 | tf_op jit(solution)/shard_map/ppermute | solution.py:337
  13.6 1.0 %shard_map.113.refs_4_ = f32[256,1024]{1,0:T(8,128)S(1)} custom-call(f32[256,512]{1,0:T(8,128)S(1)} %copy-done.6, bf16[512,1024]{1,0:T(8,128)(2,1)S(1)} %copy-done.4, bf16[512,1024]{1,0:T(8,128)(2,1)S(1)} %copy-done.3, bf16[32,4096]{1,0:T(8,128)(2,1)S(1)} %collective-permute-done.3.after_1.refs_1_, bf16[32,4096]{1,0:T(8,128)(2,1)S(1)} %collective-permute-done.4.after_2.refs_2_), custom_call_target="tpu_custom_call" | custom-call | flops 2000000000 | bytes 2000000 | tf_op jit(solution)/shard_map/pallas_call | solution.py:313
  14.6 0.7 %collective-permute-done.1.refs_2_ = bf16[256,128]{1,0:T(8,128)(2,1)S(1)} collective-permute-done((bf16[256,128]{1,0:T(8,128)(2,1)S(1)}, bf16[256,128]{1,0:T(8,128)(2,1)S(1)}, u32[]{:S(2)}, u32[]{:S(2)}) %collective-permute-start.1) | collective-permute-done | bytes 65568 | tf_op jit(solution)/shard_map/ppermute | solution.py:337
  15.3 1.7 %shard_map.114 = (bf16[256,128]{1,0:T(8,128)(2,1)S(1)}, bf16[256,128]{1,0:T(8,128)(2,1)S(1)}, bf16[256,128]{1,0:T(8,128)(2,1)S(1)}, bf16[256,128]{1,0:T(8,128)(2,1)S(1)}, f32[256,1024]{1,0:T(8,128)S(1)}) custom-call(bf16[256,128]{1,0:T(8,128)(2,1)S(1)} %get-tuple-element.36.refs_0_, bf16[256,128]{1,0:T(8,128)(2,1)S(1)} %collective-permute-done.refs_1_, ...), custom_call_target="tpu_custom_call" | custom-call | flops 2000000000 | bytes 2000000 | tf_op jit(solution)/shard_map/pallas_call | solution.py:313
  17.1 1.9 %shard_map.115 = (f32[256,128]{1,0:T(8,128)S(1)}, f32[256,128]{1,0:T(8,128)S(1)}, f32[256,128]{1,0:T(8,128)S(1)}, bf16[256,128]{1,0:T(8,128)(2,1)S(1)}, bf16[256...) custom-call(bf16[256,128]{1,0:T(8,128)(2,1)S(1)} %get-tuple-element.50.after.refs_4_.refs_0_, ...), custom_call_target="tpu_custom_call" | custom-call | flops 1000000000 | bytes 1000000 | tf_op jit(solution)/shard_map/pallas_call | solution.py:313
  19.0 3.1 %collective-permute-start.10 = (bf16[256,128]{1,0:T(8,128)(2,1)S(1)}, bf16[256,128]{1,0:T(8,128)(2,1)S(1)}, u32[]{:S(2)}, u32[]{:S(2)}) collective-permute-start(bf16[256,128]{1,0:T(8,128)(2,1)S(1)} %get-tuple-element.55), channel_id=1, source_target_pairs={{0,24},{8,16},{16,8},{24,0},{1,25},{9,17},{17,9},{25,1},{2,26},{10... | collective-permute-start | bytes 196616 | tf_op jit(solution)/shard_map/ppermute | solution.py:337
  22.1 1.3 %collective-permute-start.12 = (bf16[256,128]{1,0:T(8,128)(2,1)S(1)}, bf16[256,128]{1,0:T(8,128)(2,1)S(1)}, u32[]{:S(2)}, u32[]{:S(2)}) collective-permute-start(bf16[256,128]{1,0:T(8,128)(2,1)S(1)} %get-tuple-element.57), channel_id=1, source_target_pairs={{0,8},{8,0},{16,24},{24,16},{1,9},{9,1},{17,25},{25,17},{2,10},{10... | collective-permute-start | bytes 196616 | tf_op jit(solution)/shard_map/ppermute | solution.py:337
  23.4 0.7 %shard_map.116 = (f32[256,128]{1,0:T(8,128)S(1)}, bf16[256,128]{1,0:T(8,128)(2,1)S(1)}) custom-call(bf16[1024,4096]{1,0:T(8,128)(2,1)S(1)} %bitcast.6, bf16[1024,128]{1,0:T(8,128)(2,1)S(1)} %bitcast.8, bf16[128,4096]{1,0:T(8,128)(2,1)S(1)} %get-tuple-element.41.rows_all), custom_call_target="tpu_custom_call" | custom-call | flops 1000000000 | bytes 1000000 | tf_op jit(solution)/shard_map/pallas_call | solution.py:313
  24.1 0.8 %collective-permute-start.7 = (bf16[256,128]{1,0:T(8,128)(2,1)S(1)}, bf16[256,128]{1,0:T(8,128)(2,1)S(1)}, u32[]{:S(2)}, u32[]{:S(2)}) collective-permute-start(bf16[256,128]{1,0:T(8,128)(2,1)S(1)} %get-tuple-element.51), channel_id=1, source_target_pairs={{0,8},{8,0},{16,24},{24,16},{1,9},{9,1},{17,25},{25,17},{2,10},{10... | collective-permute-start | bytes 196616 | tf_op jit(solution)/shard_map/ppermute | solution.py:337
  24.9 2.9 %collective-permute-start.8 = (bf16[256,128]{1,0:T(8,128)(2,1)S(1)}, bf16[256,128]{1,0:T(8,128)(2,1)S(1)}, u32[]{:S(2)}, u32[]{:S(2)}) collective-permute-start(bf16[256,128]{1,0:T(8,128)(2,1)S(1)} %get-tuple-element.52), channel_id=1, source_target_pairs={{0,16},{8,24},{16,0},{24,8},{1,17},{9,25},{17,1},{25,9},{2,18},{10... | collective-permute-start | bytes 196616 | tf_op jit(solution)/shard_map/ppermute | solution.py:337
  27.8 0.8 %collective-permute-start.9 = (bf16[256,128]{1,0:T(8,128)(2,1)S(1)}, bf16[256,128]{1,0:T(8,128)(2,1)S(1)}, u32[]{:S(2)}, u32[]{:S(2)}) collective-permute-start(bf16[256,128]{1,0:T(8,128)(2,1)S(1)} %get-tuple-element.53), channel_id=1, source_target_pairs={{0,24},{8,16},{16,8},{24,0},{1,25},{9,17},{17,9},{25,1},{2,26},{10... | collective-permute-start | bytes 196616 | tf_op jit(solution)/shard_map/ppermute | solution.py:337
  28.9 1.7 %shard_map.118 = (bf16[256,128]{1,0:T(8,128)(2,1)S(1)}, bf16[256,128]{1,0:T(8,128)(2,1)S(1)}, bf16[256,128]{1,0:T(8,128)(2,1)S(1)}, bf16[256,128]{1,0:T(8,128)(2,1)S(1)}, f32[256,1024]{1,0:T(8,128)S(1)}) custom-call(bf16[256,128]{1,0:T(8,128)(2,1)S(1)} %get-tuple-element.54.refs_0_, bf16[256,128]{1,0:T(8,128)(2,1)S(1)} %collective-permute-done.10.refs_1_, ...), custom_call_target="tpu_custom_call" | custom-call | flops 1000000000 | bytes 1000000 | tf_op jit(solution)/shard_map/pallas_call | solution.py:313
  31.2 2.4 %collective-permute-start.14 = (bf16[256,128]{1,0:T(8,128)(2,1)S(1)}, bf16[256,128]{1,0:T(8,128)(2,1)S(1)}, u32[]{:S(2)}, u32[]{:S(2)}) collective-permute-start(bf16[256,128]{1,0:T(8,128)(2,1)S(1)} %get-tuple-element.60), channel_id=1, source_target_pairs={{0,24},{8,16},{16,8},{24,0},{1,25},{9,17},{17,9},{25,1},{2,26},{10... | collective-permute-start | bytes 196616 | tf_op jit(solution)/shard_map/ppermute | solution.py:337
  33.5 0.7 %collective-permute-start.15 = (bf16[256,128]{1,0:T(8,128)(2,1)S(1)}, bf16[256,128]{1,0:T(8,128)(2,1)S(1)}, u32[]{:S(2)}, u32[]{:S(2)}) collective-permute-start(bf16[256,128]{1,0:T(8,128)(2,1)S(1)} %get-tuple-element.61), channel_id=1, source_target_pairs={{0,8},{8,0},{16,24},{24,16},{1,9},{9,1},{17,25},{25,17},{2,10},{10... | collective-permute-start | bytes 196616 | tf_op jit(solution)/shard_map/ppermute | solution.py:337
  34.6 1.1 %shard_map.119 = (f32[128,512]{1,0:T(8,128)S(1)}, bf16[64,512]{1,0:T(8,128)(2,1)S(1)}, bf16[64,512]{1,0:T(8,128)(2,1)S(1)}) custom-call(f32[256,1024]{1,0:T(8,128)S(1)} %get-tuple-element.62.spec_conv, f32[256,1024]{1,0:T(8,128)S(1)} %get-tuple-element.63.spec_gate, bf16[1024,512]{1,0:T(8,128)(2,1)S(1)} %copy-done.2, bf16[1024,512]{1,0:T(8,128)(2,1)S(1)} %copy-done.1, ...), custom_call_target="tpu_custom_call" | custom-call | flops 2000000000 | bytes 2000000 | tf_op jit(solution)/shard_map/pallas_call | solution.py:313
  36.2 0.7 %shard_map.117 = bf16[1024,128]{1,0:T(8,128)(2,1)} custom-call(f32[256,128]{1,0:T(8,128)S(1)} %get-tuple-element.42.refs_0_, f32[256,128]{1,0:T(8,128)S(1)} %get-tuple-element.43.refs_1_, f32[256,128]{1,0:T(8,128)S(1)} %get-tuple-element.44.refs_2_, f32[256,128]{1,0:T(8,128)S(1)} %get-tuple-element.45.refs_3_, ...), custom_call_target="tpu_custom_call" | custom-call | flops 1000000000 | bytes 1000000 | tf_op jit(solution)/shard_map/pallas_call | solution.py:313
  37.0 0.9 %collective-permute-done.13.refs_1_ = bf16[256,128]{1,0:T(8,128)(2,1)S(1)} collective-permute-done((bf16[256,128]{1,0:T(8,128)(2,1)S(1)}, bf16[256,128]{1,0:T(8,128)(2,1)S(1)}, u32[]{:S(2)}, u32[]{:S(2)}) %collective-permute-start.13) | collective-permute-done | bytes 65568 | tf_op jit(solution)/shard_map/ppermute | solution.py:337
  38.5 0.8 %shard_map.120 = (f32[128,512]{1,0:T(8,128)}, bf16[1024,128]{1,0:T(8,128)(2,1)}) custom-call(bf16[256,128]{1,0:T(8,128)(2,1)S(1)} %get-tuple-element.58.refs_0_, bf16[256,128]{1,0:T(8,128)(2,1)S(1)} %collective-permute-done.13.refs_1_, bf16[256,128]{1,0:T(8,128)(2,1)S(1)} %collective-permute-done.14.refs_2_, ...), custom_call_target="tpu_custom_call" | custom-call | flops 1000000000 | bytes 1000000 | tf_op jit(solution)/shard_map/pallas_call | solution.py:313
  (42 shorter events, 2.5 us)
Async XLA Ops:
  0.6 10.2 %collective-permute-start.4 = (bf16[32,4096]{1,0:T(8,128)(2,1)}, bf16[32,4096]{1,0:T(8,128)(2,1)S(1)}, u32[]{:S(2)}, u32[]{:S(2)}) collective-permute-start(bf16[32,4096]{1,0:T(8,128)(2,1)} %bitcast.9), channel_id=1, source_target_pairs={{0,4},{2,6},{4,0},{6,2},{1,5},{3,7},{5,1},{7,3},{8,12},{10,14},{12... | collective-permute-start | bytes 786440 | tf_op jit(solution)/shard_map/ppermute | solution.py:337
  3.7 8.3 %collective-permute-start.3 = (bf16[32,4096]{1,0:T(8,128)(2,1)}, bf16[32,4096]{1,0:T(8,128)(2,1)S(1)}, u32[]{:S(2)}, u32[]{:S(2)}) collective-permute-start(bf16[32,4096]{1,0:T(8,128)(2,1)} %bitcast.10), channel_id=1, source_target_pairs={{0,2},{2,0},{4,6},{6,4},{1,3},{3,1},{5,7},{7,5},{8,10},{10,8},{12,... | collective-permute-start | bytes 786440 | tf_op jit(solution)/shard_map/ppermute | solution.py:337
  5.2 8.4 %copy-start.6 = (f32[256,512]{1,0:T(8,128)S(1)}, f32[256,512]{1,0:T(8,128)}, u32[]{:S(2)}) copy-start(f32[256,512]{1,0:T(8,128)} %filt.1) | copy-start | bytes 1572868
  5.2 10.1 %copy-start.1 = (bf16[1024,512]{1,0:T(8,128)(2,1)S(1)}, bf16[1024,512]{1,0:T(8,128)(2,1)}, u32[]{:S(2)}) copy-start(bf16[1024,512]{1,0:T(8,128)(2,1)} %constant.11.clone.refs_8_.inv_lo) | copy-start | bytes 3145732
  5.2 10.1 %copy-start.2 = (bf16[1024,512]{1,0:T(8,128)(2,1)S(1)}, bf16[1024,512]{1,0:T(8,128)(2,1)}, u32[]{:S(2)}) copy-start(bf16[1024,512]{1,0:T(8,128)(2,1)} %constant.10.clone.refs_7_.inv_hi) | copy-start | bytes 3145732
  6.3 10.7 %slice-start = ((s8[8388608]{0:T(1024)(128)(4,1)}), s8[4194304]{0:T(1024)(128)(4,1)S(1)}, s32[]{:S(2)}) async-start(s8[8388608]{0:T(1024)(128)(4,1)} %bitcast.5), calls=%async_computation | async-start | bytes 8388608
  6.3 10.7 %copy-start = (bf16[1,1024,128]{2,1,0:T(8,128)(2,1)S(1)}, bf16[1,1024,128]{2,1,0:T(8,128)(2,1)}, u32[]{:S(2)}) copy-start(bf16[1,1024,128]{2,1,0:T(8,128)(2,1)} %param.10) | copy-start | bytes 786436
  6.3 10.7 %copy-start.5 = (bf16[1,32,4096]{2,1,0:T(8,128)(2,1)S(1)}, bf16[1,32,4096]{2,1,0:T(8,128)(2,1)}, u32[]{:S(2)}) copy-start(bf16[1,32,4096]{2,1,0:T(8,128)(2,1)} %param.9) | copy-start | bytes 786436
  6.4 8.2 %collective-permute-start = (bf16[256,128]{1,0:T(8,128)(2,1)S(1)}, bf16[256,128]{1,0:T(8,128)(2,1)S(1)}, u32[]{:S(2)}, u32[]{:S(2)}) collective-permute-start(bf16[256,128]{1,0:T(8,128)(2,1)S(1)} %get-tuple-element.37), channel_id=1, source_target_pairs={{0,24},{8,16},{16,8},{24,0},{1,25},{9,17},{17,9},{25,1},{2,26},{10... | collective-permute-start | bytes 196616 | tf_op jit(solution)/shard_map/ppermute | solution.py:337
  10.0 5.2 %collective-permute-start.1 = (bf16[256,128]{1,0:T(8,128)(2,1)S(1)}, bf16[256,128]{1,0:T(8,128)(2,1)S(1)}, u32[]{:S(2)}, u32[]{:S(2)}) collective-permute-start(bf16[256,128]{1,0:T(8,128)(2,1)S(1)} %get-tuple-element.38), channel_id=1, source_target_pairs={{0,16},{8,24},{16,0},{24,8},{1,17},{9,25},{17,1},{25,9},{2,18},{10... | collective-permute-start | bytes 196616 | tf_op jit(solution)/shard_map/ppermute | solution.py:337
  10.0 5.2 %collective-permute-start.2 = (bf16[256,128]{1,0:T(8,128)(2,1)S(1)}, bf16[256,128]{1,0:T(8,128)(2,1)S(1)}, u32[]{:S(2)}, u32[]{:S(2)}) collective-permute-start(bf16[256,128]{1,0:T(8,128)(2,1)S(1)} %get-tuple-element.39), channel_id=1, source_target_pairs={{0,8},{8,0},{16,24},{24,16},{1,9},{9,1},{17,25},{25,17},{2,10},{10... | collective-permute-start | bytes 196616 | tf_op jit(solution)/shard_map/ppermute | solution.py:337
  10.8 6.2 %collective-permute-start.6 = (bf16[32,2816]{1,0:T(8,128)(2,1)S(1)}, bf16[32,2816]{1,0:T(8,128)(2,1)S(1)}, u32[]{:S(2)}, u32[]{:S(2)}) collective-permute-start(bf16[32,2816]{1,0:T(8,128)(2,1)S(1)} %slice.9), channel_id=1, source_target_pairs={{0,2},{2,0},{4,6},{6,4},{1,3},{3,1},{5,7},{7,5},{8,10},{10,8},{12,... | collective-permute-start | bytes 540680 | tf_op jit(solution)/shard_map/ppermute | solution.py:337
  12.0 5.0 %collective-permute-start.5 = (bf16[32,1280]{1,0:T(8,128)(2,1)S(1)}, bf16[32,1280]{1,0:T(8,128)(2,1)S(1)}, u32[]{:S(2)}, u32[]{:S(2)}) collective-permute-start(bf16[32,1280]{1,0:T(8,128)(2,1)S(1)} %slice.8), channel_id=1, source_target_pairs={{0,4},{2,6},{4,0},{6,2},{1,5},{3,7},{5,1},{7,3},{8,12},{10,14},{12... | collective-permute-start | bytes 245768 | tf_op jit(solution)/shard_map/ppermute | solution.py:337
  19.0 8.8 %collective-permute-start.10 = (bf16[256,128]{1,0:T(8,128)(2,1)S(1)}, bf16[256,128]{1,0:T(8,128)(2,1)S(1)}, u32[]{:S(2)}, u32[]{:S(2)}) collective-permute-start(bf16[256,128]{1,0:T(8,128)(2,1)S(1)} %get-tuple-element.55), channel_id=1, source_target_pairs={{0,24},{8,16},{16,8},{24,0},{1,25},{9,17},{17,9},{25,1},{2,26},{10... | collective-permute-start | bytes 196616 | tf_op jit(solution)/shard_map/ppermute | solution.py:337
  22.1 6.8 %collective-permute-start.11 = (bf16[256,128]{1,0:T(8,128)(2,1)S(1)}, bf16[256,128]{1,0:T(8,128)(2,1)S(1)}, u32[]{:S(2)}, u32[]{:S(2)}) collective-permute-start(bf16[256,128]{1,0:T(8,128)(2,1)S(1)} %get-tuple-element.56), channel_id=1, source_target_pairs={{0,16},{8,24},{16,0},{24,8},{1,17},{9,25},{17,1},{25,9},{2,18},{10... | collective-permute-start | bytes 196616 | tf_op jit(solution)/shard_map/ppermute | solution.py:337
  22.1 6.8 %collective-permute-start.12 = (bf16[256,128]{1,0:T(8,128)(2,1)S(1)}, bf16[256,128]{1,0:T(8,128)(2,1)S(1)}, u32[]{:S(2)}, u32[]{:S(2)}) collective-permute-start(bf16[256,128]{1,0:T(8,128)(2,1)S(1)} %get-tuple-element.57), channel_id=1, source_target_pairs={{0,8},{8,0},{16,24},{24,16},{1,9},{9,1},{17,25},{25,17},{2,10},{10... | collective-permute-start | bytes 196616 | tf_op jit(solution)/shard_map/ppermute | solution.py:337
  24.1 9.4 %collective-permute-start.7 = (bf16[256,128]{1,0:T(8,128)(2,1)S(1)}, bf16[256,128]{1,0:T(8,128)(2,1)S(1)}, u32[]{:S(2)}, u32[]{:S(2)}) collective-permute-start(bf16[256,128]{1,0:T(8,128)(2,1)S(1)} %get-tuple-element.51), channel_id=1, source_target_pairs={{0,8},{8,0},{16,24},{24,16},{1,9},{9,1},{17,25},{25,17},{2,10},{10... | collective-permute-start | bytes 196616 | tf_op jit(solution)/shard_map/ppermute | solution.py:337
  24.9 9.3 %collective-permute-start.8 = (bf16[256,128]{1,0:T(8,128)(2,1)S(1)}, bf16[256,128]{1,0:T(8,128)(2,1)S(1)}, u32[]{:S(2)}, u32[]{:S(2)}) collective-permute-start(bf16[256,128]{1,0:T(8,128)(2,1)S(1)} %get-tuple-element.52), channel_id=1, source_target_pairs={{0,16},{8,24},{16,0},{24,8},{1,17},{9,25},{17,1},{25,9},{2,18},{10... | collective-permute-start | bytes 196616 | tf_op jit(solution)/shard_map/ppermute | solution.py:337
  27.8 6.7 %collective-permute-start.9 = (bf16[256,128]{1,0:T(8,128)(2,1)S(1)}, bf16[256,128]{1,0:T(8,128)(2,1)S(1)}, u32[]{:S(2)}, u32[]{:S(2)}) collective-permute-start(bf16[256,128]{1,0:T(8,128)(2,1)S(1)} %get-tuple-element.53), channel_id=1, source_target_pairs={{0,24},{8,16},{16,8},{24,0},{1,25},{9,17},{17,9},{25,1},{2,26},{10... | collective-permute-start | bytes 196616 | tf_op jit(solution)/shard_map/ppermute | solution.py:337
  30.6 7.2 %collective-permute-start.13 = (bf16[256,128]{1,0:T(8,128)(2,1)S(1)}, bf16[256,128]{1,0:T(8,128)(2,1)S(1)}, u32[]{:S(2)}, u32[]{:S(2)}) collective-permute-start(bf16[256,128]{1,0:T(8,128)(2,1)S(1)} %get-tuple-element.59), channel_id=1, source_target_pairs={{0,16},{8,24},{16,0},{24,8},{1,17},{9,25},{17,1},{25,9},{2,18},{10... | collective-permute-start | bytes 196616 | tf_op jit(solution)/shard_map/ppermute | solution.py:337
  31.2 6.7 %collective-permute-start.14 = (bf16[256,128]{1,0:T(8,128)(2,1)S(1)}, bf16[256,128]{1,0:T(8,128)(2,1)S(1)}, u32[]{:S(2)}, u32[]{:S(2)}) collective-permute-start(bf16[256,128]{1,0:T(8,128)(2,1)S(1)} %get-tuple-element.60), channel_id=1, source_target_pairs={{0,24},{8,16},{16,8},{24,0},{1,25},{9,17},{17,9},{25,1},{2,26},{10... | collective-permute-start | bytes 196616 | tf_op jit(solution)/shard_map/ppermute | solution.py:337
  33.5 4.9 %collective-permute-start.15 = (bf16[256,128]{1,0:T(8,128)(2,1)S(1)}, bf16[256,128]{1,0:T(8,128)(2,1)S(1)}, u32[]{:S(2)}, u32[]{:S(2)}) collective-permute-start(bf16[256,128]{1,0:T(8,128)(2,1)S(1)} %get-tuple-element.61), channel_id=1, source_target_pairs={{0,8},{8,0},{16,24},{24,16},{1,9},{9,1},{17,25},{25,17},{2,10},{10... | collective-permute-start | bytes 196616 | tf_op jit(solution)/shard_map/ppermute | solution.py:337
  35.6 2.8 %collective-permute-start.16 = (bf16[64,512]{1,0:T(8,128)(2,1)S(1)}, bf16[64,512]{1,0:T(8,128)(2,1)S(1)}, u32[]{:S(2)}, u32[]{:S(2)}) collective-permute-start(bf16[64,512]{1,0:T(8,128)(2,1)S(1)} %get-tuple-element.64), channel_id=1, source_target_pairs={{0,1},{1,0},{2,3},{3,2},{4,5},{5,4},{6,7},{7,6},{8,9},{9,8},{10,11... | collective-permute-start | bytes 196616 | tf_op jit(solution)/shard_map/ppermute | solution.py:337
  35.7 2.8 %collective-permute-start.17 = (bf16[64,512]{1,0:T(8,128)(2,1)S(1)}, bf16[64,512]{1,0:T(8,128)(2,1)S(1)}, u32[]{:S(2)}, u32[]{:S(2)}) collective-permute-start(bf16[64,512]{1,0:T(8,128)(2,1)S(1)} %get-tuple-element.65), channel_id=1, source_target_pairs={{0,1},{1,0},{2,3},{3,2},{4,5},{5,4},{6,7},{7,6},{8,9},{9,8},{10,11... | collective-permute-start | bytes 196616 | tf_op jit(solution)/shard_map/ppermute | solution.py:337
  (3 other events, 22.0 us)

commit v4 on v3

--- a/solution.py
+++ b/solution.py
@@ -194,8 +194,8 @@
     here = lax.axis_index("ctx")
     rows = out[0].shape[0]
     copies = [
-        pltpu.make_async_copy(source.at[place(here ^ k, rows), :], ref, sems.at[k])
-        for k, ref in zip(offsets(len(out)), out)
+        pltpu.make_async_copy(source.at[place(here ^ k, rows), :], ref, sems.at[k - 1])
+        for k, ref in zip(offsets(len(out) + 1)[1:], out)
     ]
     for copy in copies:
         copy.start()
@@ -223,7 +223,10 @@
     out = refs[parts + 5 : 2 * parts + 5]
     spec_conv, whole = refs[2 * parts + 5 :]
     here = lax.axis_index("ctx")
-    gather_tokens(conv, whole, here)
+    step = conv[1].shape[1]
+    whole[:, place(here, step)] = conv[0][place(here, whole.shape[0]), :]
+    for k, piece in zip(offsets(parts)[1:], conv[1:]):
+        whole[:, place(here ^ k, step)] = piece[...]
     spec_conv[...] = spectrum_of(whole[...], fwd_hi, fwd_lo)
     product = spectrum_product(spec_filt[...], spec_conv[...], False)
     whole[...] = inverse_dense(product, inv_hi, inv_lo).astype(jnp.bfloat16)
@@ -343,14 +346,14 @@
     grad_2 = swap(grad_rows, "tp", groups, 2)
     blocks = call(
         blocks_kernel,
-        [shape((chans, tokens), bf16)] * parts,
+        [shape((chans, tokens), bf16)] * (parts - 1),
         [conv_local],
-        [pltpu.SemaphoreType.DMA((parts,))],
+        [pltpu.SemaphoreType.DMA((parts - 1,))],
         far=(0,),
         cost=10.0,
     )
-    conv_pieces = exchange(blocks, offsets(parts))
-    cut = width // 16 * 5
+    conv_pieces = exchange(blocks, offsets(parts)[1:])
+    cut = width // 32 * 11
     grad_3a = swap(grad_1[:, :cut], "tp", groups, 2)
     grad_3b = swap(grad_2[:, cut:], "tp", groups, 1)
 
@@ -366,7 +369,7 @@
     *conv_out, spec_conv = call(
         functools.partial(conv_kernel, parts),
         [piece] * parts + [spectrum],
-        [*conv_pieces, spec_filt, *tables],
+        [conv_local, *conv_pieces, spec_filt, *tables],
         [whole],
         cost=2.0,
     )

time: 39.5 us -> 39.4 us (level)
  no operation moved by 1% of the time
where the time goes in v4:
time: 39.4 us; the launch traced here: 39.3 us
  starting transfers between devices  24.8 us (63%)
  Pallas kernels  10.8 us (27%)
  waiting for transfers between devices  2.82 us (7%)
  between operations  0.84 us (2%)
    ppermute x18, starting transfers between devices, swap(): return lax.ppermute(value, axis, [(i, i ^ k) for i in range(size)])  24.8 us
    pallas_call x9, Pallas kernels, call(): pl.pallas_call(kernel, out_shape=outs, in_specs=[hbm if i in far else vme...  10.8 us
    ppermute x18, waiting for transfers between devices, swap(): return lax.ppermute(value, axis, [(i, i ^ k) for i in range(size)])  2.82 us
  transfers between devices with their start and end apart: 18, of which 5 were waited for; matrix products, arithmetic and copies ran while one was open for 0% of the time, Pallas kernels for 21%

profile of v4, /device:TPU:0, one launch (start us, length us, event | category | flops | bytes accessed | tf_op | source)
XLA Modules:
  0.0 39.3 jit_solution(4071044149264116651)
XLA Ops:
  0.6 3.0 %collective-permute-start.4 = (bf16[32,4096]{1,0:T(8,128)(2,1)}, bf16[32,4096]{1,0:T(8,128)(2,1)S(1)}, u32[]{:S(2)}, u32[]{:S(2)}) collective-permute-start(bf16[32,4096]{1,0:T(8,128)(2,1)} %bitcast.9), channel_id=1, source_target_pairs={{0,4},{2,6},{4,0},{6,2},{1,5},{3,7},{5,1},{7,3},{8,12},{10,14},{12... | collective-permute-start | bytes 786440 | tf_op jit(solution)/shard_map/ppermute | solution.py:340
  3.7 1.5 %collective-permute-start.3 = (bf16[32,4096]{1,0:T(8,128)(2,1)}, bf16[32,4096]{1,0:T(8,128)(2,1)S(1)}, u32[]{:S(2)}, u32[]{:S(2)}) collective-permute-start(bf16[32,4096]{1,0:T(8,128)(2,1)} %bitcast.10), channel_id=1, source_target_pairs={{0,2},{2,0},{4,6},{6,4},{1,3},{3,1},{5,7},{7,5},{8,10},{10,8},{12,... | collective-permute-start | bytes 786440 | tf_op jit(solution)/shard_map/ppermute | solution.py:340
  5.2 1.1 %shard_map.112 = (bf16[256,128]{1,0:T(8,128)(2,1)S(1)}, bf16[256,128]{1,0:T(8,128)(2,1)S(1)}, bf16[256,128]{1,0:T(8,128)(2,1)S(1)}) custom-call(bf16[1024,128]{1,0:T(8,128)(2,1)} %bitcast.12), custom_call_target="tpu_custom_call" | custom-call | flops 10000000000 | bytes 10000000 | tf_op jit(solution)/shard_map/pallas_call | solution.py:316
  6.3 3.7 %collective-permute-start = (bf16[256,128]{1,0:T(8,128)(2,1)S(1)}, bf16[256,128]{1,0:T(8,128)(2,1)S(1)}, u32[]{:S(2)}, u32[]{:S(2)}) collective-permute-start(bf16[256,128]{1,0:T(8,128)(2,1)S(1)} %get-tuple-element.35), channel_id=1, source_target_pairs={{0,24},{8,16},{16,8},{24,0},{1,25},{9,17},{17,9},{25,1},{2,26},{10... | collective-permute-start | bytes 196616 | tf_op jit(solution)/shard_map/ppermute | solution.py:340
  10.0 0.8 %collective-permute-start.2 = (bf16[256,128]{1,0:T(8,128)(2,1)S(1)}, bf16[256,128]{1,0:T(8,128)(2,1)S(1)}, u32[]{:S(2)}, u32[]{:S(2)}) collective-permute-start(bf16[256,128]{1,0:T(8,128)(2,1)S(1)} %get-tuple-element.37), channel_id=1, source_target_pairs={{0,8},{8,0},{16,24},{24,16},{1,9},{9,1},{17,25},{25,17},{2,10},{10... | collective-permute-start | bytes 196616 | tf_op jit(solution)/shard_map/ppermute | solution.py:340
  10.8 1.2 %collective-permute-start.6 = (bf16[32,2688]{1,0:T(8,128)(2,1)S(1)}, bf16[32,2688]{1,0:T(8,128)(2,1)S(1)}, u32[]{:S(2)}, u32[]{:S(2)}) collective-permute-start(bf16[32,2688]{1,0:T(8,128)(2,1)S(1)} %slice.9), channel_id=1, source_target_pairs={{0,2},{2,0},{4,6},{6,4},{1,3},{3,1},{5,7},{7,5},{8,10},{10,8},{12,... | collective-permute-start | bytes 516104 | tf_op jit(solution)/shard_map/ppermute | solution.py:340
  12.0 1.6 %collective-permute-start.5 = (bf16[32,1408]{1,0:T(8,128)(2,1)S(1)}, bf16[32,1408]{1,0:T(8,128)(2,1)S(1)}, u32[]{:S(2)}, u32[]{:S(2)}) collective-permute-start(bf16[32,1408]{1,0:T(8,128)(2,1)S(1)} %slice.8), channel_id=1, source_target_pairs={{0,4},{2,6},{4,0},{6,2},{1,5},{3,7},{5,1},{7,3},{8,12},{10,14},{12... | collective-permute-start | bytes 270344 | tf_op jit(solution)/shard_map/ppermute | solution.py:340
  13.6 1.0 %shard_map.113.refs_4_ = f32[256,1024]{1,0:T(8,128)S(1)} custom-call(f32[256,512]{1,0:T(8,128)S(1)} %copy-done.6, bf16[512,1024]{1,0:T(8,128)(2,1)S(1)} %copy-done.4, bf16[512,1024]{1,0:T(8,128)(2,1)S(1)} %copy-done.3, bf16[32,4096]{1,0:T(8,128)(2,1)S(1)} %collective-permute-done.3.after_1.refs_1_, bf16[32,4096]{1,0:T(8,128)(2,1)S(1)} %collective-permute-done.4.after_2.refs_2_), custom_call_target="tpu_custom_call" | custom-call | flops 2000000000 | bytes 2000000 | tf_op jit(solution)/shard_map/pallas_call | solution.py:316
  14.6 0.7 %collective-permute-done.1.refs_2_ = bf16[256,128]{1,0:T(8,128)(2,1)S(1)} collective-permute-done((bf16[256,128]{1,0:T(8,128)(2,1)S(1)}, bf16[256,128]{1,0:T(8,128)(2,1)S(1)}, u32[]{:S(2)}, u32[]{:S(2)}) %collective-permute-start.1) | collective-permute-done | bytes 65568 | tf_op jit(solution)/shard_map/ppermute | solution.py:340
  15.3 1.7 %shard_map.114 = (bf16[256,128]{1,0:T(8,128)(2,1)S(1)}, bf16[256,128]{1,0:T(8,128)(2,1)S(1)}, bf16[256,128]{1,0:T(8,128)(2,1)S(1)}, bf16[256,128]{1,0:T(8,128)(2,1)S(1)}, f32[256,1024]{1,0:T(8,128)S(1)}) custom-call(bf16[1024,128]{1,0:T(8,128)(2,1)S(1)} %bitcast.13, bf16[256,128]{1,0:T(8,128)(2,1)S(1)} %collective-permute-done.refs_1_, ...), custom_call_target="tpu_custom_call" | custom-call | flops 2000000000 | bytes 2000000 | tf_op jit(solution)/shard_map/pallas_call | solution.py:316
  17.1 1.9 %shard_map.115 = (f32[256,128]{1,0:T(8,128)S(1)}, f32[256,128]{1,0:T(8,128)S(1)}, f32[256,128]{1,0:T(8,128)S(1)}, bf16[256,128]{1,0:T(8,128)(2,1)S(1)}, bf16[256...) custom-call(bf16[256,128]{1,0:T(8,128)(2,1)S(1)} %get-tuple-element.48.after.refs_4_.refs_0_, ...), custom_call_target="tpu_custom_call" | custom-call | flops 1000000000 | bytes 1000000 | tf_op jit(solution)/shard_map/pallas_call | solution.py:316
  19.0 3.2 %collective-permute-start.10 = (bf16[256,128]{1,0:T(8,128)(2,1)S(1)}, bf16[256,128]{1,0:T(8,128)(2,1)S(1)}, u32[]{:S(2)}, u32[]{:S(2)}) collective-permute-start(bf16[256,128]{1,0:T(8,128)(2,1)S(1)} %get-tuple-element.53), channel_id=1, source_target_pairs={{0,24},{8,16},{16,8},{24,0},{1,25},{9,17},{17,9},{25,1},{2,26},{10... | collective-permute-start | bytes 196616 | tf_op jit(solution)/shard_map/ppermute | solution.py:340
  22.2 1.2 %collective-permute-start.12 = (bf16[256,128]{1,0:T(8,128)(2,1)S(1)}, bf16[256,128]{1,0:T(8,128)(2,1)S(1)}, u32[]{:S(2)}, u32[]{:S(2)}) collective-permute-start(bf16[256,128]{1,0:T(8,128)(2,1)S(1)} %get-tuple-element.55), channel_id=1, source_target_pairs={{0,8},{8,0},{16,24},{24,16},{1,9},{9,1},{17,25},{25,17},{2,10},{10... | collective-permute-start | bytes 196616 | tf_op jit(solution)/shard_map/ppermute | solution.py:340
  23.4 0.7 %shard_map.116 = (f32[256,128]{1,0:T(8,128)S(1)}, bf16[256,128]{1,0:T(8,128)(2,1)S(1)}) custom-call(bf16[1024,4096]{1,0:T(8,128)(2,1)S(1)} %bitcast.6, bf16[1024,128]{1,0:T(8,128)(2,1)S(1)} %bitcast.8, bf16[128,4096]{1,0:T(8,128)(2,1)S(1)} %get-tuple-element.39.rows_all), custom_call_target="tpu_custom_call" | custom-call | flops 1000000000 | bytes 1000000 | tf_op jit(solution)/shard_map/pallas_call | solution.py:316
  24.1 0.9 %collective-permute-start.7 = (bf16[256,128]{1,0:T(8,128)(2,1)S(1)}, bf16[256,128]{1,0:T(8,128)(2,1)S(1)}, u32[]{:S(2)}, u32[]{:S(2)}) collective-permute-start(bf16[256,128]{1,0:T(8,128)(2,1)S(1)} %get-tuple-element.49), channel_id=1, source_target_pairs={{0,8},{8,0},{16,24},{24,16},{1,9},{9,1},{17,25},{25,17},{2,10},{10... | collective-permute-start | bytes 196616 | tf_op jit(solution)/shard_map/ppermute | solution.py:340
  25.0 2.9 %collective-permute-start.8 = (bf16[256,128]{1,0:T(8,128)(2,1)S(1)}, bf16[256,128]{1,0:T(8,128)(2,1)S(1)}, u32[]{:S(2)}, u32[]{:S(2)}) collective-permute-start(bf16[256,128]{1,0:T(8,128)(2,1)S(1)} %get-tuple-element.50), channel_id=1, source_target_pairs={{0,16},{8,24},{16,0},{24,8},{1,17},{9,25},{17,1},{25,9},{2,18},{10... | collective-permute-start | bytes 196616 | tf_op jit(solution)/shard_map/ppermute | solution.py:340
  27.9 0.7 %collective-permute-start.9 = (bf16[256,128]{1,0:T(8,128)(2,1)S(1)}, bf16[256,128]{1,0:T(8,128)(2,1)S(1)}, u32[]{:S(2)}, u32[]{:S(2)}) collective-permute-start(bf16[256,128]{1,0:T(8,128)(2,1)S(1)} %get-tuple-element.51), channel_id=1, source_target_pairs={{0,24},{8,16},{16,8},{24,0},{1,25},{9,17},{17,9},{25,1},{2,26},{10... | collective-permute-start | bytes 196616 | tf_op jit(solution)/shard_map/ppermute | solution.py:340
  29.0 1.7 %shard_map.118 = (bf16[256,128]{1,0:T(8,128)(2,1)S(1)}, bf16[256,128]{1,0:T(8,128)(2,1)S(1)}, bf16[256,128]{1,0:T(8,128)(2,1)S(1)}, bf16[256,128]{1,0:T(8,128)(2,1)S(1)}, f32[256,1024]{1,0:T(8,128)S(1)}) custom-call(bf16[256,128]{1,0:T(8,128)(2,1)S(1)} %get-tuple-element.52.refs_0_, bf16[256,128]{1,0:T(8,128)(2,1)S(1)} %collective-permute-done.10.refs_1_, ...), custom_call_target="tpu_custom_call" | custom-call | flops 1000000000 | bytes 1000000 | tf_op jit(solution)/shard_map/pallas_call | solution.py:316
  31.3 2.4 %collective-permute-start.14 = (bf16[256,128]{1,0:T(8,128)(2,1)S(1)}, bf16[256,128]{1,0:T(8,128)(2,1)S(1)}, u32[]{:S(2)}, u32[]{:S(2)}) collective-permute-start(bf16[256,128]{1,0:T(8,128)(2,1)S(1)} %get-tuple-element.58), channel_id=1, source_target_pairs={{0,24},{8,16},{16,8},{24,0},{1,25},{9,17},{17,9},{25,1},{2,26},{10... | collective-permute-start | bytes 196616 | tf_op jit(solution)/shard_map/ppermute | solution.py:340
  33.6 0.7 %collective-permute-start.15 = (bf16[256,128]{1,0:T(8,128)(2,1)S(1)}, bf16[256,128]{1,0:T(8,128)(2,1)S(1)}, u32[]{:S(2)}, u32[]{:S(2)}) collective-permute-start(bf16[256,128]{1,0:T(8,128)(2,1)S(1)} %get-tuple-element.59), channel_id=1, source_target_pairs={{0,8},{8,0},{16,24},{24,16},{1,9},{9,1},{17,25},{25,17},{2,10},{10... | collective-permute-start | bytes 196616 | tf_op jit(solution)/shard_map/ppermute | solution.py:340
  34.4 1.1 %shard_map.119 = (f32[128,512]{1,0:T(8,128)S(1)}, bf16[64,512]{1,0:T(8,128)(2,1)S(1)}, bf16[64,512]{1,0:T(8,128)(2,1)S(1)}) custom-call(f32[256,1024]{1,0:T(8,128)S(1)} %get-tuple-element.60.spec_conv, f32[256,1024]{1,0:T(8,128)S(1)} %get-tuple-element.61.spec_gate, bf16[1024,512]{1,0:T(8,128)(2,1)S(1)} %copy-done.2, bf16[1024,512]{1,0:T(8,128)(2,1)S(1)} %copy-done.1, ...), custom_call_target="tpu_custom_call" | custom-call | flops 2000000000 | bytes 2000000 | tf_op jit(solution)/shard_map/pallas_call | solution.py:316
  36.1 0.7 %shard_map.117 = bf16[1024,128]{1,0:T(8,128)(2,1)} custom-call(f32[256,128]{1,0:T(8,128)S(1)} %get-tuple-element.40.refs_0_, f32[256,128]{1,0:T(8,128)S(1)} %get-tuple-element.41.refs_1_, f32[256,128]{1,0:T(8,128)S(1)} %get-tuple-element.42.refs_2_, f32[256,128]{1,0:T(8,128)S(1)} %get-tuple-element.43.refs_3_, ...), custom_call_target="tpu_custom_call" | custom-call | flops 1000000000 | bytes 1000000 | tf_op jit(solution)/shard_map/pallas_call | solution.py:316
  36.9 0.9 %collective-permute-done.13.refs_1_ = bf16[256,128]{1,0:T(8,128)(2,1)S(1)} collective-permute-done((bf16[256,128]{1,0:T(8,128)(2,1)S(1)}, bf16[256,128]{1,0:T(8,128)(2,1)S(1)}, u32[]{:S(2)}, u32[]{:S(2)}) %collective-permute-start.13) | collective-permute-done | bytes 65568 | tf_op jit(solution)/shard_map/ppermute | solution.py:340
  38.5 0.8 %shard_map.120 = (f32[128,512]{1,0:T(8,128)}, bf16[1024,128]{1,0:T(8,128)(2,1)}) custom-call(bf16[256,128]{1,0:T(8,128)(2,1)S(1)} %get-tuple-element.56.refs_0_, bf16[256,128]{1,0:T(8,128)(2,1)S(1)} %collective-permute-done.13.refs_1_, bf16[256,128]{1,0:T(8,128)(2,1)S(1)} %collective-permute-done.14.refs_2_, ...), custom_call_target="tpu_custom_call" | custom-call | flops 1000000000 | bytes 1000000 | tf_op jit(solution)/shard_map/pallas_call | solution.py:316
  (44 shorter events, 2.4 us)
Async XLA Ops:
  0.6 10.2 %collective-permute-start.4 = (bf16[32,4096]{1,0:T(8,128)(2,1)}, bf16[32,4096]{1,0:T(8,128)(2,1)S(1)}, u32[]{:S(2)}, u32[]{:S(2)}) collective-permute-start(bf16[32,4096]{1,0:T(8,128)(2,1)} %bitcast.9), channel_id=1, source_target_pairs={{0,4},{2,6},{4,0},{6,2},{1,5},{3,7},{5,1},{7,3},{8,12},{10,14},{12... | collective-permute-start | bytes 786440 | tf_op jit(solution)/shard_map/ppermute | solution.py:340
  3.7 8.3 %collective-permute-start.3 = (bf16[32,4096]{1,0:T(8,128)(2,1)}, bf16[32,4096]{1,0:T(8,128)(2,1)S(1)}, u32[]{:S(2)}, u32[]{:S(2)}) collective-permute-start(bf16[32,4096]{1,0:T(8,128)(2,1)} %bitcast.10), channel_id=1, source_target_pairs={{0,2},{2,0},{4,6},{6,4},{1,3},{3,1},{5,7},{7,5},{8,10},{10,8},{12,... | collective-permute-start | bytes 786440 | tf_op jit(solution)/shard_map/ppermute | solution.py:340
  5.2 10.1 %copy-start.1 = (bf16[1024,512]{1,0:T(8,128)(2,1)S(1)}, bf16[1024,512]{1,0:T(8,128)(2,1)}, u32[]{:S(2)}) copy-start(bf16[1024,512]{1,0:T(8,128)(2,1)} %constant.11.clone.refs_8_.inv_lo) | copy-start | bytes 3145732
  5.2 10.1 %copy-start.2 = (bf16[1024,512]{1,0:T(8,128)(2,1)S(1)}, bf16[1024,512]{1,0:T(8,128)(2,1)}, u32[]{:S(2)}) copy-start(bf16[1024,512]{1,0:T(8,128)(2,1)} %constant.10.clone.refs_7_.inv_hi) | copy-start | bytes 3145732
  5.2 10.1 %copy-start.7 = (bf16[1,1024,128]{2,1,0:T(8,128)(2,1)S(1)}, bf16[1,1024,128]{2,1,0:T(8,128)(2,1)}, u32[]{:S(2)}) copy-start(bf16[1,1024,128]{2,1,0:T(8,128)(2,1)} %param.11) | copy-start | bytes 786436
  6.3 10.7 %slice-start = ((s8[8388608]{0:T(1024)(128)(4,1)}), s8[4194304]{0:T(1024)(128)(4,1)S(1)}, s32[]{:S(2)}) async-start(s8[8388608]{0:T(1024)(128)(4,1)} %bitcast.5), calls=%async_computation | async-start | bytes 8388608
  6.3 10.7 %copy-start = (bf16[1,1024,128]{2,1,0:T(8,128)(2,1)S(1)}, bf16[1,1024,128]{2,1,0:T(8,128)(2,1)}, u32[]{:S(2)}) copy-start(bf16[1,1024,128]{2,1,0:T(8,128)(2,1)} %param.10) | copy-start | bytes 786436
  6.3 10.7 %copy-start.5 = (bf16[1,32,4096]{2,1,0:T(8,128)(2,1)S(1)}, bf16[1,32,4096]{2,1,0:T(8,128)(2,1)}, u32[]{:S(2)}) copy-start(bf16[1,32,4096]{2,1,0:T(8,128)(2,1)} %param.9) | copy-start | bytes 786436
  6.3 8.3 %collective-permute-start = (bf16[256,128]{1,0:T(8,128)(2,1)S(1)}, bf16[256,128]{1,0:T(8,128)(2,1)S(1)}, u32[]{:S(2)}, u32[]{:S(2)}) collective-permute-start(bf16[256,128]{1,0:T(8,128)(2,1)S(1)} %get-tuple-element.35), channel_id=1, source_target_pairs={{0,24},{8,16},{16,8},{24,0},{1,25},{9,17},{17,9},{25,1},{2,26},{10... | collective-permute-start | bytes 196616 | tf_op jit(solution)/shard_map/ppermute | solution.py:340
  10.0 5.2 %collective-permute-start.1 = (bf16[256,128]{1,0:T(8,128)(2,1)S(1)}, bf16[256,128]{1,0:T(8,128)(2,1)S(1)}, u32[]{:S(2)}, u32[]{:S(2)}) collective-permute-start(bf16[256,128]{1,0:T(8,128)(2,1)S(1)} %get-tuple-element.36), channel_id=1, source_target_pairs={{0,16},{8,24},{16,0},{24,8},{1,17},{9,25},{17,1},{25,9},{2,18},{10... | collective-permute-start | bytes 196616 | tf_op jit(solution)/shard_map/ppermute | solution.py:340
  10.0 5.2 %collective-permute-start.2 = (bf16[256,128]{1,0:T(8,128)(2,1)S(1)}, bf16[256,128]{1,0:T(8,128)(2,1)S(1)}, u32[]{:S(2)}, u32[]{:S(2)}) collective-permute-start(bf16[256,128]{1,0:T(8,128)(2,1)S(1)} %get-tuple-element.37), channel_id=1, source_target_pairs={{0,8},{8,0},{16,24},{24,16},{1,9},{9,1},{17,25},{25,17},{2,10},{10... | collective-permute-start | bytes 196616 | tf_op jit(solution)/shard_map/ppermute | solution.py:340
  10.8 6.2 %collective-permute-start.6 = (bf16[32,2688]{1,0:T(8,128)(2,1)S(1)}, bf16[32,2688]{1,0:T(8,128)(2,1)S(1)}, u32[]{:S(2)}, u32[]{:S(2)}) collective-permute-start(bf16[32,2688]{1,0:T(8,128)(2,1)S(1)} %slice.9), channel_id=1, source_target_pairs={{0,2},{2,0},{4,6},{6,4},{1,3},{3,1},{5,7},{7,5},{8,10},{10,8},{12,... | collective-permute-start | bytes 516104 | tf_op jit(solution)/shard_map/ppermute | solution.py:340
  12.0 5.0 %collective-permute-start.5 = (bf16[32,1408]{1,0:T(8,128)(2,1)S(1)}, bf16[32,1408]{1,0:T(8,128)(2,1)S(1)}, u32[]{:S(2)}, u32[]{:S(2)}) collective-permute-start(bf16[32,1408]{1,0:T(8,128)(2,1)S(1)} %slice.8), channel_id=1, source_target_pairs={{0,4},{2,6},{4,0},{6,2},{1,5},{3,7},{5,1},{7,3},{8,12},{10,14},{12... | collective-permute-start | bytes 270344 | tf_op jit(solution)/shard_map/ppermute | solution.py:340
  19.0 9.0 %collective-permute-start.10 = (bf16[256,128]{1,0:T(8,128)(2,1)S(1)}, bf16[256,128]{1,0:T(8,128)(2,1)S(1)}, u32[]{:S(2)}, u32[]{:S(2)}) collective-permute-start(bf16[256,128]{1,0:T(8,128)(2,1)S(1)} %get-tuple-element.53), channel_id=1, source_target_pairs={{0,24},{8,16},{16,8},{24,0},{1,25},{9,17},{17,9},{25,1},{2,26},{10... | collective-permute-start | bytes 196616 | tf_op jit(solution)/shard_map/ppermute | solution.py:340
  22.2 6.8 %collective-permute-start.11 = (bf16[256,128]{1,0:T(8,128)(2,1)S(1)}, bf16[256,128]{1,0:T(8,128)(2,1)S(1)}, u32[]{:S(2)}, u32[]{:S(2)}) collective-permute-start(bf16[256,128]{1,0:T(8,128)(2,1)S(1)} %get-tuple-element.54), channel_id=1, source_target_pairs={{0,16},{8,24},{16,0},{24,8},{1,17},{9,25},{17,1},{25,9},{2,18},{10... | collective-permute-start | bytes 196616 | tf_op jit(solution)/shard_map/ppermute | solution.py:340
  22.2 6.8 %collective-permute-start.12 = (bf16[256,128]{1,0:T(8,128)(2,1)S(1)}, bf16[256,128]{1,0:T(8,128)(2,1)S(1)}, u32[]{:S(2)}, u32[]{:S(2)}) collective-permute-start(bf16[256,128]{1,0:T(8,128)(2,1)S(1)} %get-tuple-element.55), channel_id=1, source_target_pairs={{0,8},{8,0},{16,24},{24,16},{1,9},{9,1},{17,25},{25,17},{2,10},{10... | collective-permute-start | bytes 196616 | tf_op jit(solution)/shard_map/ppermute | solution.py:340
  24.1 9.5 %collective-permute-start.7 = (bf16[256,128]{1,0:T(8,128)(2,1)S(1)}, bf16[256,128]{1,0:T(8,128)(2,1)S(1)}, u32[]{:S(2)}, u32[]{:S(2)}) collective-permute-start(bf16[256,128]{1,0:T(8,128)(2,1)S(1)} %get-tuple-element.49), channel_id=1, source_target_pairs={{0,8},{8,0},{16,24},{24,16},{1,9},{9,1},{17,25},{25,17},{2,10},{10... | collective-permute-start | bytes 196616 | tf_op jit(solution)/shard_map/ppermute | solution.py:340
  25.0 9.3 %collective-permute-start.8 = (bf16[256,128]{1,0:T(8,128)(2,1)S(1)}, bf16[256,128]{1,0:T(8,128)(2,1)S(1)}, u32[]{:S(2)}, u32[]{:S(2)}) collective-permute-start(bf16[256,128]{1,0:T(8,128)(2,1)S(1)} %get-tuple-element.50), channel_id=1, source_target_pairs={{0,16},{8,24},{16,0},{24,8},{1,17},{9,25},{17,1},{25,9},{2,18},{10... | collective-permute-start | bytes 196616 | tf_op jit(solution)/shard_map/ppermute | solution.py:340
  27.9 6.5 %collective-permute-start.9 = (bf16[256,128]{1,0:T(8,128)(2,1)S(1)}, bf16[256,128]{1,0:T(8,128)(2,1)S(1)}, u32[]{:S(2)}, u32[]{:S(2)}) collective-permute-start(bf16[256,128]{1,0:T(8,128)(2,1)S(1)} %get-tuple-element.51), channel_id=1, source_target_pairs={{0,24},{8,16},{16,8},{24,0},{1,25},{9,17},{17,9},{25,1},{2,26},{10... | collective-permute-start | bytes 196616 | tf_op jit(solution)/shard_map/ppermute | solution.py:340
  30.7 7.1 %collective-permute-start.13 = (bf16[256,128]{1,0:T(8,128)(2,1)S(1)}, bf16[256,128]{1,0:T(8,128)(2,1)S(1)}, u32[]{:S(2)}, u32[]{:S(2)}) collective-permute-start(bf16[256,128]{1,0:T(8,128)(2,1)S(1)} %get-tuple-element.57), channel_id=1, source_target_pairs={{0,16},{8,24},{16,0},{24,8},{1,17},{9,25},{17,1},{25,9},{2,18},{10... | collective-permute-start | bytes 196616 | tf_op jit(solution)/shard_map/ppermute | solution.py:340
  31.3 6.5 %collective-permute-start.14 = (bf16[256,128]{1,0:T(8,128)(2,1)S(1)}, bf16[256,128]{1,0:T(8,128)(2,1)S(1)}, u32[]{:S(2)}, u32[]{:S(2)}) collective-permute-start(bf16[256,128]{1,0:T(8,128)(2,1)S(1)} %get-tuple-element.58), channel_id=1, source_target_pairs={{0,24},{8,16},{16,8},{24,0},{1,25},{9,17},{17,9},{25,1},{2,26},{10... | collective-permute-start | bytes 196616 | tf_op jit(solution)/shard_map/ppermute | solution.py:340
  33.6 4.8 %collective-permute-start.15 = (bf16[256,128]{1,0:T(8,128)(2,1)S(1)}, bf16[256,128]{1,0:T(8,128)(2,1)S(1)}, u32[]{:S(2)}, u32[]{:S(2)}) collective-permute-start(bf16[256,128]{1,0:T(8,128)(2,1)S(1)} %get-tuple-element.59), channel_id=1, source_target_pairs={{0,8},{8,0},{16,24},{24,16},{1,9},{9,1},{17,25},{25,17},{2,10},{10... | collective-permute-start | bytes 196616 | tf_op jit(solution)/shard_map/ppermute | solution.py:340
  35.6 2.9 %collective-permute-start.16 = (bf16[64,512]{1,0:T(8,128)(2,1)S(1)}, bf16[64,512]{1,0:T(8,128)(2,1)S(1)}, u32[]{:S(2)}, u32[]{:S(2)}) collective-permute-start(bf16[64,512]{1,0:T(8,128)(2,1)S(1)} %get-tuple-element.62), channel_id=1, source_target_pairs={{0,1},{1,0},{2,3},{3,2},{4,5},{5,4},{6,7},{7,6},{8,9},{9,8},{10,11... | collective-permute-start | bytes 196616 | tf_op jit(solution)/shard_map/ppermute | solution.py:340
  35.6 2.8 %collective-permute-start.17 = (bf16[64,512]{1,0:T(8,128)(2,1)S(1)}, bf16[64,512]{1,0:T(8,128)(2,1)S(1)}, u32[]{:S(2)}, u32[]{:S(2)}) collective-permute-start(bf16[64,512]{1,0:T(8,128)(2,1)S(1)} %get-tuple-element.63), channel_id=1, source_target_pairs={{0,1},{1,0},{2,3},{3,2},{4,5},{5,4},{6,7},{7,6},{8,9},{9,8},{10,11... | collective-permute-start | bytes 196616 | tf_op jit(solution)/shard_map/ppermute | solution.py:340
  (4 other events, 30.4 us)

commit v5 on v4

--- a/solution.py
+++ b/solution.py
@@ -274,7 +274,7 @@
 
 
 def filter_kernel(parts, scale, spec_conv, spec_gate, inv_hi, inv_lo, *refs):
-    keep, *send, whole = refs[parts:]
+    keep, *send, whole = refs[parts - 2 :]
     product = spectrum_product(spec_conv[...], spec_gate[...], True)
     whole[...] = inverse_dense(product, inv_hi, inv_lo) * scale
     rows = keep.shape[0]
@@ -408,7 +408,7 @@
     keep, send_low, send_high = call(
         functools.partial(filter_kernel, parts, scale),
         [half, quarter, quarter],
-        [spec_conv, spec_gate, *tables[2:], *conv_back],
+        [spec_conv, spec_gate, *tables[2:], *conv_back[1:-1]],
         [pltpu.VMEM((chans, length), f32)],
         cost=2.0,
     )

time: 39.4 us -> 39.4 us (level)
  transfers between devices with their start and end apart: 18 -> 18, of which waited for: 5 -> 4; matrix products, arithmetic and copies ran while one was open for 0% -> 0% of each run, Pallas kernels for 21% -> 21%
where the time goes in v5:
time: 39.4 us; the launch traced here: 39.3 us
  starting transfers between devices  24.8 us (63%)
  Pallas kernels  10.8 us (27%)
  waiting for transfers between devices  2.82 us (7%)
  between operations  0.85 us (2%)
    ppermute x18, starting transfers between devices, swap(): return lax.ppermute(value, axis, [(i, i ^ k) for i in range(size)])  24.8 us
    pallas_call x9, Pallas kernels, call(): pl.pallas_call(kernel, out_shape=outs, in_specs=[hbm if i in far else vme...  10.8 us
    ppermute x18, waiting for transfers between devices, swap(): return lax.ppermute(value, axis, [(i, i ^ k) for i in range(size)])  2.82 us
  transfers between devices with their start and end apart: 18, of which 4 were waited for; matrix products, arithmetic and copies ran while one was open for 0% of the time, Pallas kernels for 21%

profile of v5, /device:TPU:0, one launch (start us, length us, event | category | flops | bytes accessed | tf_op | source)
XLA Modules:
  0.0 39.3 jit_solution(2195026404808356895)
XLA Ops:
  0.6 3.0 %collective-permute-start.4 = (bf16[32,4096]{1,0:T(8,128)(2,1)}, bf16[32,4096]{1,0:T(8,128)(2,1)S(1)}, u32[]{:S(2)}, u32[]{:S(2)}) collective-permute-start(bf16[32,4096]{1,0:T(8,128)(2,1)} %bitcast.9), channel_id=1, source_target_pairs={{0,4},{2,6},{4,0},{6,2},{1,5},{3,7},{5,1},{7,3},{8,12},{10,14},{12... | collective-permute-start | bytes 786440 | tf_op jit(solution)/shard_map/ppermute | solution.py:340
  3.7 1.5 %collective-permute-start.3 = (bf16[32,4096]{1,0:T(8,128)(2,1)}, bf16[32,4096]{1,0:T(8,128)(2,1)S(1)}, u32[]{:S(2)}, u32[]{:S(2)}) collective-permute-start(bf16[32,4096]{1,0:T(8,128)(2,1)} %bitcast.10), channel_id=1, source_target_pairs={{0,2},{2,0},{4,6},{6,4},{1,3},{3,1},{5,7},{7,5},{8,10},{10,8},{12,... | collective-permute-start | bytes 786440 | tf_op jit(solution)/shard_map/ppermute | solution.py:340
  5.2 1.1 %shard_map.112 = (bf16[256,128]{1,0:T(8,128)(2,1)S(1)}, bf16[256,128]{1,0:T(8,128)(2,1)S(1)}, bf16[256,128]{1,0:T(8,128)(2,1)S(1)}) custom-call(bf16[1024,128]{1,0:T(8,128)(2,1)} %bitcast.12), custom_call_target="tpu_custom_call" | custom-call | flops 10000000000 | bytes 10000000 | tf_op jit(solution)/shard_map/pallas_call | solution.py:316
  6.3 3.7 %collective-permute-start = (bf16[256,128]{1,0:T(8,128)(2,1)S(1)}, bf16[256,128]{1,0:T(8,128)(2,1)S(1)}, u32[]{:S(2)}, u32[]{:S(2)}) collective-permute-start(bf16[256,128]{1,0:T(8,128)(2,1)S(1)} %get-tuple-element.35), channel_id=1, source_target_pairs={{0,24},{8,16},{16,8},{24,0},{1,25},{9,17},{17,9},{25,1},{2,26},{10... | collective-permute-start | bytes 196616 | tf_op jit(solution)/shard_map/ppermute | solution.py:340
  10.0 0.8 %collective-permute-start.2 = (bf16[256,128]{1,0:T(8,128)(2,1)S(1)}, bf16[256,128]{1,0:T(8,128)(2,1)S(1)}, u32[]{:S(2)}, u32[]{:S(2)}) collective-permute-start(bf16[256,128]{1,0:T(8,128)(2,1)S(1)} %get-tuple-element.37), channel_id=1, source_target_pairs={{0,8},{8,0},{16,24},{24,16},{1,9},{9,1},{17,25},{25,17},{2,10},{10... | collective-permute-start | bytes 196616 | tf_op jit(solution)/shard_map/ppermute | solution.py:340
  10.8 1.2 %collective-permute-start.6 = (bf16[32,2688]{1,0:T(8,128)(2,1)S(1)}, bf16[32,2688]{1,0:T(8,128)(2,1)S(1)}, u32[]{:S(2)}, u32[]{:S(2)}) collective-permute-start(bf16[32,2688]{1,0:T(8,128)(2,1)S(1)} %slice.9), channel_id=1, source_target_pairs={{0,2},{2,0},{4,6},{6,4},{1,3},{3,1},{5,7},{7,5},{8,10},{10,8},{12,... | collective-permute-start | bytes 516104 | tf_op jit(solution)/shard_map/ppermute | solution.py:340
  12.0 1.6 %collective-permute-start.5 = (bf16[32,1408]{1,0:T(8,128)(2,1)S(1)}, bf16[32,1408]{1,0:T(8,128)(2,1)S(1)}, u32[]{:S(2)}, u32[]{:S(2)}) collective-permute-start(bf16[32,1408]{1,0:T(8,128)(2,1)S(1)} %slice.8), channel_id=1, source_target_pairs={{0,4},{2,6},{4,0},{6,2},{1,5},{3,7},{5,1},{7,3},{8,12},{10,14},{12... | collective-permute-start | bytes 270344 | tf_op jit(solution)/shard_map/ppermute | solution.py:340
  13.6 1.0 %shard_map.113.refs_4_ = f32[256,1024]{1,0:T(8,128)S(1)} custom-call(f32[256,512]{1,0:T(8,128)S(1)} %copy-done.6, bf16[512,1024]{1,0:T(8,128)(2,1)S(1)} %copy-done.4, bf16[512,1024]{1,0:T(8,128)(2,1)S(1)} %copy-done.3, bf16[32,4096]{1,0:T(8,128)(2,1)S(1)} %collective-permute-done.3.after_1.refs_1_, bf16[32,4096]{1,0:T(8,128)(2,1)S(1)} %collective-permute-done.4.after_2.refs_2_), custom_call_target="tpu_custom_call" | custom-call | flops 2000000000 | bytes 2000000 | tf_op jit(solution)/shard_map/pallas_call | solution.py:316
  14.6 0.7 %collective-permute-done.1.refs_2_ = bf16[256,128]{1,0:T(8,128)(2,1)S(1)} collective-permute-done((bf16[256,128]{1,0:T(8,128)(2,1)S(1)}, bf16[256,128]{1,0:T(8,128)(2,1)S(1)}, u32[]{:S(2)}, u32[]{:S(2)}) %collective-permute-start.1) | collective-permute-done | bytes 65568 | tf_op jit(solution)/shard_map/ppermute | solution.py:340
  15.3 1.7 %shard_map.114 = (bf16[256,128]{1,0:T(8,128)(2,1)S(1)}, bf16[256,128]{1,0:T(8,128)(2,1)S(1)}, bf16[256,128]{1,0:T(8,128)(2,1)S(1)}, bf16[256,128]{1,0:T(8,128)(2,1)S(1)}, f32[256,1024]{1,0:T(8,128)S(1)}) custom-call(bf16[1024,128]{1,0:T(8,128)(2,1)S(1)} %bitcast.13, bf16[256,128]{1,0:T(8,128)(2,1)S(1)} %collective-permute-done.refs_1_, ...), custom_call_target="tpu_custom_call" | custom-call | flops 2000000000 | bytes 2000000 | tf_op jit(solution)/shard_map/pallas_call | solution.py:316
  17.1 1.9 %shard_map.115 = (f32[256,128]{1,0:T(8,128)S(1)}, f32[256,128]{1,0:T(8,128)S(1)}, f32[256,128]{1,0:T(8,128)S(1)}, bf16[256,128]{1,0:T(8,128)(2,1)S(1)}, bf16[256...) custom-call(bf16[256,128]{1,0:T(8,128)(2,1)S(1)} %get-tuple-element.48.after.refs_4_, ...), custom_call_target="tpu_custom_call" | custom-call | flops 1000000000 | bytes 1000000 | tf_op jit(solution)/shard_map/pallas_call | solution.py:316
  19.0 3.2 %collective-permute-start.10 = (bf16[256,128]{1,0:T(8,128)(2,1)S(1)}, bf16[256,128]{1,0:T(8,128)(2,1)S(1)}, u32[]{:S(2)}, u32[]{:S(2)}) collective-permute-start(bf16[256,128]{1,0:T(8,128)(2,1)S(1)} %get-tuple-element.53), channel_id=1, source_target_pairs={{0,24},{8,16},{16,8},{24,0},{1,25},{9,17},{17,9},{25,1},{2,26},{10... | collective-permute-start | bytes 196616 | tf_op jit(solution)/shard_map/ppermute | solution.py:340
  22.2 1.2 %collective-permute-start.12 = (bf16[256,128]{1,0:T(8,128)(2,1)S(1)}, bf16[256,128]{1,0:T(8,128)(2,1)S(1)}, u32[]{:S(2)}, u32[]{:S(2)}) collective-permute-start(bf16[256,128]{1,0:T(8,128)(2,1)S(1)} %get-tuple-element.55), channel_id=1, source_target_pairs={{0,8},{8,0},{16,24},{24,16},{1,9},{9,1},{17,25},{25,17},{2,10},{10... | collective-permute-start | bytes 196616 | tf_op jit(solution)/shard_map/ppermute | solution.py:340
  23.4 0.7 %shard_map.116 = (f32[256,128]{1,0:T(8,128)S(1)}, bf16[256,128]{1,0:T(8,128)(2,1)S(1)}) custom-call(bf16[1024,4096]{1,0:T(8,128)(2,1)S(1)} %bitcast.6, bf16[1024,128]{1,0:T(8,128)(2,1)S(1)} %bitcast.8, bf16[128,4096]{1,0:T(8,128)(2,1)S(1)} %get-tuple-element.39.rows_all), custom_call_target="tpu_custom_call" | custom-call | flops 1000000000 | bytes 1000000 | tf_op jit(solution)/shard_map/pallas_call | solution.py:316
  24.1 0.9 %collective-permute-start.7 = (bf16[256,128]{1,0:T(8,128)(2,1)S(1)}, bf16[256,128]{1,0:T(8,128)(2,1)S(1)}, u32[]{:S(2)}, u32[]{:S(2)}) collective-permute-start(bf16[256,128]{1,0:T(8,128)(2,1)S(1)} %get-tuple-element.49), channel_id=1, source_target_pairs={{0,8},{8,0},{16,24},{24,16},{1,9},{9,1},{17,25},{25,17},{2,10},{10... | collective-permute-start | bytes 196616 | tf_op jit(solution)/shard_map/ppermute | solution.py:340
  25.0 2.9 %collective-permute-start.8 = (bf16[256,128]{1,0:T(8,128)(2,1)S(1)}, bf16[256,128]{1,0:T(8,128)(2,1)S(1)}, u32[]{:S(2)}, u32[]{:S(2)}) collective-permute-start(bf16[256,128]{1,0:T(8,128)(2,1)S(1)} %get-tuple-element.50), channel_id=1, source_target_pairs={{0,16},{8,24},{16,0},{24,8},{1,17},{9,25},{17,1},{25,9},{2,18},{10... | collective-permute-start | bytes 196616 | tf_op jit(solution)/shard_map/ppermute | solution.py:340
  27.9 0.7 %collective-permute-start.9 = (bf16[256,128]{1,0:T(8,128)(2,1)S(1)}, bf16[256,128]{1,0:T(8,128)(2,1)S(1)}, u32[]{:S(2)}, u32[]{:S(2)}) collective-permute-start(bf16[256,128]{1,0:T(8,128)(2,1)S(1)} %get-tuple-element.51), channel_id=1, source_target_pairs={{0,24},{8,16},{16,8},{24,0},{1,25},{9,17},{17,9},{25,1},{2,26},{10... | collective-permute-start | bytes 196616 | tf_op jit(solution)/shard_map/ppermute | solution.py:340
  29.0 1.7 %shard_map.118 = (bf16[256,128]{1,0:T(8,128)(2,1)S(1)}, bf16[256,128]{1,0:T(8,128)(2,1)S(1)}, bf16[256,128]{1,0:T(8,128)(2,1)S(1)}, bf16[256,128]{1,0:T(8,128)(2,1)S(1)}, f32[256,1024]{1,0:T(8,128)S(1)}) custom-call(bf16[256,128]{1,0:T(8,128)(2,1)S(1)} %get-tuple-element.52.refs_0_, bf16[256,128]{1,0:T(8,128)(2,1)S(1)} %collective-permute-done.10.refs_1_, ...), custom_call_target="tpu_custom_call" | custom-call | flops 1000000000 | bytes 1000000 | tf_op jit(solution)/shard_map/pallas_call | solution.py:316
  31.3 2.4 %collective-permute-start.14 = (bf16[256,128]{1,0:T(8,128)(2,1)S(1)}, bf16[256,128]{1,0:T(8,128)(2,1)S(1)}, u32[]{:S(2)}, u32[]{:S(2)}) collective-permute-start(bf16[256,128]{1,0:T(8,128)(2,1)S(1)} %get-tuple-element.58), channel_id=1, source_target_pairs={{0,24},{8,16},{16,8},{24,0},{1,25},{9,17},{17,9},{25,1},{2,26},{10... | collective-permute-start | bytes 196616 | tf_op jit(solution)/shard_map/ppermute | solution.py:340
  33.6 0.7 %collective-permute-start.15 = (bf16[256,128]{1,0:T(8,128)(2,1)S(1)}, bf16[256,128]{1,0:T(8,128)(2,1)S(1)}, u32[]{:S(2)}, u32[]{:S(2)}) collective-permute-start(bf16[256,128]{1,0:T(8,128)(2,1)S(1)} %get-tuple-element.59), channel_id=1, source_target_pairs={{0,8},{8,0},{16,24},{24,16},{1,9},{9,1},{17,25},{25,17},{2,10},{10... | collective-permute-start | bytes 196616 | tf_op jit(solution)/shard_map/ppermute | solution.py:340
  34.3 1.1 %shard_map.119 = (f32[128,512]{1,0:T(8,128)S(1)}, bf16[64,512]{1,0:T(8,128)(2,1)S(1)}, bf16[64,512]{1,0:T(8,128)(2,1)S(1)}) custom-call(f32[256,1024]{1,0:T(8,128)S(1)} %get-tuple-element.60.spec_conv, f32[256,1024]{1,0:T(8,128)S(1)} %get-tuple-element.61.spec_gate, bf16[1024,512]{1,0:T(8,128)(2,1)S(1)} %copy-done.2, bf16[1024,512]{1,0:T(8,128)(2,1)S(1)} %copy-done.1, ...), custom_call_target="tpu_custom_call" | custom-call | flops 2000000000 | bytes 2000000 | tf_op jit(solution)/shard_map/pallas_call | solution.py:316
  36.0 0.7 %shard_map.117 = bf16[1024,128]{1,0:T(8,128)(2,1)} custom-call(f32[256,128]{1,0:T(8,128)S(1)} %get-tuple-element.40.refs_0_, f32[256,128]{1,0:T(8,128)S(1)} %get-tuple-element.41.refs_1_, f32[256,128]{1,0:T(8,128)S(1)} %get-tuple-element.42.refs_2_, f32[256,128]{1,0:T(8,128)S(1)} %get-tuple-element.43.refs_3_, ...), custom_call_target="tpu_custom_call" | custom-call | flops 1000000000 | bytes 1000000 | tf_op jit(solution)/shard_map/pallas_call | solution.py:316
  36.7 1.1 %collective-permute-done.13.refs_1_ = bf16[256,128]{1,0:T(8,128)(2,1)S(1)} collective-permute-done((bf16[256,128]{1,0:T(8,128)(2,1)S(1)}, bf16[256,128]{1,0:T(8,128)(2,1)S(1)}, u32[]{:S(2)}, u32[]{:S(2)}) %collective-permute-start.13) | collective-permute-done | bytes 65568 | tf_op jit(solution)/shard_map/ppermute | solution.py:340
  38.5 0.8 %shard_map.120 = (f32[128,512]{1,0:T(8,128)}, bf16[1024,128]{1,0:T(8,128)(2,1)}) custom-call(bf16[256,128]{1,0:T(8,128)(2,1)S(1)} %get-tuple-element.56.refs_0_, bf16[256,128]{1,0:T(8,128)(2,1)S(1)} %collective-permute-done.13.refs_1_, bf16[256,128]{1,0:T(8,128)(2,1)S(1)} %collective-permute-done.14.refs_2_, ...), custom_call_target="tpu_custom_call" | custom-call | flops 1000000000 | bytes 1000000 | tf_op jit(solution)/shard_map/pallas_call | solution.py:316
  (44 shorter events, 2.3 us)
Async XLA Ops:
  0.6 10.2 %collective-permute-start.4 = (bf16[32,4096]{1,0:T(8,128)(2,1)}, bf16[32,4096]{1,0:T(8,128)(2,1)S(1)}, u32[]{:S(2)}, u32[]{:S(2)}) collective-permute-start(bf16[32,4096]{1,0:T(8,128)(2,1)} %bitcast.9), channel_id=1, source_target_pairs={{0,4},{2,6},{4,0},{6,2},{1,5},{3,7},{5,1},{7,3},{8,12},{10,14},{12... | collective-permute-start | bytes 786440 | tf_op jit(solution)/shard_map/ppermute | solution.py:340
  3.7 8.3 %collective-permute-start.3 = (bf16[32,4096]{1,0:T(8,128)(2,1)}, bf16[32,4096]{1,0:T(8,128)(2,1)S(1)}, u32[]{:S(2)}, u32[]{:S(2)}) collective-permute-start(bf16[32,4096]{1,0:T(8,128)(2,1)} %bitcast.10), channel_id=1, source_target_pairs={{0,2},{2,0},{4,6},{6,4},{1,3},{3,1},{5,7},{7,5},{8,10},{10,8},{12,... | collective-permute-start | bytes 786440 | tf_op jit(solution)/shard_map/ppermute | solution.py:340
  5.2 10.1 %copy-start.1 = (bf16[1024,512]{1,0:T(8,128)(2,1)S(1)}, bf16[1024,512]{1,0:T(8,128)(2,1)}, u32[]{:S(2)}) copy-start(bf16[1024,512]{1,0:T(8,128)(2,1)} %constant.11.clone.refs_8_.inv_lo) | copy-start | bytes 3145732
  5.2 10.1 %copy-start.2 = (bf16[1024,512]{1,0:T(8,128)(2,1)S(1)}, bf16[1024,512]{1,0:T(8,128)(2,1)}, u32[]{:S(2)}) copy-start(bf16[1024,512]{1,0:T(8,128)(2,1)} %constant.10.clone.refs_7_.inv_hi) | copy-start | bytes 3145732
  5.2 10.1 %copy-start.7 = (bf16[1,1024,128]{2,1,0:T(8,128)(2,1)S(1)}, bf16[1,1024,128]{2,1,0:T(8,128)(2,1)}, u32[]{:S(2)}) copy-start(bf16[1,1024,128]{2,1,0:T(8,128)(2,1)} %param.11) | copy-start | bytes 786436
  6.3 10.7 %slice-start = ((s8[8388608]{0:T(1024)(128)(4,1)}), s8[4194304]{0:T(1024)(128)(4,1)S(1)}, s32[]{:S(2)}) async-start(s8[8388608]{0:T(1024)(128)(4,1)} %bitcast.5), calls=%async_computation | async-start | bytes 8388608
  6.3 10.7 %copy-start = (bf16[1,1024,128]{2,1,0:T(8,128)(2,1)S(1)}, bf16[1,1024,128]{2,1,0:T(8,128)(2,1)}, u32[]{:S(2)}) copy-start(bf16[1,1024,128]{2,1,0:T(8,128)(2,1)} %param.10) | copy-start | bytes 786436
  6.3 10.7 %copy-start.5 = (bf16[1,32,4096]{2,1,0:T(8,128)(2,1)S(1)}, bf16[1,32,4096]{2,1,0:T(8,128)(2,1)}, u32[]{:S(2)}) copy-start(bf16[1,32,4096]{2,1,0:T(8,128)(2,1)} %param.9) | copy-start | bytes 786436
  6.3 8.3 %collective-permute-start = (bf16[256,128]{1,0:T(8,128)(2,1)S(1)}, bf16[256,128]{1,0:T(8,128)(2,1)S(1)}, u32[]{:S(2)}, u32[]{:S(2)}) collective-permute-start(bf16[256,128]{1,0:T(8,128)(2,1)S(1)} %get-tuple-element.35), channel_id=1, source_target_pairs={{0,24},{8,16},{16,8},{24,0},{1,25},{9,17},{17,9},{25,1},{2,26},{10... | collective-permute-start | bytes 196616 | tf_op jit(solution)/shard_map/ppermute | solution.py:340
  10.0 5.2 %collective-permute-start.1 = (bf16[256,128]{1,0:T(8,128)(2,1)S(1)}, bf16[256,128]{1,0:T(8,128)(2,1)S(1)}, u32[]{:S(2)}, u32[]{:S(2)}) collective-permute-start(bf16[256,128]{1,0:T(8,128)(2,1)S(1)} %get-tuple-element.36), channel_id=1, source_target_pairs={{0,16},{8,24},{16,0},{24,8},{1,17},{9,25},{17,1},{25,9},{2,18},{10... | collective-permute-start | bytes 196616 | tf_op jit(solution)/shard_map/ppermute | solution.py:340
  10.0 5.2 %collective-permute-start.2 = (bf16[256,128]{1,0:T(8,128)(2,1)S(1)}, bf16[256,128]{1,0:T(8,128)(2,1)S(1)}, u32[]{:S(2)}, u32[]{:S(2)}) collective-permute-start(bf16[256,128]{1,0:T(8,128)(2,1)S(1)} %get-tuple-element.37), channel_id=1, source_target_pairs={{0,8},{8,0},{16,24},{24,16},{1,9},{9,1},{17,25},{25,17},{2,10},{10... | collective-permute-start | bytes 196616 | tf_op jit(solution)/shard_map/ppermute | solution.py:340
  10.8 6.2 %collective-permute-start.6 = (bf16[32,2688]{1,0:T(8,128)(2,1)S(1)}, bf16[32,2688]{1,0:T(8,128)(2,1)S(1)}, u32[]{:S(2)}, u32[]{:S(2)}) collective-permute-start(bf16[32,2688]{1,0:T(8,128)(2,1)S(1)} %slice.9), channel_id=1, source_target_pairs={{0,2},{2,0},{4,6},{6,4},{1,3},{3,1},{5,7},{7,5},{8,10},{10,8},{12,... | collective-permute-start | bytes 516104 | tf_op jit(solution)/shard_map/ppermute | solution.py:340
  12.0 5.0 %collective-permute-start.5 = (bf16[32,1408]{1,0:T(8,128)(2,1)S(1)}, bf16[32,1408]{1,0:T(8,128)(2,1)S(1)}, u32[]{:S(2)}, u32[]{:S(2)}) collective-permute-start(bf16[32,1408]{1,0:T(8,128)(2,1)S(1)} %slice.8), channel_id=1, source_target_pairs={{0,4},{2,6},{4,0},{6,2},{1,5},{3,7},{5,1},{7,3},{8,12},{10,14},{12... | collective-permute-start | bytes 270344 | tf_op jit(solution)/shard_map/ppermute | solution.py:340
  19.0 9.0 %collective-permute-start.10 = (bf16[256,128]{1,0:T(8,128)(2,1)S(1)}, bf16[256,128]{1,0:T(8,128)(2,1)S(1)}, u32[]{:S(2)}, u32[]{:S(2)}) collective-permute-start(bf16[256,128]{1,0:T(8,128)(2,1)S(1)} %get-tuple-element.53), channel_id=1, source_target_pairs={{0,24},{8,16},{16,8},{24,0},{1,25},{9,17},{17,9},{25,1},{2,26},{10... | collective-permute-start | bytes 196616 | tf_op jit(solution)/shard_map/ppermute | solution.py:340
  22.2 6.8 %collective-permute-start.11 = (bf16[256,128]{1,0:T(8,128)(2,1)S(1)}, bf16[256,128]{1,0:T(8,128)(2,1)S(1)}, u32[]{:S(2)}, u32[]{:S(2)}) collective-permute-start(bf16[256,128]{1,0:T(8,128)(2,1)S(1)} %get-tuple-element.54), channel_id=1, source_target_pairs={{0,16},{8,24},{16,0},{24,8},{1,17},{9,25},{17,1},{25,9},{2,18},{10... | collective-permute-start | bytes 196616 | tf_op jit(solution)/shard_map/ppermute | solution.py:340
  22.2 6.8 %collective-permute-start.12 = (bf16[256,128]{1,0:T(8,128)(2,1)S(1)}, bf16[256,128]{1,0:T(8,128)(2,1)S(1)}, u32[]{:S(2)}, u32[]{:S(2)}) collective-permute-start(bf16[256,128]{1,0:T(8,128)(2,1)S(1)} %get-tuple-element.55), channel_id=1, source_target_pairs={{0,8},{8,0},{16,24},{24,16},{1,9},{9,1},{17,25},{25,17},{2,10},{10... | collective-permute-start | bytes 196616 | tf_op jit(solution)/shard_map/ppermute | solution.py:340
  24.1 9.5 %collective-permute-start.7 = (bf16[256,128]{1,0:T(8,128)(2,1)S(1)}, bf16[256,128]{1,0:T(8,128)(2,1)S(1)}, u32[]{:S(2)}, u32[]{:S(2)}) collective-permute-start(bf16[256,128]{1,0:T(8,128)(2,1)S(1)} %get-tuple-element.49), channel_id=1, source_target_pairs={{0,8},{8,0},{16,24},{24,16},{1,9},{9,1},{17,25},{25,17},{2,10},{10... | collective-permute-start | bytes 196616 | tf_op jit(solution)/shard_map/ppermute | solution.py:340
  25.0 9.3 %collective-permute-start.8 = (bf16[256,128]{1,0:T(8,128)(2,1)S(1)}, bf16[256,128]{1,0:T(8,128)(2,1)S(1)}, u32[]{:S(2)}, u32[]{:S(2)}) collective-permute-start(bf16[256,128]{1,0:T(8,128)(2,1)S(1)} %get-tuple-element.50), channel_id=1, source_target_pairs={{0,16},{8,24},{16,0},{24,8},{1,17},{9,25},{17,1},{25,9},{2,18},{10... | collective-permute-start | bytes 196616 | tf_op jit(solution)/shard_map/ppermute | solution.py:340
  27.9 7.6 %collective-permute-start.9 = (bf16[256,128]{1,0:T(8,128)(2,1)S(1)}, bf16[256,128]{1,0:T(8,128)(2,1)S(1)}, u32[]{:S(2)}, u32[]{:S(2)}) collective-permute-start(bf16[256,128]{1,0:T(8,128)(2,1)S(1)} %get-tuple-element.51), channel_id=1, source_target_pairs={{0,24},{8,16},{16,8},{24,0},{1,25},{9,17},{17,9},{25,1},{2,26},{10... | collective-permute-start | bytes 196616 | tf_op jit(solution)/shard_map/ppermute | solution.py:340
  30.7 7.1 %collective-permute-start.13 = (bf16[256,128]{1,0:T(8,128)(2,1)S(1)}, bf16[256,128]{1,0:T(8,128)(2,1)S(1)}, u32[]{:S(2)}, u32[]{:S(2)}) collective-permute-start(bf16[256,128]{1,0:T(8,128)(2,1)S(1)} %get-tuple-element.57), channel_id=1, source_target_pairs={{0,16},{8,24},{16,0},{24,8},{1,17},{9,25},{17,1},{25,9},{2,18},{10... | collective-permute-start | bytes 196616 | tf_op jit(solution)/shard_map/ppermute | solution.py:340
  31.3 6.5 %collective-permute-start.14 = (bf16[256,128]{1,0:T(8,128)(2,1)S(1)}, bf16[256,128]{1,0:T(8,128)(2,1)S(1)}, u32[]{:S(2)}, u32[]{:S(2)}) collective-permute-start(bf16[256,128]{1,0:T(8,128)(2,1)S(1)} %get-tuple-element.58), channel_id=1, source_target_pairs={{0,24},{8,16},{16,8},{24,0},{1,25},{9,17},{17,9},{25,1},{2,26},{10... | collective-permute-start | bytes 196616 | tf_op jit(solution)/shard_map/ppermute | solution.py:340
  33.6 4.8 %collective-permute-start.15 = (bf16[256,128]{1,0:T(8,128)(2,1)S(1)}, bf16[256,128]{1,0:T(8,128)(2,1)S(1)}, u32[]{:S(2)}, u32[]{:S(2)}) collective-permute-start(bf16[256,128]{1,0:T(8,128)(2,1)S(1)} %get-tuple-element.59), channel_id=1, source_target_pairs={{0,8},{8,0},{16,24},{24,16},{1,9},{9,1},{17,25},{25,17},{2,10},{10... | collective-permute-start | bytes 196616 | tf_op jit(solution)/shard_map/ppermute | solution.py:340
  35.4 3.0 %collective-permute-start.16 = (bf16[64,512]{1,0:T(8,128)(2,1)S(1)}, bf16[64,512]{1,0:T(8,128)(2,1)S(1)}, u32[]{:S(2)}, u32[]{:S(2)}) collective-permute-start(bf16[64,512]{1,0:T(8,128)(2,1)S(1)} %get-tuple-element.62), channel_id=1, source_target_pairs={{0,1},{1,0},{2,3},{3,2},{4,5},{5,4},{6,7},{7,6},{8,9},{9,8},{10,11... | collective-permute-start | bytes 196616 | tf_op jit(solution)/shard_map/ppermute | solution.py:340
  35.5 3.0 %collective-permute-start.17 = (bf16[64,512]{1,0:T(8,128)(2,1)S(1)}, bf16[64,512]{1,0:T(8,128)(2,1)S(1)}, u32[]{:S(2)}, u32[]{:S(2)}) collective-permute-start(bf16[64,512]{1,0:T(8,128)(2,1)S(1)} %get-tuple-element.63), channel_id=1, source_target_pairs={{0,1},{1,0},{2,3},{3,2},{4,5},{5,4},{6,7},{7,6},{8,9},{9,8},{10,11... | collective-permute-start | bytes 196616 | tf_op jit(solution)/shard_map/ppermute | solution.py:340
  (4 other events, 30.4 us)

commit v6 on v5

--- a/solution.py
+++ b/solution.py
@@ -274,7 +274,7 @@
 
 
 def filter_kernel(parts, scale, spec_conv, spec_gate, inv_hi, inv_lo, *refs):
-    keep, *send, whole = refs[parts - 2 :]
+    keep, *send, whole = refs[1:]
     product = spectrum_product(spec_conv[...], spec_gate[...], True)
     whole[...] = inverse_dense(product, inv_hi, inv_lo) * scale
     rows = keep.shape[0]
@@ -408,7 +408,7 @@
     keep, send_low, send_high = call(
         functools.partial(filter_kernel, parts, scale),
         [half, quarter, quarter],
-        [spec_conv, spec_gate, *tables[2:], *conv_back[1:-1]],
+        [spec_conv, spec_gate, *tables[2:], conv_back[1]],
         [pltpu.VMEM((chans, length), f32)],
         cost=2.0,
     )

time: 39.4 us -> 39.4 us (level)
  no operation moved by 1% of the time
where the time goes in v6:
time: 39.4 us; the launch traced here: 39.3 us
  starting transfers between devices  24.8 us (63%)
  Pallas kernels  10.8 us (27%)
  waiting for transfers between devices  2.82 us (7%)
  between operations  0.86 us (2%)
    ppermute x18, starting transfers between devices, swap(): return lax.ppermute(value, axis, [(i, i ^ k) for i in range(size)])  24.8 us
    pallas_call x9, Pallas kernels, call(): pl.pallas_call(kernel, out_shape=outs, in_specs=[hbm if i in far else vme...  10.8 us
    ppermute x18, waiting for transfers between devices, swap(): return lax.ppermute(value, axis, [(i, i ^ k) for i in range(size)])  2.82 us
  transfers between devices with their start and end apart: 18, of which 4 were waited for; matrix products, arithmetic and copies ran while one was open for 0% of the time, Pallas kernels for 21%

profile of v6, /device:TPU:0, one launch (start us, length us, event | category | flops | bytes accessed | tf_op | source)
XLA Modules:
  0.0 39.3 jit_solution(9682515927810926870)
XLA Ops:
  0.6 3.0 %collective-permute-start.4 = (bf16[32,4096]{1,0:T(8,128)(2,1)}, bf16[32,4096]{1,0:T(8,128)(2,1)S(1)}, u32[]{:S(2)}, u32[]{:S(2)}) collective-permute-start(bf16[32,4096]{1,0:T(8,128)(2,1)} %bitcast.9), channel_id=1, source_target_pairs={{0,4},{2,6},{4,0},{6,2},{1,5},{3,7},{5,1},{7,3},{8,12},{10,14},{12... | collective-permute-start | bytes 786440 | tf_op jit(solution)/shard_map/ppermute | solution.py:340
  3.7 1.5 %collective-permute-start.3 = (bf16[32,4096]{1,0:T(8,128)(2,1)}, bf16[32,4096]{1,0:T(8,128)(2,1)S(1)}, u32[]{:S(2)}, u32[]{:S(2)}) collective-permute-start(bf16[32,4096]{1,0:T(8,128)(2,1)} %bitcast.10), channel_id=1, source_target_pairs={{0,2},{2,0},{4,6},{6,4},{1,3},{3,1},{5,7},{7,5},{8,10},{10,8},{12,... | collective-permute-start | bytes 786440 | tf_op jit(solution)/shard_map/ppermute | solution.py:340
  5.2 1.1 %shard_map.112 = (bf16[256,128]{1,0:T(8,128)(2,1)S(1)}, bf16[256,128]{1,0:T(8,128)(2,1)S(1)}, bf16[256,128]{1,0:T(8,128)(2,1)S(1)}) custom-call(bf16[1024,128]{1,0:T(8,128)(2,1)} %bitcast.12), custom_call_target="tpu_custom_call" | custom-call | flops 10000000000 | bytes 10000000 | tf_op jit(solution)/shard_map/pallas_call | solution.py:316
  6.3 3.7 %collective-permute-start = (bf16[256,128]{1,0:T(8,128)(2,1)S(1)}, bf16[256,128]{1,0:T(8,128)(2,1)S(1)}, u32[]{:S(2)}, u32[]{:S(2)}) collective-permute-start(bf16[256,128]{1,0:T(8,128)(2,1)S(1)} %get-tuple-element.35), channel_id=1, source_target_pairs={{0,24},{8,16},{16,8},{24,0},{1,25},{9,17},{17,9},{25,1},{2,26},{10... | collective-permute-start | bytes 196616 | tf_op jit(solution)/shard_map/ppermute | solution.py:340
  10.0 0.8 %collective-permute-start.2 = (bf16[256,128]{1,0:T(8,128)(2,1)S(1)}, bf16[256,128]{1,0:T(8,128)(2,1)S(1)}, u32[]{:S(2)}, u32[]{:S(2)}) collective-permute-start(bf16[256,128]{1,0:T(8,128)(2,1)S(1)} %get-tuple-element.37), channel_id=1, source_target_pairs={{0,8},{8,0},{16,24},{24,16},{1,9},{9,1},{17,25},{25,17},{2,10},{10... | collective-permute-start | bytes 196616 | tf_op jit(solution)/shard_map/ppermute | solution.py:340
  10.8 1.2 %collective-permute-start.6 = (bf16[32,2688]{1,0:T(8,128)(2,1)S(1)}, bf16[32,2688]{1,0:T(8,128)(2,1)S(1)}, u32[]{:S(2)}, u32[]{:S(2)}) collective-permute-start(bf16[32,2688]{1,0:T(8,128)(2,1)S(1)} %slice.9), channel_id=1, source_target_pairs={{0,2},{2,0},{4,6},{6,4},{1,3},{3,1},{5,7},{7,5},{8,10},{10,8},{12,... | collective-permute-start | bytes 516104 | tf_op jit(solution)/shard_map/ppermute | solution.py:340
  12.0 1.6 %collective-permute-start.5 = (bf16[32,1408]{1,0:T(8,128)(2,1)S(1)}, bf16[32,1408]{1,0:T(8,128)(2,1)S(1)}, u32[]{:S(2)}, u32[]{:S(2)}) collective-permute-start(bf16[32,1408]{1,0:T(8,128)(2,1)S(1)} %slice.8), channel_id=1, source_target_pairs={{0,4},{2,6},{4,0},{6,2},{1,5},{3,7},{5,1},{7,3},{8,12},{10,14},{12... | collective-permute-start | bytes 270344 | tf_op jit(solution)/shard_map/ppermute | solution.py:340
  13.6 1.0 %shard_map.113.refs_4_ = f32[256,1024]{1,0:T(8,128)S(1)} custom-call(f32[256,512]{1,0:T(8,128)S(1)} %copy-done.6, bf16[512,1024]{1,0:T(8,128)(2,1)S(1)} %copy-done.4, bf16[512,1024]{1,0:T(8,128)(2,1)S(1)} %copy-done.3, bf16[32,4096]{1,0:T(8,128)(2,1)S(1)} %collective-permute-done.3.after_1.refs_1_, bf16[32,4096]{1,0:T(8,128)(2,1)S(1)} %collective-permute-done.4.after_2.refs_2_), custom_call_target="tpu_custom_call" | custom-call | flops 2000000000 | bytes 2000000 | tf_op jit(solution)/shard_map/pallas_call | solution.py:316
  14.6 0.7 %collective-permute-done.1.refs_2_ = bf16[256,128]{1,0:T(8,128)(2,1)S(1)} collective-permute-done((bf16[256,128]{1,0:T(8,128)(2,1)S(1)}, bf16[256,128]{1,0:T(8,128)(2,1)S(1)}, u32[]{:S(2)}, u32[]{:S(2)}) %collective-permute-start.1) | collective-permute-done | bytes 65568 | tf_op jit(solution)/shard_map/ppermute | solution.py:340
  15.3 1.7 %shard_map.114 = (bf16[256,128]{1,0:T(8,128)(2,1)S(1)}, bf16[256,128]{1,0:T(8,128)(2,1)S(1)}, bf16[256,128]{1,0:T(8,128)(2,1)S(1)}, bf16[256,128]{1,0:T(8,128)(2,1)S(1)}, f32[256,1024]{1,0:T(8,128)S(1)}) custom-call(bf16[1024,128]{1,0:T(8,128)(2,1)S(1)} %bitcast.13, bf16[256,128]{1,0:T(8,128)(2,1)S(1)} %collective-permute-done.refs_1_, ...), custom_call_target="tpu_custom_call" | custom-call | flops 2000000000 | bytes 2000000 | tf_op jit(solution)/shard_map/pallas_call | solution.py:316
  17.1 1.9 %shard_map.115 = (f32[256,128]{1,0:T(8,128)S(1)}, f32[256,128]{1,0:T(8,128)S(1)}, f32[256,128]{1,0:T(8,128)S(1)}, bf16[256,128]{1,0:T(8,128)(2,1)S(1)}, bf16[256...) custom-call(bf16[256,128]{1,0:T(8,128)(2,1)S(1)} %get-tuple-element.48.after.refs_4_, ...), custom_call_target="tpu_custom_call" | custom-call | flops 1000000000 | bytes 1000000 | tf_op jit(solution)/shard_map/pallas_call | solution.py:316
  19.0 3.2 %collective-permute-start.10 = (bf16[256,128]{1,0:T(8,128)(2,1)S(1)}, bf16[256,128]{1,0:T(8,128)(2,1)S(1)}, u32[]{:S(2)}, u32[]{:S(2)}) collective-permute-start(bf16[256,128]{1,0:T(8,128)(2,1)S(1)} %get-tuple-element.53), channel_id=1, source_target_pairs={{0,24},{8,16},{16,8},{24,0},{1,25},{9,17},{17,9},{25,1},{2,26},{10... | collective-permute-start | bytes 196616 | tf_op jit(solution)/shard_map/ppermute | solution.py:340
  22.2 1.2 %collective-permute-start.12 = (bf16[256,128]{1,0:T(8,128)(2,1)S(1)}, bf16[256,128]{1,0:T(8,128)(2,1)S(1)}, u32[]{:S(2)}, u32[]{:S(2)}) collective-permute-start(bf16[256,128]{1,0:T(8,128)(2,1)S(1)} %get-tuple-element.55), channel_id=1, source_target_pairs={{0,8},{8,0},{16,24},{24,16},{1,9},{9,1},{17,25},{25,17},{2,10},{10... | collective-permute-start | bytes 196616 | tf_op jit(solution)/shard_map/ppermute | solution.py:340
  23.4 0.7 %shard_map.116 = (f32[256,128]{1,0:T(8,128)S(1)}, bf16[256,128]{1,0:T(8,128)(2,1)S(1)}) custom-call(bf16[1024,4096]{1,0:T(8,128)(2,1)S(1)} %bitcast.6, bf16[1024,128]{1,0:T(8,128)(2,1)S(1)} %bitcast.8, bf16[128,4096]{1,0:T(8,128)(2,1)S(1)} %get-tuple-element.39.rows_all), custom_call_target="tpu_custom_call" | custom-call | flops 1000000000 | bytes 1000000 | tf_op jit(solution)/shard_map/pallas_call | solution.py:316
  24.1 0.9 %collective-permute-start.7 = (bf16[256,128]{1,0:T(8,128)(2,1)S(1)}, bf16[256,128]{1,0:T(8,128)(2,1)S(1)}, u32[]{:S(2)}, u32[]{:S(2)}) collective-permute-start(bf16[256,128]{1,0:T(8,128)(2,1)S(1)} %get-tuple-element.49), channel_id=1, source_target_pairs={{0,8},{8,0},{16,24},{24,16},{1,9},{9,1},{17,25},{25,17},{2,10},{10... | collective-permute-start | bytes 196616 | tf_op jit(solution)/shard_map/ppermute | solution.py:340
  25.0 2.9 %collective-permute-start.8 = (bf16[256,128]{1,0:T(8,128)(2,1)S(1)}, bf16[256,128]{1,0:T(8,128)(2,1)S(1)}, u32[]{:S(2)}, u32[]{:S(2)}) collective-permute-start(bf16[256,128]{1,0:T(8,128)(2,1)S(1)} %get-tuple-element.50), channel_id=1, source_target_pairs={{0,16},{8,24},{16,0},{24,8},{1,17},{9,25},{17,1},{25,9},{2,18},{10... | collective-permute-start | bytes 196616 | tf_op jit(solution)/shard_map/ppermute | solution.py:340
  27.9 0.7 %collective-permute-start.9 = (bf16[256,128]{1,0:T(8,128)(2,1)S(1)}, bf16[256,128]{1,0:T(8,128)(2,1)S(1)}, u32[]{:S(2)}, u32[]{:S(2)}) collective-permute-start(bf16[256,128]{1,0:T(8,128)(2,1)S(1)} %get-tuple-element.51), channel_id=1, source_target_pairs={{0,24},{8,16},{16,8},{24,0},{1,25},{9,17},{17,9},{25,1},{2,26},{10... | collective-permute-start | bytes 196616 | tf_op jit(solution)/shard_map/ppermute | solution.py:340
  29.0 1.7 %shard_map.118 = (bf16[256,128]{1,0:T(8,128)(2,1)S(1)}, bf16[256,128]{1,0:T(8,128)(2,1)S(1)}, bf16[256,128]{1,0:T(8,128)(2,1)S(1)}, bf16[256,128]{1,0:T(8,128)(2,1)S(1)}, f32[256,1024]{1,0:T(8,128)S(1)}) custom-call(bf16[256,128]{1,0:T(8,128)(2,1)S(1)} %get-tuple-element.52.refs_0_, bf16[256,128]{1,0:T(8,128)(2,1)S(1)} %collective-permute-done.10.refs_1_, ...), custom_call_target="tpu_custom_call" | custom-call | flops 1000000000 | bytes 1000000 | tf_op jit(solution)/shard_map/pallas_call | solution.py:316
  31.3 2.4 %collective-permute-start.14 = (bf16[256,128]{1,0:T(8,128)(2,1)S(1)}, bf16[256,128]{1,0:T(8,128)(2,1)S(1)}, u32[]{:S(2)}, u32[]{:S(2)}) collective-permute-start(bf16[256,128]{1,0:T(8,128)(2,1)S(1)} %get-tuple-element.58), channel_id=1, source_target_pairs={{0,24},{8,16},{16,8},{24,0},{1,25},{9,17},{17,9},{25,1},{2,26},{10... | collective-permute-start | bytes 196616 | tf_op jit(solution)/shard_map/ppermute | solution.py:340
  33.6 0.7 %collective-permute-start.15 = (bf16[256,128]{1,0:T(8,128)(2,1)S(1)}, bf16[256,128]{1,0:T(8,128)(2,1)S(1)}, u32[]{:S(2)}, u32[]{:S(2)}) collective-permute-start(bf16[256,128]{1,0:T(8,128)(2,1)S(1)} %get-tuple-element.59), channel_id=1, source_target_pairs={{0,8},{8,0},{16,24},{24,16},{1,9},{9,1},{17,25},{25,17},{2,10},{10... | collective-permute-start | bytes 196616 | tf_op jit(solution)/shard_map/ppermute | solution.py:340
  34.3 1.1 %shard_map.119 = (f32[128,512]{1,0:T(8,128)S(1)}, bf16[64,512]{1,0:T(8,128)(2,1)S(1)}, bf16[64,512]{1,0:T(8,128)(2,1)S(1)}) custom-call(f32[256,1024]{1,0:T(8,128)S(1)} %get-tuple-element.60.spec_conv, f32[256,1024]{1,0:T(8,128)S(1)} %get-tuple-element.61.spec_gate, bf16[1024,512]{1,0:T(8,128)(2,1)S(1)} %copy-done.2, bf16[1024,512]{1,0:T(8,128)(2,1)S(1)} %copy-done.1, ...), custom_call_target="tpu_custom_call" | custom-call | flops 2000000000 | bytes 2000000 | tf_op jit(solution)/shard_map/pallas_call | solution.py:316
  36.0 0.7 %shard_map.117 = bf16[1024,128]{1,0:T(8,128)(2,1)} custom-call(f32[256,128]{1,0:T(8,128)S(1)} %get-tuple-element.40.refs_0_, f32[256,128]{1,0:T(8,128)S(1)} %get-tuple-element.41.refs_1_, f32[256,128]{1,0:T(8,128)S(1)} %get-tuple-element.42.refs_2_, f32[256,128]{1,0:T(8,128)S(1)} %get-tuple-element.43.refs_3_, ...), custom_call_target="tpu_custom_call" | custom-call | flops 1000000000 | bytes 1000000 | tf_op jit(solution)/shard_map/pallas_call | solution.py:316
  36.7 1.1 %collective-permute-done.13.refs_1_ = bf16[256,128]{1,0:T(8,128)(2,1)S(1)} collective-permute-done((bf16[256,128]{1,0:T(8,128)(2,1)S(1)}, bf16[256,128]{1,0:T(8,128)(2,1)S(1)}, u32[]{:S(2)}, u32[]{:S(2)}) %collective-permute-start.13) | collective-permute-done | bytes 65568 | tf_op jit(solution)/shard_map/ppermute | solution.py:340
  38.5 0.8 %shard_map.120 = (f32[128,512]{1,0:T(8,128)}, bf16[1024,128]{1,0:T(8,128)(2,1)}) custom-call(bf16[256,128]{1,0:T(8,128)(2,1)S(1)} %get-tuple-element.56.refs_0_, bf16[256,128]{1,0:T(8,128)(2,1)S(1)} %collective-permute-done.13.refs_1_, bf16[256,128]{1,0:T(8,128)(2,1)S(1)} %collective-permute-done.14.refs_2_, ...), custom_call_target="tpu_custom_call" | custom-call | flops 1000000000 | bytes 1000000 | tf_op jit(solution)/shard_map/pallas_call | solution.py:316
  (44 shorter events, 2.3 us)
Async XLA Ops:
  0.6 10.2 %collective-permute-start.4 = (bf16[32,4096]{1,0:T(8,128)(2,1)}, bf16[32,4096]{1,0:T(8,128)(2,1)S(1)}, u32[]{:S(2)}, u32[]{:S(2)}) collective-permute-start(bf16[32,4096]{1,0:T(8,128)(2,1)} %bitcast.9), channel_id=1, source_target_pairs={{0,4},{2,6},{4,0},{6,2},{1,5},{3,7},{5,1},{7,3},{8,12},{10,14},{12... | collective-permute-start | bytes 786440 | tf_op jit(solution)/shard_map/ppermute | solution.py:340
  3.7 8.3 %collective-permute-start.3 = (bf16[32,4096]{1,0:T(8,128)(2,1)}, bf16[32,4096]{1,0:T(8,128)(2,1)S(1)}, u32[]{:S(2)}, u32[]{:S(2)}) collective-permute-start(bf16[32,4096]{1,0:T(8,128)(2,1)} %bitcast.10), channel_id=1, source_target_pairs={{0,2},{2,0},{4,6},{6,4},{1,3},{3,1},{5,7},{7,5},{8,10},{10,8},{12,... | collective-permute-start | bytes 786440 | tf_op jit(solution)/shard_map/ppermute | solution.py:340
  5.2 10.1 %copy-start.1 = (bf16[1024,512]{1,0:T(8,128)(2,1)S(1)}, bf16[1024,512]{1,0:T(8,128)(2,1)}, u32[]{:S(2)}) copy-start(bf16[1024,512]{1,0:T(8,128)(2,1)} %constant.11.clone.refs_8_.inv_lo) | copy-start | bytes 3145732
  5.2 10.1 %copy-start.2 = (bf16[1024,512]{1,0:T(8,128)(2,1)S(1)}, bf16[1024,512]{1,0:T(8,128)(2,1)}, u32[]{:S(2)}) copy-start(bf16[1024,512]{1,0:T(8,128)(2,1)} %constant.10.clone.refs_7_.inv_hi) | copy-start | bytes 3145732
  5.2 10.1 %copy-start.7 = (bf16[1,1024,128]{2,1,0:T(8,128)(2,1)S(1)}, bf16[1,1024,128]{2,1,0:T(8,128)(2,1)}, u32[]{:S(2)}) copy-start(bf16[1,1024,128]{2,1,0:T(8,128)(2,1)} %param.11) | copy-start | bytes 786436
  6.3 10.7 %slice-start = ((s8[8388608]{0:T(1024)(128)(4,1)}), s8[4194304]{0:T(1024)(128)(4,1)S(1)}, s32[]{:S(2)}) async-start(s8[8388608]{0:T(1024)(128)(4,1)} %bitcast.5), calls=%async_computation | async-start | bytes 8388608
  6.3 10.7 %copy-start = (bf16[1,1024,128]{2,1,0:T(8,128)(2,1)S(1)}, bf16[1,1024,128]{2,1,0:T(8,128)(2,1)}, u32[]{:S(2)}) copy-start(bf16[1,1024,128]{2,1,0:T(8,128)(2,1)} %param.10) | copy-start | bytes 786436
  6.3 10.7 %copy-start.5 = (bf16[1,32,4096]{2,1,0:T(8,128)(2,1)S(1)}, bf16[1,32,4096]{2,1,0:T(8,128)(2,1)}, u32[]{:S(2)}) copy-start(bf16[1,32,4096]{2,1,0:T(8,128)(2,1)} %param.9) | copy-start | bytes 786436
  6.3 8.3 %collective-permute-start = (bf16[256,128]{1,0:T(8,128)(2,1)S(1)}, bf16[256,128]{1,0:T(8,128)(2,1)S(1)}, u32[]{:S(2)}, u32[]{:S(2)}) collective-permute-start(bf16[256,128]{1,0:T(8,128)(2,1)S(1)} %get-tuple-element.35), channel_id=1, source_target_pairs={{0,24},{8,16},{16,8},{24,0},{1,25},{9,17},{17,9},{25,1},{2,26},{10... | collective-permute-start | bytes 196616 | tf_op jit(solution)/shard_map/ppermute | solution.py:340
  10.0 5.2 %collective-permute-start.1 = (bf16[256,128]{1,0:T(8,128)(2,1)S(1)}, bf16[256,128]{1,0:T(8,128)(2,1)S(1)}, u32[]{:S(2)}, u32[]{:S(2)}) collective-permute-start(bf16[256,128]{1,0:T(8,128)(2,1)S(1)} %get-tuple-element.36), channel_id=1, source_target_pairs={{0,16},{8,24},{16,0},{24,8},{1,17},{9,25},{17,1},{25,9},{2,18},{10... | collective-permute-start | bytes 196616 | tf_op jit(solution)/shard_map/ppermute | solution.py:340
  10.0 5.2 %collective-permute-start.2 = (bf16[256,128]{1,0:T(8,128)(2,1)S(1)}, bf16[256,128]{1,0:T(8,128)(2,1)S(1)}, u32[]{:S(2)}, u32[]{:S(2)}) collective-permute-start(bf16[256,128]{1,0:T(8,128)(2,1)S(1)} %get-tuple-element.37), channel_id=1, source_target_pairs={{0,8},{8,0},{16,24},{24,16},{1,9},{9,1},{17,25},{25,17},{2,10},{10... | collective-permute-start | bytes 196616 | tf_op jit(solution)/shard_map/ppermute | solution.py:340
  10.8 6.2 %collective-permute-start.6 = (bf16[32,2688]{1,0:T(8,128)(2,1)S(1)}, bf16[32,2688]{1,0:T(8,128)(2,1)S(1)}, u32[]{:S(2)}, u32[]{:S(2)}) collective-permute-start(bf16[32,2688]{1,0:T(8,128)(2,1)S(1)} %slice.9), channel_id=1, source_target_pairs={{0,2},{2,0},{4,6},{6,4},{1,3},{3,1},{5,7},{7,5},{8,10},{10,8},{12,... | collective-permute-start | bytes 516104 | tf_op jit(solution)/shard_map/ppermute | solution.py:340
  12.0 5.0 %collective-permute-start.5 = (bf16[32,1408]{1,0:T(8,128)(2,1)S(1)}, bf16[32,1408]{1,0:T(8,128)(2,1)S(1)}, u32[]{:S(2)}, u32[]{:S(2)}) collective-permute-start(bf16[32,1408]{1,0:T(8,128)(2,1)S(1)} %slice.8), channel_id=1, source_target_pairs={{0,4},{2,6},{4,0},{6,2},{1,5},{3,7},{5,1},{7,3},{8,12},{10,14},{12... | collective-permute-start | bytes 270344 | tf_op jit(solution)/shard_map/ppermute | solution.py:340
  19.0 9.0 %collective-permute-start.10 = (bf16[256,128]{1,0:T(8,128)(2,1)S(1)}, bf16[256,128]{1,0:T(8,128)(2,1)S(1)}, u32[]{:S(2)}, u32[]{:S(2)}) collective-permute-start(bf16[256,128]{1,0:T(8,128)(2,1)S(1)} %get-tuple-element.53), channel_id=1, source_target_pairs={{0,24},{8,16},{16,8},{24,0},{1,25},{9,17},{17,9},{25,1},{2,26},{10... | collective-permute-start | bytes 196616 | tf_op jit(solution)/shard_map/ppermute | solution.py:340
  22.2 6.8 %collective-permute-start.11 = (bf16[256,128]{1,0:T(8,128)(2,1)S(1)}, bf16[256,128]{1,0:T(8,128)(2,1)S(1)}, u32[]{:S(2)}, u32[]{:S(2)}) collective-permute-start(bf16[256,128]{1,0:T(8,128)(2,1)S(1)} %get-tuple-element.54), channel_id=1, source_target_pairs={{0,16},{8,24},{16,0},{24,8},{1,17},{9,25},{17,1},{25,9},{2,18},{10... | collective-permute-start | bytes 196616 | tf_op jit(solution)/shard_map/ppermute | solution.py:340
  22.2 6.8 %collective-permute-start.12 = (bf16[256,128]{1,0:T(8,128)(2,1)S(1)}, bf16[256,128]{1,0:T(8,128)(2,1)S(1)}, u32[]{:S(2)}, u32[]{:S(2)}) collective-permute-start(bf16[256,128]{1,0:T(8,128)(2,1)S(1)} %get-tuple-element.55), channel_id=1, source_target_pairs={{0,8},{8,0},{16,24},{24,16},{1,9},{9,1},{17,25},{25,17},{2,10},{10... | collective-permute-start | bytes 196616 | tf_op jit(solution)/shard_map/ppermute | solution.py:340
  24.1 9.5 %collective-permute-start.7 = (bf16[256,128]{1,0:T(8,128)(2,1)S(1)}, bf16[256,128]{1,0:T(8,128)(2,1)S(1)}, u32[]{:S(2)}, u32[]{:S(2)}) collective-permute-start(bf16[256,128]{1,0:T(8,128)(2,1)S(1)} %get-tuple-element.49), channel_id=1, source_target_pairs={{0,8},{8,0},{16,24},{24,16},{1,9},{9,1},{17,25},{25,17},{2,10},{10... | collective-permute-start | bytes 196616 | tf_op jit(solution)/shard_map/ppermute | solution.py:340
  25.0 10.4 %collective-permute-start.8 = (bf16[256,128]{1,0:T(8,128)(2,1)S(1)}, bf16[256,128]{1,0:T(8,128)(2,1)S(1)}, u32[]{:S(2)}, u32[]{:S(2)}) collective-permute-start(bf16[256,128]{1,0:T(8,128)(2,1)S(1)} %get-tuple-element.50), channel_id=1, source_target_pairs={{0,16},{8,24},{16,0},{24,8},{1,17},{9,25},{17,1},{25,9},{2,18},{10... | collective-permute-start | bytes 196616 | tf_op jit(solution)/shard_map/ppermute | solution.py:340
  27.9 7.6 %collective-permute-start.9 = (bf16[256,128]{1,0:T(8,128)(2,1)S(1)}, bf16[256,128]{1,0:T(8,128)(2,1)S(1)}, u32[]{:S(2)}, u32[]{:S(2)}) collective-permute-start(bf16[256,128]{1,0:T(8,128)(2,1)S(1)} %get-tuple-element.51), channel_id=1, source_target_pairs={{0,24},{8,16},{16,8},{24,0},{1,25},{9,17},{17,9},{25,1},{2,26},{10... | collective-permute-start | bytes 196616 | tf_op jit(solution)/shard_map/ppermute | solution.py:340
  30.7 7.1 %collective-permute-start.13 = (bf16[256,128]{1,0:T(8,128)(2,1)S(1)}, bf16[256,128]{1,0:T(8,128)(2,1)S(1)}, u32[]{:S(2)}, u32[]{:S(2)}) collective-permute-start(bf16[256,128]{1,0:T(8,128)(2,1)S(1)} %get-tuple-element.57), channel_id=1, source_target_pairs={{0,16},{8,24},{16,0},{24,8},{1,17},{9,25},{17,1},{25,9},{2,18},{10... | collective-permute-start | bytes 196616 | tf_op jit(solution)/shard_map/ppermute | solution.py:340
  31.3 6.5 %collective-permute-start.14 = (bf16[256,128]{1,0:T(8,128)(2,1)S(1)}, bf16[256,128]{1,0:T(8,128)(2,1)S(1)}, u32[]{:S(2)}, u32[]{:S(2)}) collective-permute-start(bf16[256,128]{1,0:T(8,128)(2,1)S(1)} %get-tuple-element.58), channel_id=1, source_target_pairs={{0,24},{8,16},{16,8},{24,0},{1,25},{9,17},{17,9},{25,1},{2,26},{10... | collective-permute-start | bytes 196616 | tf_op jit(solution)/shard_map/ppermute | solution.py:340
  33.6 4.8 %collective-permute-start.15 = (bf16[256,128]{1,0:T(8,128)(2,1)S(1)}, bf16[256,128]{1,0:T(8,128)(2,1)S(1)}, u32[]{:S(2)}, u32[]{:S(2)}) collective-permute-start(bf16[256,128]{1,0:T(8,128)(2,1)S(1)} %get-tuple-element.59), channel_id=1, source_target_pairs={{0,8},{8,0},{16,24},{24,16},{1,9},{9,1},{17,25},{25,17},{2,10},{10... | collective-permute-start | bytes 196616 | tf_op jit(solution)/shard_map/ppermute | solution.py:340
  35.4 3.0 %collective-permute-start.16 = (bf16[64,512]{1,0:T(8,128)(2,1)S(1)}, bf16[64,512]{1,0:T(8,128)(2,1)S(1)}, u32[]{:S(2)}, u32[]{:S(2)}) collective-permute-start(bf16[64,512]{1,0:T(8,128)(2,1)S(1)} %get-tuple-element.62), channel_id=1, source_target_pairs={{0,1},{1,0},{2,3},{3,2},{4,5},{5,4},{6,7},{7,6},{8,9},{9,8},{10,11... | collective-permute-start | bytes 196616 | tf_op jit(solution)/shard_map/ppermute | solution.py:340
  35.5 3.0 %collective-permute-start.17 = (bf16[64,512]{1,0:T(8,128)(2,1)S(1)}, bf16[64,512]{1,0:T(8,128)(2,1)S(1)}, u32[]{:S(2)}, u32[]{:S(2)}) collective-permute-start(bf16[64,512]{1,0:T(8,128)(2,1)S(1)} %get-tuple-element.63), channel_id=1, source_target_pairs={{0,1},{1,0},{2,3},{3,2},{4,5},{5,4},{6,7},{7,6},{8,9},{9,8},{10,11... | collective-permute-start | bytes 196616 | tf_op jit(solution)/shard_map/ppermute | solution.py:340
  (4 other events, 30.4 us)

commit v7 on v5

--- a/solution.py
+++ b/solution.py
@@ -162,7 +162,7 @@
 
 def inverse_dense(spec, inv_hi, inv_lo):
     high, low = halves(spec)
-    return mm(high, inv_hi[...]) + mm(low, inv_hi[...]) + mm(high, inv_lo[...])
+    return mm(high, inv_hi[...]) + mm(high, inv_lo[...]) + mm(low, inv_hi[...])
 
 
 def place(index, size):

time: 39.4 us -> 39.5 us (level)
  no operation moved by 1% of the time
where the time goes in v7:
time: 39.5 us; the launch traced here: 39.4 us
  starting transfers between devices  24.8 us (63%)
  Pallas kernels  10.9 us (28%)
  waiting for transfers between devices  2.78 us (7%)
  between operations  0.85 us (2%)
    ppermute x18, starting transfers between devices, swap(): return lax.ppermute(value, axis, [(i, i ^ k) for i in range(size)])  24.8 us
    pallas_call x9, Pallas kernels, call(): pl.pallas_call(kernel, out_shape=outs, in_specs=[hbm if i in far else vme...  10.9 us
    ppermute x18, waiting for transfers between devices, swap(): return lax.ppermute(value, axis, [(i, i ^ k) for i in range(size)])  2.78 us
  transfers between devices with their start and end apart: 18, of which 4 were waited for; matrix products, arithmetic and copies ran while one was open for 0% of the time, Pallas kernels for 21%

profile of v7, /device:TPU:0, one launch (start us, length us, event | category | flops | bytes accessed | tf_op | source)
XLA Modules:
  0.0 39.4 jit_solution(5903237090531219843)
XLA Ops:
  0.6 3.0 %collective-permute-start.4 = (bf16[32,4096]{1,0:T(8,128)(2,1)}, bf16[32,4096]{1,0:T(8,128)(2,1)S(1)}, u32[]{:S(2)}, u32[]{:S(2)}) collective-permute-start(bf16[32,4096]{1,0:T(8,128)(2,1)} %bitcast.9), channel_id=1, source_target_pairs={{0,4},{2,6},{4,0},{6,2},{1,5},{3,7},{5,1},{7,3},{8,12},{10,14},{12... | collective-permute-start | bytes 786440 | tf_op jit(solution)/shard_map/ppermute | solution.py:340
  3.7 1.5 %collective-permute-start.3 = (bf16[32,4096]{1,0:T(8,128)(2,1)}, bf16[32,4096]{1,0:T(8,128)(2,1)S(1)}, u32[]{:S(2)}, u32[]{:S(2)}) collective-permute-start(bf16[32,4096]{1,0:T(8,128)(2,1)} %bitcast.10), channel_id=1, source_target_pairs={{0,2},{2,0},{4,6},{6,4},{1,3},{3,1},{5,7},{7,5},{8,10},{10,8},{12,... | collective-permute-start | bytes 786440 | tf_op jit(solution)/shard_map/ppermute | solution.py:340
  5.2 1.1 %shard_map.112 = (bf16[256,128]{1,0:T(8,128)(2,1)S(1)}, bf16[256,128]{1,0:T(8,128)(2,1)S(1)}, bf16[256,128]{1,0:T(8,128)(2,1)S(1)}) custom-call(bf16[1024,128]{1,0:T(8,128)(2,1)} %bitcast.12), custom_call_target="tpu_custom_call" | custom-call | flops 10000000000 | bytes 10000000 | tf_op jit(solution)/shard_map/pallas_call | solution.py:316
  6.3 3.7 %collective-permute-start = (bf16[256,128]{1,0:T(8,128)(2,1)S(1)}, bf16[256,128]{1,0:T(8,128)(2,1)S(1)}, u32[]{:S(2)}, u32[]{:S(2)}) collective-permute-start(bf16[256,128]{1,0:T(8,128)(2,1)S(1)} %get-tuple-element.35), channel_id=1, source_target_pairs={{0,24},{8,16},{16,8},{24,0},{1,25},{9,17},{17,9},{25,1},{2,26},{10... | collective-permute-start | bytes 196616 | tf_op jit(solution)/shard_map/ppermute | solution.py:340
  10.0 0.8 %collective-permute-start.2 = (bf16[256,128]{1,0:T(8,128)(2,1)S(1)}, bf16[256,128]{1,0:T(8,128)(2,1)S(1)}, u32[]{:S(2)}, u32[]{:S(2)}) collective-permute-start(bf16[256,128]{1,0:T(8,128)(2,1)S(1)} %get-tuple-element.37), channel_id=1, source_target_pairs={{0,8},{8,0},{16,24},{24,16},{1,9},{9,1},{17,25},{25,17},{2,10},{10... | collective-permute-start | bytes 196616 | tf_op jit(solution)/shard_map/ppermute | solution.py:340
  10.8 1.2 %collective-permute-start.6 = (bf16[32,2688]{1,0:T(8,128)(2,1)S(1)}, bf16[32,2688]{1,0:T(8,128)(2,1)S(1)}, u32[]{:S(2)}, u32[]{:S(2)}) collective-permute-start(bf16[32,2688]{1,0:T(8,128)(2,1)S(1)} %slice.9), channel_id=1, source_target_pairs={{0,2},{2,0},{4,6},{6,4},{1,3},{3,1},{5,7},{7,5},{8,10},{10,8},{12,... | collective-permute-start | bytes 516104 | tf_op jit(solution)/shard_map/ppermute | solution.py:340
  12.0 1.6 %collective-permute-start.5 = (bf16[32,1408]{1,0:T(8,128)(2,1)S(1)}, bf16[32,1408]{1,0:T(8,128)(2,1)S(1)}, u32[]{:S(2)}, u32[]{:S(2)}) collective-permute-start(bf16[32,1408]{1,0:T(8,128)(2,1)S(1)} %slice.8), channel_id=1, source_target_pairs={{0,4},{2,6},{4,0},{6,2},{1,5},{3,7},{5,1},{7,3},{8,12},{10,14},{12... | collective-permute-start | bytes 270344 | tf_op jit(solution)/shard_map/ppermute | solution.py:340
  13.6 1.0 %shard_map.113.refs_4_ = f32[256,1024]{1,0:T(8,128)S(1)} custom-call(f32[256,512]{1,0:T(8,128)S(1)} %copy-done.6, bf16[512,1024]{1,0:T(8,128)(2,1)S(1)} %copy-done.4, bf16[512,1024]{1,0:T(8,128)(2,1)S(1)} %copy-done.3, bf16[32,4096]{1,0:T(8,128)(2,1)S(1)} %collective-permute-done.3.after_1.refs_1_, bf16[32,4096]{1,0:T(8,128)(2,1)S(1)} %collective-permute-done.4.after_2.refs_2_), custom_call_target="tpu_custom_call" | custom-call | flops 2000000000 | bytes 2000000 | tf_op jit(solution)/shard_map/pallas_call | solution.py:316
  14.6 0.7 %collective-permute-done.1.refs_2_ = bf16[256,128]{1,0:T(8,128)(2,1)S(1)} collective-permute-done((bf16[256,128]{1,0:T(8,128)(2,1)S(1)}, bf16[256,128]{1,0:T(8,128)(2,1)S(1)}, u32[]{:S(2)}, u32[]{:S(2)}) %collective-permute-start.1) | collective-permute-done | bytes 65568 | tf_op jit(solution)/shard_map/ppermute | solution.py:340
  15.3 1.8 %shard_map.114 = (bf16[256,128]{1,0:T(8,128)(2,1)S(1)}, bf16[256,128]{1,0:T(8,128)(2,1)S(1)}, bf16[256,128]{1,0:T(8,128)(2,1)S(1)}, bf16[256,128]{1,0:T(8,128)(2,1)S(1)}, f32[256,1024]{1,0:T(8,128)S(1)}) custom-call(bf16[1024,128]{1,0:T(8,128)(2,1)S(1)} %bitcast.13, bf16[256,128]{1,0:T(8,128)(2,1)S(1)} %collective-permute-done.refs_1_, ...), custom_call_target="tpu_custom_call" | custom-call | flops 2000000000 | bytes 2000000 | tf_op jit(solution)/shard_map/pallas_call | solution.py:316
  17.1 1.9 %shard_map.115 = (f32[256,128]{1,0:T(8,128)S(1)}, f32[256,128]{1,0:T(8,128)S(1)}, f32[256,128]{1,0:T(8,128)S(1)}, bf16[256,128]{1,0:T(8,128)(2,1)S(1)}, bf16[256...) custom-call(bf16[256,128]{1,0:T(8,128)(2,1)S(1)} %get-tuple-element.48.after.refs_4_, ...), custom_call_target="tpu_custom_call" | custom-call | flops 1000000000 | bytes 1000000 | tf_op jit(solution)/shard_map/pallas_call | solution.py:316
  19.0 3.2 %collective-permute-start.10 = (bf16[256,128]{1,0:T(8,128)(2,1)S(1)}, bf16[256,128]{1,0:T(8,128)(2,1)S(1)}, u32[]{:S(2)}, u32[]{:S(2)}) collective-permute-start(bf16[256,128]{1,0:T(8,128)(2,1)S(1)} %get-tuple-element.53), channel_id=1, source_target_pairs={{0,24},{8,16},{16,8},{24,0},{1,25},{9,17},{17,9},{25,1},{2,26},{10... | collective-permute-start | bytes 196616 | tf_op jit(solution)/shard_map/ppermute | solution.py:340
  22.2 1.3 %collective-permute-start.12 = (bf16[256,128]{1,0:T(8,128)(2,1)S(1)}, bf16[256,128]{1,0:T(8,128)(2,1)S(1)}, u32[]{:S(2)}, u32[]{:S(2)}) collective-permute-start(bf16[256,128]{1,0:T(8,128)(2,1)S(1)} %get-tuple-element.55), channel_id=1, source_target_pairs={{0,8},{8,0},{16,24},{24,16},{1,9},{9,1},{17,25},{25,17},{2,10},{10... | collective-permute-start | bytes 196616 | tf_op jit(solution)/shard_map/ppermute | solution.py:340
  23.5 0.7 %shard_map.116 = (f32[256,128]{1,0:T(8,128)S(1)}, bf16[256,128]{1,0:T(8,128)(2,1)S(1)}) custom-call(bf16[1024,4096]{1,0:T(8,128)(2,1)S(1)} %bitcast.6, bf16[1024,128]{1,0:T(8,128)(2,1)S(1)} %bitcast.8, bf16[128,4096]{1,0:T(8,128)(2,1)S(1)} %get-tuple-element.39.rows_all), custom_call_target="tpu_custom_call" | custom-call | flops 1000000000 | bytes 1000000 | tf_op jit(solution)/shard_map/pallas_call | solution.py:316
  24.2 0.8 %collective-permute-start.7 = (bf16[256,128]{1,0:T(8,128)(2,1)S(1)}, bf16[256,128]{1,0:T(8,128)(2,1)S(1)}, u32[]{:S(2)}, u32[]{:S(2)}) collective-permute-start(bf16[256,128]{1,0:T(8,128)(2,1)S(1)} %get-tuple-element.49), channel_id=1, source_target_pairs={{0,8},{8,0},{16,24},{24,16},{1,9},{9,1},{17,25},{25,17},{2,10},{10... | collective-permute-start | bytes 196616 | tf_op jit(solution)/shard_map/ppermute | solution.py:340
  25.0 2.9 %collective-permute-start.8 = (bf16[256,128]{1,0:T(8,128)(2,1)S(1)}, bf16[256,128]{1,0:T(8,128)(2,1)S(1)}, u32[]{:S(2)}, u32[]{:S(2)}) collective-permute-start(bf16[256,128]{1,0:T(8,128)(2,1)S(1)} %get-tuple-element.50), channel_id=1, source_target_pairs={{0,16},{8,24},{16,0},{24,8},{1,17},{9,25},{17,1},{25,9},{2,18},{10... | collective-permute-start | bytes 196616 | tf_op jit(solution)/shard_map/ppermute | solution.py:340
  27.9 0.7 %collective-permute-start.9 = (bf16[256,128]{1,0:T(8,128)(2,1)S(1)}, bf16[256,128]{1,0:T(8,128)(2,1)S(1)}, u32[]{:S(2)}, u32[]{:S(2)}) collective-permute-start(bf16[256,128]{1,0:T(8,128)(2,1)S(1)} %get-tuple-element.51), channel_id=1, source_target_pairs={{0,24},{8,16},{16,8},{24,0},{1,25},{9,17},{17,9},{25,1},{2,26},{10... | collective-permute-start | bytes 196616 | tf_op jit(solution)/shard_map/ppermute | solution.py:340
  29.0 1.8 %shard_map.118 = (bf16[256,128]{1,0:T(8,128)(2,1)S(1)}, bf16[256,128]{1,0:T(8,128)(2,1)S(1)}, bf16[256,128]{1,0:T(8,128)(2,1)S(1)}, bf16[256,128]{1,0:T(8,128)(2,1)S(1)}, f32[256,1024]{1,0:T(8,128)S(1)}) custom-call(bf16[256,128]{1,0:T(8,128)(2,1)S(1)} %get-tuple-element.52.refs_0_, bf16[256,128]{1,0:T(8,128)(2,1)S(1)} %collective-permute-done.10.refs_1_, ...), custom_call_target="tpu_custom_call" | custom-call | flops 1000000000 | bytes 1000000 | tf_op jit(solution)/shard_map/pallas_call | solution.py:316
  31.3 2.4 %collective-permute-start.14 = (bf16[256,128]{1,0:T(8,128)(2,1)S(1)}, bf16[256,128]{1,0:T(8,128)(2,1)S(1)}, u32[]{:S(2)}, u32[]{:S(2)}) collective-permute-start(bf16[256,128]{1,0:T(8,128)(2,1)S(1)} %get-tuple-element.58), channel_id=1, source_target_pairs={{0,24},{8,16},{16,8},{24,0},{1,25},{9,17},{17,9},{25,1},{2,26},{10... | collective-permute-start | bytes 196616 | tf_op jit(solution)/shard_map/ppermute | solution.py:340
  33.7 0.7 %collective-permute-start.15 = (bf16[256,128]{1,0:T(8,128)(2,1)S(1)}, bf16[256,128]{1,0:T(8,128)(2,1)S(1)}, u32[]{:S(2)}, u32[]{:S(2)}) collective-permute-start(bf16[256,128]{1,0:T(8,128)(2,1)S(1)} %get-tuple-element.59), channel_id=1, source_target_pairs={{0,8},{8,0},{16,24},{24,16},{1,9},{9,1},{17,25},{25,17},{2,10},{10... | collective-permute-start | bytes 196616 | tf_op jit(solution)/shard_map/ppermute | solution.py:340
  34.4 1.1 %shard_map.119 = (f32[128,512]{1,0:T(8,128)S(1)}, bf16[64,512]{1,0:T(8,128)(2,1)S(1)}, bf16[64,512]{1,0:T(8,128)(2,1)S(1)}) custom-call(f32[256,1024]{1,0:T(8,128)S(1)} %get-tuple-element.60.spec_conv, f32[256,1024]{1,0:T(8,128)S(1)} %get-tuple-element.61.spec_gate, bf16[1024,512]{1,0:T(8,128)(2,1)S(1)} %copy-done.2, bf16[1024,512]{1,0:T(8,128)(2,1)S(1)} %copy-done.1, ...), custom_call_target="tpu_custom_call" | custom-call | flops 2000000000 | bytes 2000000 | tf_op jit(solution)/shard_map/pallas_call | solution.py:316
  36.0 0.7 %shard_map.117 = bf16[1024,128]{1,0:T(8,128)(2,1)} custom-call(f32[256,128]{1,0:T(8,128)S(1)} %get-tuple-element.40.refs_0_, f32[256,128]{1,0:T(8,128)S(1)} %get-tuple-element.41.refs_1_, f32[256,128]{1,0:T(8,128)S(1)} %get-tuple-element.42.refs_2_, f32[256,128]{1,0:T(8,128)S(1)} %get-tuple-element.43.refs_3_, ...), custom_call_target="tpu_custom_call" | custom-call | flops 1000000000 | bytes 1000000 | tf_op jit(solution)/shard_map/pallas_call | solution.py:316
  36.8 1.1 %collective-permute-done.13.refs_1_ = bf16[256,128]{1,0:T(8,128)(2,1)S(1)} collective-permute-done((bf16[256,128]{1,0:T(8,128)(2,1)S(1)}, bf16[256,128]{1,0:T(8,128)(2,1)S(1)}, u32[]{:S(2)}, u32[]{:S(2)}) %collective-permute-start.13) | collective-permute-done | bytes 65568 | tf_op jit(solution)/shard_map/ppermute | solution.py:340
  38.5 0.8 %shard_map.120 = (f32[128,512]{1,0:T(8,128)}, bf16[1024,128]{1,0:T(8,128)(2,1)}) custom-call(bf16[256,128]{1,0:T(8,128)(2,1)S(1)} %get-tuple-element.56.refs_0_, bf16[256,128]{1,0:T(8,128)(2,1)S(1)} %collective-permute-done.13.refs_1_, bf16[256,128]{1,0:T(8,128)(2,1)S(1)} %collective-permute-done.14.refs_2_, ...), custom_call_target="tpu_custom_call" | custom-call | flops 1000000000 | bytes 1000000 | tf_op jit(solution)/shard_map/pallas_call | solution.py:316
  (44 shorter events, 2.2 us)
Async XLA Ops:
  0.6 10.2 %collective-permute-start.4 = (bf16[32,4096]{1,0:T(8,128)(2,1)}, bf16[32,4096]{1,0:T(8,128)(2,1)S(1)}, u32[]{:S(2)}, u32[]{:S(2)}) collective-permute-start(bf16[32,4096]{1,0:T(8,128)(2,1)} %bitcast.9), channel_id=1, source_target_pairs={{0,4},{2,6},{4,0},{6,2},{1,5},{3,7},{5,1},{7,3},{8,12},{10,14},{12... | collective-permute-start | bytes 786440 | tf_op jit(solution)/shard_map/ppermute | solution.py:340
  3.7 8.3 %collective-permute-start.3 = (bf16[32,4096]{1,0:T(8,128)(2,1)}, bf16[32,4096]{1,0:T(8,128)(2,1)S(1)}, u32[]{:S(2)}, u32[]{:S(2)}) collective-permute-start(bf16[32,4096]{1,0:T(8,128)(2,1)} %bitcast.10), channel_id=1, source_target_pairs={{0,2},{2,0},{4,6},{6,4},{1,3},{3,1},{5,7},{7,5},{8,10},{10,8},{12,... | collective-permute-start | bytes 786440 | tf_op jit(solution)/shard_map/ppermute | solution.py:340
  5.2 10.1 %copy-start.1 = (bf16[1024,512]{1,0:T(8,128)(2,1)S(1)}, bf16[1024,512]{1,0:T(8,128)(2,1)}, u32[]{:S(2)}) copy-start(bf16[1024,512]{1,0:T(8,128)(2,1)} %constant.11.clone.refs_8_.inv_lo) | copy-start | bytes 3145732
  5.2 10.1 %copy-start.2 = (bf16[1024,512]{1,0:T(8,128)(2,1)S(1)}, bf16[1024,512]{1,0:T(8,128)(2,1)}, u32[]{:S(2)}) copy-start(bf16[1024,512]{1,0:T(8,128)(2,1)} %constant.10.clone.refs_7_.inv_hi) | copy-start | bytes 3145732
  5.2 10.1 %copy-start.7 = (bf16[1,1024,128]{2,1,0:T(8,128)(2,1)S(1)}, bf16[1,1024,128]{2,1,0:T(8,128)(2,1)}, u32[]{:S(2)}) copy-start(bf16[1,1024,128]{2,1,0:T(8,128)(2,1)} %param.11) | copy-start | bytes 786436
  6.3 10.8 %slice-start = ((s8[8388608]{0:T(1024)(128)(4,1)}), s8[4194304]{0:T(1024)(128)(4,1)S(1)}, s32[]{:S(2)}) async-start(s8[8388608]{0:T(1024)(128)(4,1)} %bitcast.5), calls=%async_computation | async-start | bytes 8388608
  6.3 10.8 %copy-start = (bf16[1,1024,128]{2,1,0:T(8,128)(2,1)S(1)}, bf16[1,1024,128]{2,1,0:T(8,128)(2,1)}, u32[]{:S(2)}) copy-start(bf16[1,1024,128]{2,1,0:T(8,128)(2,1)} %param.10) | copy-start | bytes 786436
  6.3 10.8 %copy-start.5 = (bf16[1,32,4096]{2,1,0:T(8,128)(2,1)S(1)}, bf16[1,32,4096]{2,1,0:T(8,128)(2,1)}, u32[]{:S(2)}) copy-start(bf16[1,32,4096]{2,1,0:T(8,128)(2,1)} %param.9) | copy-start | bytes 786436
  6.3 8.3 %collective-permute-start = (bf16[256,128]{1,0:T(8,128)(2,1)S(1)}, bf16[256,128]{1,0:T(8,128)(2,1)S(1)}, u32[]{:S(2)}, u32[]{:S(2)}) collective-permute-start(bf16[256,128]{1,0:T(8,128)(2,1)S(1)} %get-tuple-element.35), channel_id=1, source_target_pairs={{0,24},{8,16},{16,8},{24,0},{1,25},{9,17},{17,9},{25,1},{2,26},{10... | collective-permute-start | bytes 196616 | tf_op jit(solution)/shard_map/ppermute | solution.py:340
  10.0 5.2 %collective-permute-start.1 = (bf16[256,128]{1,0:T(8,128)(2,1)S(1)}, bf16[256,128]{1,0:T(8,128)(2,1)S(1)}, u32[]{:S(2)}, u32[]{:S(2)}) collective-permute-start(bf16[256,128]{1,0:T(8,128)(2,1)S(1)} %get-tuple-element.36), channel_id=1, source_target_pairs={{0,16},{8,24},{16,0},{24,8},{1,17},{9,25},{17,1},{25,9},{2,18},{10... | collective-permute-start | bytes 196616 | tf_op jit(solution)/shard_map/ppermute | solution.py:340
  10.0 5.2 %collective-permute-start.2 = (bf16[256,128]{1,0:T(8,128)(2,1)S(1)}, bf16[256,128]{1,0:T(8,128)(2,1)S(1)}, u32[]{:S(2)}, u32[]{:S(2)}) collective-permute-start(bf16[256,128]{1,0:T(8,128)(2,1)S(1)} %get-tuple-element.37), channel_id=1, source_target_pairs={{0,8},{8,0},{16,24},{24,16},{1,9},{9,1},{17,25},{25,17},{2,10},{10... | collective-permute-start | bytes 196616 | tf_op jit(solution)/shard_map/ppermute | solution.py:340
  10.8 6.3 %collective-permute-start.6 = (bf16[32,2688]{1,0:T(8,128)(2,1)S(1)}, bf16[32,2688]{1,0:T(8,128)(2,1)S(1)}, u32[]{:S(2)}, u32[]{:S(2)}) collective-permute-start(bf16[32,2688]{1,0:T(8,128)(2,1)S(1)} %slice.9), channel_id=1, source_target_pairs={{0,2},{2,0},{4,6},{6,4},{1,3},{3,1},{5,7},{7,5},{8,10},{10,8},{12,... | collective-permute-start | bytes 516104 | tf_op jit(solution)/shard_map/ppermute | solution.py:340
  12.0 5.1 %collective-permute-start.5 = (bf16[32,1408]{1,0:T(8,128)(2,1)S(1)}, bf16[32,1408]{1,0:T(8,128)(2,1)S(1)}, u32[]{:S(2)}, u32[]{:S(2)}) collective-permute-start(bf16[32,1408]{1,0:T(8,128)(2,1)S(1)} %slice.8), channel_id=1, source_target_pairs={{0,4},{2,6},{4,0},{6,2},{1,5},{3,7},{5,1},{7,3},{8,12},{10,14},{12... | collective-permute-start | bytes 270344 | tf_op jit(solution)/shard_map/ppermute | solution.py:340
  19.0 8.9 %collective-permute-start.10 = (bf16[256,128]{1,0:T(8,128)(2,1)S(1)}, bf16[256,128]{1,0:T(8,128)(2,1)S(1)}, u32[]{:S(2)}, u32[]{:S(2)}) collective-permute-start(bf16[256,128]{1,0:T(8,128)(2,1)S(1)} %get-tuple-element.53), channel_id=1, source_target_pairs={{0,24},{8,16},{16,8},{24,0},{1,25},{9,17},{17,9},{25,1},{2,26},{10... | collective-permute-start | bytes 196616 | tf_op jit(solution)/shard_map/ppermute | solution.py:340
  22.2 6.8 %collective-permute-start.11 = (bf16[256,128]{1,0:T(8,128)(2,1)S(1)}, bf16[256,128]{1,0:T(8,128)(2,1)S(1)}, u32[]{:S(2)}, u32[]{:S(2)}) collective-permute-start(bf16[256,128]{1,0:T(8,128)(2,1)S(1)} %get-tuple-element.54), channel_id=1, source_target_pairs={{0,16},{8,24},{16,0},{24,8},{1,17},{9,25},{17,1},{25,9},{2,18},{10... | collective-permute-start | bytes 196616 | tf_op jit(solution)/shard_map/ppermute | solution.py:340
  22.2 6.8 %collective-permute-start.12 = (bf16[256,128]{1,0:T(8,128)(2,1)S(1)}, bf16[256,128]{1,0:T(8,128)(2,1)S(1)}, u32[]{:S(2)}, u32[]{:S(2)}) collective-permute-start(bf16[256,128]{1,0:T(8,128)(2,1)S(1)} %get-tuple-element.55), channel_id=1, source_target_pairs={{0,8},{8,0},{16,24},{24,16},{1,9},{9,1},{17,25},{25,17},{2,10},{10... | collective-permute-start | bytes 196616 | tf_op jit(solution)/shard_map/ppermute | solution.py:340
  24.2 9.5 %collective-permute-start.7 = (bf16[256,128]{1,0:T(8,128)(2,1)S(1)}, bf16[256,128]{1,0:T(8,128)(2,1)S(1)}, u32[]{:S(2)}, u32[]{:S(2)}) collective-permute-start(bf16[256,128]{1,0:T(8,128)(2,1)S(1)} %get-tuple-element.49), channel_id=1, source_target_pairs={{0,8},{8,0},{16,24},{24,16},{1,9},{9,1},{17,25},{25,17},{2,10},{10... | collective-permute-start | bytes 196616 | tf_op jit(solution)/shard_map/ppermute | solution.py:340
  25.0 9.4 %collective-permute-start.8 = (bf16[256,128]{1,0:T(8,128)(2,1)S(1)}, bf16[256,128]{1,0:T(8,128)(2,1)S(1)}, u32[]{:S(2)}, u32[]{:S(2)}) collective-permute-start(bf16[256,128]{1,0:T(8,128)(2,1)S(1)} %get-tuple-element.50), channel_id=1, source_target_pairs={{0,16},{8,24},{16,0},{24,8},{1,17},{9,25},{17,1},{25,9},{2,18},{10... | collective-permute-start | bytes 196616 | tf_op jit(solution)/shard_map/ppermute | solution.py:340
  27.9 7.6 %collective-permute-start.9 = (bf16[256,128]{1,0:T(8,128)(2,1)S(1)}, bf16[256,128]{1,0:T(8,128)(2,1)S(1)}, u32[]{:S(2)}, u32[]{:S(2)}) collective-permute-start(bf16[256,128]{1,0:T(8,128)(2,1)S(1)} %get-tuple-element.51), channel_id=1, source_target_pairs={{0,24},{8,16},{16,8},{24,0},{1,25},{9,17},{17,9},{25,1},{2,26},{10... | collective-permute-start | bytes 196616 | tf_op jit(solution)/shard_map/ppermute | solution.py:340
  30.8 7.1 %collective-permute-start.13 = (bf16[256,128]{1,0:T(8,128)(2,1)S(1)}, bf16[256,128]{1,0:T(8,128)(2,1)S(1)}, u32[]{:S(2)}, u32[]{:S(2)}) collective-permute-start(bf16[256,128]{1,0:T(8,128)(2,1)S(1)} %get-tuple-element.57), channel_id=1, source_target_pairs={{0,16},{8,24},{16,0},{24,8},{1,17},{9,25},{17,1},{25,9},{2,18},{10... | collective-permute-start | bytes 196616 | tf_op jit(solution)/shard_map/ppermute | solution.py:340
  31.3 6.6 %collective-permute-start.14 = (bf16[256,128]{1,0:T(8,128)(2,1)S(1)}, bf16[256,128]{1,0:T(8,128)(2,1)S(1)}, u32[]{:S(2)}, u32[]{:S(2)}) collective-permute-start(bf16[256,128]{1,0:T(8,128)(2,1)S(1)} %get-tuple-element.58), channel_id=1, source_target_pairs={{0,24},{8,16},{16,8},{24,0},{1,25},{9,17},{17,9},{25,1},{2,26},{10... | collective-permute-start | bytes 196616 | tf_op jit(solution)/shard_map/ppermute | solution.py:340
  33.7 4.8 %collective-permute-start.15 = (bf16[256,128]{1,0:T(8,128)(2,1)S(1)}, bf16[256,128]{1,0:T(8,128)(2,1)S(1)}, u32[]{:S(2)}, u32[]{:S(2)}) collective-permute-start(bf16[256,128]{1,0:T(8,128)(2,1)S(1)} %get-tuple-element.59), channel_id=1, source_target_pairs={{0,8},{8,0},{16,24},{24,16},{1,9},{9,1},{17,25},{25,17},{2,10},{10... | collective-permute-start | bytes 196616 | tf_op jit(solution)/shard_map/ppermute | solution.py:340
  35.5 3.0 %collective-permute-start.16 = (bf16[64,512]{1,0:T(8,128)(2,1)S(1)}, bf16[64,512]{1,0:T(8,128)(2,1)S(1)}, u32[]{:S(2)}, u32[]{:S(2)}) collective-permute-start(bf16[64,512]{1,0:T(8,128)(2,1)S(1)} %get-tuple-element.62), channel_id=1, source_target_pairs={{0,1},{1,0},{2,3},{3,2},{4,5},{5,4},{6,7},{7,6},{8,9},{9,8},{10,11... | collective-permute-start | bytes 196616 | tf_op jit(solution)/shard_map/ppermute | solution.py:340
  35.6 3.0 %collective-permute-start.17 = (bf16[64,512]{1,0:T(8,128)(2,1)S(1)}, bf16[64,512]{1,0:T(8,128)(2,1)S(1)}, u32[]{:S(2)}, u32[]{:S(2)}) collective-permute-start(bf16[64,512]{1,0:T(8,128)(2,1)S(1)} %get-tuple-element.63), channel_id=1, source_target_pairs={{0,1},{1,0},{2,3},{3,2},{4,5},{5,4},{6,7},{7,6},{8,9},{9,8},{10,11... | collective-permute-start | bytes 196616 | tf_op jit(solution)/shard_map/ppermute | solution.py:340
  (4 other events, 30.4 us)
